TPU v7x, 32 devices: a whole 2x2x4 slice. The times are simulated.
32 devices in a mesh: section: 2 (over y), hid: 4 (over x, core), dp: 4 (over z).
Axes of the slice: x: 2, y: 2, z: 4, core: 2. Of those that a mesh axis runs over, the one named last changes fastest.
Arguments:
- acts_in: bfloat16 [2, 2, 512, 8192], P('section', None, 'dp', 'hid'), may hold values from -6 to 6
- pre_act: bfloat16 [2, 2, 512, 16384], P('section', None, 'dp', 'hid'), may hold values from -6 to 6
- out_grad: bfloat16 [2, 512, 8192], P(None, 'dp', 'hid'), may hold values from -6 to 6
- up_weight: bfloat16 [2, 3, 64, 256, 256], P('section', None, 'hid'), may hold values from -0.21875 to 0.21875
- down_weight: bfloat16 [2, 3, 64, 256, 256], P('section', None, 'hid'), may hold values from -0.21875 to 0.21875
- up_pick: int32 [2, 3, 64], P('section', None, 'hid'), may hold values from 0 to 7
- down_pick: int32 [2, 3, 64], P('section', None, 'hid'), may hold values from 0 to 7
- factor_order: int32 [2, 3], P('section'), may hold values from 0 to 2, each once within a row
Outputs:
- grad_in: bfloat16 [2, 2, 512, 8192], P('section', None, 'dp', 'hid')
- up_grad: float32 [2, 3, 64, 256, 256], P('section', None, 'hid', 'dp')
- down_grad: float32 [2, 3, 64, 256, 256], P('section', None, 'hid', None, 'dp')
Inputs may be any that keep to these rules, and one draw needn't show every extreme that they name: Each row of factor_order names each of the 3 weight slots once.
All inputs are finite; a program needn't handle non-finite values.
Results may differ from a plain program's by a relative error of at most 0.019.
Values may be sent and summed in bfloat16 or wider, within the bound.
No kernel may reach another device: no remote copies, remote signals or barrier semaphores. Data moves between devices by JAX's collectives and lax.ppermute only.
A program may use at most 128 MiB of HBM per device.

v0:
```python
import jax
import jax.numpy as jnp
from jax import lax
from jax.sharding import PartitionSpec as P


def from_partner(block, axis, apart):
    count = lax.axis_size(axis)
    route = []
    for low in range(count):
        high = low | 1 << apart
        if high != low and high < count:
            route += [(low, high), (high, low)]
    return lax.ppermute(block, axis, route)


def shifted(value, axis, steps):
    count = lax.axis_size(axis)
    first, last = (max(0, -steps), min(count, count - steps))
    return lax.ppermute(value, axis, [(source, source + steps) for source in range(first, last)])


def gelu_tanh(values):
    return jax.nn.gelu(values, approximate=True)


def gelu_slope(values, pull_in):
    _, pull_back = jax.vjp(gelu_tanh, values)
    return pull_back(pull_in)[0]


def put_slot(store, value, current, running):
    old_value = lax.dynamic_index_in_dim(store, current, 0, False)
    new_value = jnp.where(running, value, old_value)
    return lax.dynamic_update_index_in_dim(store, new_value, current, 0)


def local(acts_in, pre_act, out_grad, up_weight, down_weight, up_pick, down_pick, factor_order):
    highest = lax.Precision.HIGHEST
    bit_count = lax.axis_size("hid").bit_length() - 1
    factor_count = bit_count + 1
    sections = lax.axis_size("section")
    section_index = lax.axis_index("section")
    micro_count = acts_in.shape[1]
    tokens = acts_in.shape[2]
    local_width = acts_in.shape[3]
    block_size = up_weight.shape[-1]
    fgroup = local_width // block_size
    hgroup = up_weight.shape[2]
    step_count = sections * micro_count
    weight_index = factor_order[0]
    w_up = jnp.take(up_weight[0], weight_index, axis=0)
    w_down = jnp.take(down_weight[0], weight_index, axis=0)
    pick_up = jnp.take(up_pick[0], weight_index, axis=0)
    pick_down = jnp.take(down_pick[0], weight_index, axis=0)
    onehot_up = (pick_up[:, :, None] == jnp.arange(fgroup, dtype=jnp.int32)[None, None, :]).astype(
        jnp.float32
    )
    input_own = acts_in[0].reshape(micro_count, tokens, fgroup, block_size)
    input_list = [input_own]
    for bit_number in range(bit_count):
        input_list.append(from_partner(input_own, "hid", bit_number))
    input_all = jnp.stack(input_list)
    input_sel = jnp.take_along_axis(input_all, pick_up[:, None, None, :, None], axis=3)
    pre_all = pre_act[0].reshape(micro_count, tokens, hgroup, block_size)
    grad_top = out_grad.reshape(micro_count, tokens, fgroup, block_size)

    def do_work(operands):
        g_stack, pre_now = operands
        chosen = jnp.take_along_axis(g_stack, pick_down[:, None, :, None], axis=2)
        slope_in = jnp.einsum("ftjc,fjdc->tjd", chosen, w_down, preferred_element_type=jnp.float32)
        hidden_grad = gelu_slope(pre_now.astype(jnp.float32), slope_in).astype(jnp.bfloat16)
        product = jnp.einsum(
            "tjd,fjcd->ftjc", hidden_grad, w_up, preferred_element_type=jnp.float32
        )
        term_blocks = jnp.einsum("ftjc,fje->ftec", product, onehot_up, precision=highest)
        return (term_blocks[0], term_blocks[1:].astype(jnp.bfloat16), hidden_grad, chosen)

    def skip_work(operands):
        return (
            jnp.zeros((tokens, fgroup, block_size), jnp.float32),
            jnp.zeros((bit_count, tokens, fgroup, block_size), jnp.bfloat16),
            jnp.zeros((tokens, hgroup, block_size), jnp.bfloat16),
            jnp.zeros((factor_count, tokens, hgroup, block_size), jnp.bfloat16),
        )

    incoming = jnp.zeros((tokens, fgroup, block_size), jnp.bfloat16)
    grad_out = jnp.zeros((micro_count, tokens, fgroup, block_size), jnp.bfloat16)
    hidden_store = jnp.zeros((micro_count, tokens, hgroup, block_size), jnp.bfloat16)
    chosen_store = jnp.zeros((micro_count, factor_count, tokens, hgroup, block_size), jnp.bfloat16)
    for step_number in range(step_count):
        current = jnp.int32(step_number // sections)
        running = section_index == sections - 1 - step_number % sections
        current = jnp.clip(current, 0, micro_count - 1)
        top_grad = lax.dynamic_index_in_dim(grad_top, current, 0, False)
        g_now = jnp.where(section_index == sections - 1, top_grad, incoming)
        g_list = [g_now]
        for bit_number in range(bit_count):
            g_list.append(from_partner(g_now, "hid", bit_number))
        g_stack = jnp.stack(g_list)
        pre_now = lax.dynamic_index_in_dim(pre_all, current, 0, False)
        own_term, crossing, hidden_grad, chosen = lax.cond(
            running, do_work, skip_work, (g_stack, pre_now)
        )
        summed = g_now.astype(jnp.float32) + own_term
        for bit_number in range(bit_count):
            summed = summed + from_partner(crossing[bit_number], "hid", bit_number).astype(
                jnp.float32
            )
        result = summed.astype(jnp.bfloat16)
        grad_out = put_slot(grad_out, result, current, running)
        hidden_store = put_slot(hidden_store, hidden_grad, current, running)
        chosen_store = put_slot(chosen_store, chosen, current, running)
        if step_number + 1 < step_count:
            incoming = shifted(result, "section", -1)
    inverse = jnp.sum(
        jnp.arange(factor_count, dtype=jnp.int32)[:, None]
        * (weight_index[:, None] == jnp.arange(factor_count, dtype=jnp.int32)[None, :]).astype(
            jnp.int32
        ),
        axis=0,
    )
    active_all = gelu_tanh(pre_all.astype(jnp.float32)).astype(jnp.bfloat16)
    acc_down = jnp.einsum(
        "mtjd,mftjc->fjdc", active_all, chosen_store, preferred_element_type=jnp.float32
    )
    acc_up = jnp.einsum(
        "fmtjc,mtjd->fjcd", input_sel, hidden_store, preferred_element_type=jnp.float32
    )
    down_part, up_part = (
        lax.psum_scatter(
            acc_down.astype(jnp.bfloat16), "dp", scatter_dimension=3, tiled=True
        ).astype(jnp.float32),
        lax.psum_scatter(acc_up.astype(jnp.bfloat16), "dp", scatter_dimension=2, tiled=True).astype(
            jnp.float32
        ),
    )
    down_grad = jnp.take(down_part, inverse, axis=0)[None]
    up_grad = jnp.take(up_part, inverse, axis=0)[None]
    return (grad_out.reshape(1, micro_count, tokens, local_width), up_grad, down_grad)


def solution(mesh):
    placed = (
        P("section", None, "dp", "hid"),
        P("section", None, "dp", "hid"),
        P(None, "dp", "hid"),
        P("section", None, "hid", None, None),
        P("section", None, "hid", None, None),
        P("section", None, "hid"),
        P("section", None, "hid"),
        P("section", None),
    )
    return jax.shard_map(
        local,
        mesh=mesh,
        in_specs=placed,
        out_specs=(
            P("section", None, "dp", "hid"),
            P("section", None, "hid", "dp", None),
            P("section", None, "hid", None, "dp"),
        ),
        check_vma=False,
    )
```

profile of v0, /device:TPU:0, one launch (start us, length us, event | category | flops | bytes accessed | tf_op | source)
XLA Modules:
  0.0 575.0 jit_solution(13667574578495990387)
XLA Ops:
  7.2 2.3 fusion.127
  10.6 2.9 collective-permute-start.1
  13.6 5.1 fusion.124
  19.3 4.4 gather_fusion.11
  23.7 2.5 gather_fusion.10
  26.2 5.1 fusion.125
  31.3 4.4 gather_fusion.9
  35.7 2.5 gather_fusion.8
  38.2 2.8 fusion.126
  41.1 11.0 %maximum_select_fusion.1 = (bf16[3,16,256,256]{3,2,1,0:T(8,128)(2,1)}, bf16[3,16,256,256]{3,2,1,0:T(8,128)(2,1)}) fusion(bf16[3,16,128,256]{3,2,1,0:T(8,128)(2,1)S(1)} %copy-done.7, bf16[3,16,128,256]{3,2,1,0:T(8,128)(2,1)} %gather_fusion.10, pred[3]{0:T(512)(128)(4,1)S(1)} %compare_and_fusion, bf16[3,16,128,256]{3,2,1,0:T(8,128)(2,1)} %gather_fusion.9, ...), kind=kLoop, calls=%fused_computation.138 | loop fusion | flops 31457280 | bytes 25165828 | tf_op jit(solution)/shard_map/jit(_take)/select_n | solution.py:52
  54.3 2.5 pad_maximum_fusion.1
  56.8 11.5 %conditional.4 = (f32[128,8,256]{2,1,0:T(8,128)S(1)}, bf16[2,128,8,256]{3,2,1,0:T(8,128)(2,1)S(1)}, bf16[128,16,256]{2,0,1:T(8,128)(2,1)}, bf16[3,128,16,256]{3,1,2,0:T(8,128)(2,1)S(1)}) conditional(s32[]{:T(128)} %convert_element_type.116, () %tuple.43, (s32[3,16]{1,0:T(4,128)S(1)}, bf16[3,128,8,256]{3,2,1,0:T(8,128)(2,1)}, ...), branch_computations={%region_0.3_spmd, %region_1.5_spmd} | conditional | flops 1774191232 | bytes 115346952 | solution.py:102
  69.0 13.7 %collective-permute-done.3 = bf16[128,8,256]{2,1,0:T(8,128)(2,1)S(1)} collective-permute-done((bf16[128,8,256]{2,1,0:T(8,128)(2,1)S(1)}, bf16[128,8,256]{2,1,0:T(8,128)(2,1)S(1)}, u32[]{:S(2)}, u32[]{:S(2)}) %collective-permute-start.3) | collective-permute-done | bytes 524320 | tf_op jit(solution)/shard_map/ppermute | solution.py:14
  82.8 2.2 fusion.117
  86.3 27.9 %collective-permute-done.4 = bf16[128,8,256]{2,1,0:T(8,128)(2,1)S(1)} collective-permute-done((bf16[128,8,256]{2,1,0:T(8,128)(2,1)S(1)}, bf16[128,8,256]{2,1,0:T(8,128)(2,1)S(1)}, u32[]{:S(2)}, u32[]{:S(2)}) %collective-permute-start.4) | collective-permute-done | bytes 524320 | tf_op jit(solution)/shard_map/ppermute | solution.py:20
  115.7 12.7 %collective-permute-done.6 = bf16[128,8,256]{2,1,0:T(8,128)(2,1)} collective-permute-done((bf16[128,8,256]{2,1,0:T(8,128)(2,1)}, bf16[128,8,256]{2,1,0:T(8,128)(2,1)}, u32[]{:S(2)}, u32[]{:S(2)}) %collective-permute-start.6) | collective-permute-done | bytes 524320 | tf_op jit(solution)/shard_map/ppermute | solution.py:14
  128.5 2.7 pad_maximum_fusion.2
  131.1 38.0 %conditional.5 = (f32[128,8,256]{2,1,0:T(8,128)S(1)}, bf16[2,128,8,256]{3,2,1,0:T(8,128)(2,1)S(1)}, bf16[128,16,256]{2,0,1:T(8,128)(2,1)}, bf16[3,128,16,256]{3,1,2,0:T(8,128)(2,1)}) conditional(s32[]{:T(128)} %convert_element_type.122, () %tuple.45, (s32[3,16]{1,0:T(4,128)S(1)}, bf16[3,128,8,256]{3,2,1,0:T(8,128)(2,1)}, ...), branch_computations={%region_2.0_spmd, %region_3.7_spmd} | conditional | flops 1774191232 | bytes 96472520 | solution.py:102
  131.1 2.3 copy.153
  133.4 2.9 copy.152
  136.4 3.9 gather_fusion.1
  140.4 2.4 select_bitcast_fusion.1
  142.8 6.5 %fusion.32 = bf16[128,16,256]{2,0,1:T(8,128)(2,1)S(1)} fusion(bf16[128,16,256]{2,0,1:T(8,128)(2,1)S(1)} %copy-done.32, bf16[3,128,16,256]{3,1,2,0:T(8,128)(2,1)S(1)} %select_bitcast_fusion.1, bf16[3,16,256,256]{3,2,1,0:T(8,128)(2,1)} %get-tuple-element.59), kind=kOutput, calls=%fused_computation.56 | convolution fusion | flops 816316416 | bytes 11534336 | tf_op jit(solution)/shard_map/cond/branch_1_fun/ftjc,fjdc->tjd/dot_general | solution.py:71
  151.6 7.1 %fusion.39 = f32[3,128,8,256]{3,2,1,0:T(8,128)S(1)} fusion(f32[3,128,16,256]{3,1,0,2:T(8,128)S(1)} %fusion.27, f32[3,16,8]{1,2,0:T(8,128)S(1)} %get-tuple-element.62), kind=kOutput, calls=%fused_computation.65 | convolution fusion | flops 150994944 | bytes 9438720 | tf_op jit(solution)/shard_map/cond/branch_1_fun/ftjc,fje->ftec/dot_general | solution.py:76
  171.9 9.4 %collective-permute-done.8 = bf16[128,8,256]{2,1,0:T(8,128)(2,1)S(1)} collective-permute-done((bf16[128,8,256]{2,1,0:T(8,128)(2,1)S(1)}, bf16[128,8,256]{2,1,0:T(8,128)(2,1)S(1)}, u32[]{:S(2)}, u32[]{:S(2)}) %collective-permute-start.8) | collective-permute-done | bytes 524320 | tf_op jit(solution)/shard_map/ppermute | solution.py:14
  181.3 2.3 bitcast_dynamic-update-slice_fusion.7
  185.1 11.6 %collective-permute-done.9 = bf16[128,8,256]{2,1,0:T(8,128)(2,1)S(1)} collective-permute-done((bf16[128,8,256]{2,1,0:T(8,128)(2,1)S(1)}, bf16[128,8,256]{2,1,0:T(8,128)(2,1)S(1)}, u32[]{:S(2)}, u32[]{:S(2)}) %collective-permute-start.9) | collective-permute-done | bytes 524320 | tf_op jit(solution)/shard_map/ppermute | solution.py:20
  198.1 2.3 copy.195
  200.4 7.7 %collective-permute-done.11 = bf16[128,8,256]{2,1,0:T(8,128)(2,1)} collective-permute-done((bf16[128,8,256]{2,1,0:T(8,128)(2,1)}, bf16[128,8,256]{2,1,0:T(8,128)(2,1)}, u32[]{:S(2)}, u32[]{:S(2)}) %collective-permute-start.11) | collective-permute-done | bytes 524320 | tf_op jit(solution)/shard_map/ppermute | solution.py:14
  208.1 2.7 pad_maximum_fusion.3
  210.8 4.4 conditional.6
  216.9 2.3 copy.162
  219.1 2.3 copy.164
  223.1 2.3 copy.166
  226.9 3.1 fusion.116
  233.0 15.3 %collective-permute-done.20 = bf16[2,128,8,256]{3,1,2,0:T(8,128)(2,1)} collective-permute-done((bf16[2,128,8,256]{3,1,2,0:T(8,128)(2,1)}, bf16[2,128,8,256]{3,1,2,0:T(8,128)(2,1)}, u32[]{:S(2)}, u32[]{:S(2)}) %collective-permute-start.20) | collective-permute-done | bytes 1048608 | tf_op jit(solution)/shard_map/ppermute | solution.py:14
  248.4 3.5 pad_maximum_fusion
  251.9 7.2 %gather_fusion.6 = bf16[48,2,128,256]{3,2,1,0:T(8,128)(2,1)} fusion(bf16[3,2,128,8,256]{4,2,3,1,0:T(8,128)(2,1)} %pad_maximum_fusion, s32[48]{0:T(128)S(1)} %reshape.214), kind=kCustom, calls=%fused_computation.12 | custom fusion | bytes 12583296 | tf_op jit(solution)/shard_map/jit(take_along_axis)/gather | solution.py:64
  259.1 2.6 bitcast_dynamic-update-slice_fusion.5
  261.6 8.9 %collective-permute-done.14 = bf16[128,8,256]{2,1,0:T(8,128)(2,1)} collective-permute-done((bf16[128,8,256]{2,1,0:T(8,128)(2,1)}, bf16[128,8,256]{2,1,0:T(8,128)(2,1)}, u32[]{:S(2)}, u32[]{:S(2)}) %collective-permute-start.14) | collective-permute-done | bytes 524320 | tf_op jit(solution)/shard_map/ppermute | solution.py:20
  273.7 10.1 %collective-permute-done.16 = bf16[128,8,256]{2,1,0:T(8,128)(2,1)S(1)} collective-permute-done((bf16[128,8,256]{2,1,0:T(8,128)(2,1)S(1)}, bf16[128,8,256]{2,1,0:T(8,128)(2,1)S(1)}, u32[]{:S(2)}, u32[]{:S(2)}) %collective-permute-start.16) | collective-permute-done | bytes 524320 | tf_op jit(solution)/shard_map/ppermute | solution.py:14
  285.1 31.0 %conditional.7 = (f32[128,8,256]{2,1,0:T(8,128)S(1)}, bf16[2,128,8,256]{3,2,1,0:T(8,128)(2,1)S(1)}, bf16[128,16,256]{2,0,1:T(8,128)(2,1)S(1)}, bf16[3,128,16,256]{3,1,2,0:T(8,128)(2,1)}) conditional(s32[]{:T(128)} %convert_element_type.122, () %tuple.49, (s32[3,16]{1,0:T(4,128)S(1)}, bf16[3,128,8,256]{3,2,1,0:T(8,128)(2,1)}, ...), branch_computations={%region_6.10_spmd, %region_7.11_spmd} | conditional | flops 1774191232 | bytes 88083912 | solution.py:102
  285.1 2.5 copy.160
  287.6 2.9 copy.159
  290.7 3.9 gather_fusion.3
  294.6 4.1 select_bitcast_fusion.3
  298.7 6.4 %fusion.76 = bf16[128,16,256]{2,0,1:T(8,128)(2,1)S(1)} fusion(bf16[128,16,256]{2,0,1:T(8,128)(2,1)S(1)} %copy-done.34, bf16[3,128,16,256]{3,1,2,0:T(8,128)(2,1)} %select_bitcast_fusion.3, bf16[3,16,256,256]{3,2,1,0:T(8,128)(2,1)} %get-tuple-element.71), kind=kOutput, calls=%fused_computation.116 | convolution fusion | flops 816316416 | bytes 11534336 | tf_op jit(solution)/shard_map/cond/branch_1_fun/ftjc,fjdc->tjd/dot_general | solution.py:71
  307.4 7.1 %fusion.83 = f32[3,128,8,256]{3,2,1,0:T(8,128)S(1)} fusion(f32[3,128,16,256]{3,1,0,2:T(8,128)S(1)} %fusion.71, f32[3,16,8]{1,2,0:T(8,128)S(1)} %get-tuple-element.74), kind=kOutput, calls=%fused_computation.125 | convolution fusion | flops 150994944 | bytes 9438720 | tf_op jit(solution)/shard_map/cond/branch_1_fun/ftjc,fje->ftec/dot_general | solution.py:76
  317.9 8.1 %fusion.88 = bf16[3,16,256,256]{2,3,0,1:T(8,128)(2,1)} fusion(bf16[3,16,2,128,256]{4,3,2,1,0:T(8,128)(2,1)} %bitcast.335, pred[3,16]{1,0:T(4,128)(4,1)S(1)} %get-tuple-element.248, bf16[2,128,16,256]{3,1,2,0:T(8,128)(2,1)} %bitcast_dynamic-update-slice_fusion.3), kind=kOutput, calls=%fused_computation.135 | convolution fusion | flops 1616904192 | bytes 14680112 | tf_op jit(solution)/shard_map/fmtjc,mtjd->fjcd/dot_general | solution.py:127
  325.9 9.1 %copy.169 = bf16[3,16,256,256]{3,1,0,2:T(8,128)(2,1)} copy(bf16[3,16,256,256]{2,3,0,1:T(8,128)(2,1)} %fusion.88) | data formatting | bytes 12582912 | tf_op jit(solution)/shard_map/convert_element_type | solution.py:134
  335.3 4.2 copy.199
  343.8 3.1 bitcast_dynamic-update-slice_fusion
  346.9 2.7 copy-done.4
  349.6 8.7 %fusion.104 = bf16[16,3,256,256,1]{3,2,0,1,4:T(8,128)(2,1)S(1)} fusion(bf16[2,3,128,16,256]{4,2,3,1,0:T(8,128)(2,1)} %copy-done.4, f32[2,128,16,256]{3,2,1,0:T(8,128)} %bitcast.337), kind=kOutput, calls=%fused_computation.161 | convolution fusion | flops 1620049920 | bytes 16777216 | tf_op jit(solution)/shard_map/mtjd,mftjc->fjdc/dot_general | solution.py:124
  358.3 3.0 copy.247
  364.9 10.1 %collective-permute-done.18 = bf16[128,8,256]{2,1,0:T(8,128)(2,1)S(1)} collective-permute-done((bf16[128,8,256]{2,1,0:T(8,128)(2,1)S(1)}, bf16[128,8,256]{2,1,0:T(8,128)(2,1)S(1)}, u32[]{:S(2)}, u32[]{:S(2)}) %collective-permute-start.18) | collective-permute-done | bytes 524320 | tf_op jit(solution)/shard_map/ppermute | solution.py:14
  376.2 2.5 reshape.120
  378.7 67.5 %reduce-scatter.3.cloned.1.call-done = bf16[3,16,64,256]{3,1,0,2:T(8,128)(2,1)} async-done(((bf16[3,16,256,256]{3,1,0,2:T(8,128)(2,1)}), bf16[3,16,64,256]{3,1,0,2:T(8,128)(2,1)}) %reduce-scatter.3.cloned.1.call-update) | async-done | bytes 1572880 | tf_op jit(solution)/shard_map/reduce_scatter | solution.py:134
  448.0 2.4 gather_fusion.4
  450.4 2.3 bitcast_select_fusion.1
  452.8 3.7 copy.176
  456.4 103.3 %reduce-scatter.5.cloned.1.call-done = bf16[3,16,256,64]{2,3,0,1:T(8,128)(2,1)} async-done(((bf16[3,16,256,256]{2,3,0,1:T(8,128)(2,1)}), bf16[3,16,256,64]{2,3,0,1:T(8,128)(2,1)}) %reduce-scatter.5.cloned.1.call-update) | async-done | bytes 1572880 | tf_op jit(solution)/shard_map/reduce_scatter | solution.py:131
  559.8 3.5 convert_element_type.142
  563.2 2.6 gather_fusion.5
  (176 shorter events, 51.8 us)
Async XLA Ops:
  7.2 6.4 %copy-start.37 = (s32[1,3]{1,0:T(1,128)S(1)}, s32[1,3]{1,0:T(1,128)}, u32[]{:S(2)}) copy-start(s32[1,3]{1,0:T(1,128)} %param.29) | copy-start | bytes 40
  7.2 6.4 %copy-start.35 = (s32[1,3,16]{2,0,1:T(1,128)S(1)}, s32[1,3,16]{2,0,1:T(1,128)}, u32[]{:S(2)}) copy-start(s32[1,3,16]{2,0,1:T(1,128)} %param.28) | copy-start | bytes 580
  7.2 439.0 %reduce-scatter.3.cloned.1.call-start = ((), (), s32[]{:S(2)}) async-start(), calls=%async_computation.2 | async-start | bytes 7864320 | tf_op jit(solution)/shard_map/reduce_scatter | solution.py:134
  9.6 4.0 copy-start.12
  10.6 43.7 %collective-permute-start.1 = (bf16[128,8,256]{2,1,0:T(8,128)(2,1)}, bf16[128,8,256]{2,1,0:T(8,128)(2,1)}, u32[]{:S(2)}, u32[]{:S(2)}) collective-permute-start(bf16[128,8,256]{2,1,0:T(8,128)(2,1)} %bitcast_select_fusion.5), channel_id=1, source_target_pairs={{0,8},{8,0},{4,12},{12,4},{1,9},{9,1},{5,13},{13,5},{2,10},{10,2},... | collective-permute-start | bytes 1572872 | tf_op jit(solution)/shard_map/ppermute | solution.py:14
  13.5 40.7 %collective-permute-start = (bf16[128,8,256]{2,1,0:T(8,128)(2,1)}, bf16[128,8,256]{2,1,0:T(8,128)(2,1)}, u32[]{:S(2)}, u32[]{:S(2)}) collective-permute-start(bf16[128,8,256]{2,1,0:T(8,128)(2,1)} %bitcast_select_fusion.5), channel_id=1, source_target_pairs={{0,4},{4,0},{8,12},{12,8},{1,5},{5,1},{9,13},{13,9},{2,6},{6,2},{1... | collective-permute-start | bytes 1572872 | tf_op jit(solution)/shard_map/ppermute | solution.py:14
  38.2 2.8 copy-start.7
  41.1 11.1 %copy-start.30 = (bf16[1,128,2048]{2,1,0:T(8,128)(2,1)S(1)}, bf16[1,128,2048]{2,1,0:T(8,128)(2,1)}, u32[]{:S(2)}) copy-start(bf16[1,128,2048]{2,1,0:T(8,128)(2,1)} %get-tuple-element.267) | copy-start | bytes 1572868
  52.1 1.5 copy-start.36
  68.3 46.0 %copy-start.13 = (bf16[16,8,8,256]{3,2,1,0:T(8,128)(2,1)S(1)}, bf16[16,8,8,256]{3,2,1,0:T(8,128)(2,1)}, u32[]{:S(2)}) copy-start(bf16[16,8,8,256]{3,2,1,0:T(8,128)(2,1)} %copy-done.12) | copy-start | bytes 1572868
  68.4 14.4 %collective-permute-start.3 = (bf16[128,8,256]{2,1,0:T(8,128)(2,1)S(1)}, bf16[128,8,256]{2,1,0:T(8,128)(2,1)S(1)}, u32[]{:S(2)}, u32[]{:S(2)}) collective-permute-start(bf16[128,8,256]{2,1,0:T(8,128)(2,1)S(1)} %get-tuple-element.272), channel_id=1, source_target_pairs={{0,8},{8,0},{4,12},{12,4},{1,9},{9,1},{5,13},{13,5},{2,10},{10,2},... | collective-permute-start | bytes 1572872 | tf_op jit(solution)/shard_map/ppermute | solution.py:14
  68.5 14.3 %collective-permute-start.2 = (bf16[128,8,256]{2,1,0:T(8,128)(2,1)S(1)}, bf16[128,8,256]{2,1,0:T(8,128)(2,1)S(1)}, u32[]{:S(2)}, u32[]{:S(2)}) collective-permute-start(bf16[128,8,256]{2,1,0:T(8,128)(2,1)S(1)} %get-tuple-element.271), channel_id=1, source_target_pairs={{0,4},{4,0},{8,12},{12,8},{1,5},{5,1},{9,13},{13,9},{2,6},{6,2},{1... | collective-permute-start | bytes 1572872 | tf_op jit(solution)/shard_map/ppermute | solution.py:14
  85.0 30.1 %copy-start.27 = (bf16[128,8,256]{2,1,0:T(8,128)(2,1)}, bf16[128,8,256]{2,1,0:T(8,128)(2,1)S(1)}, u32[]{:S(2)}) copy-start(bf16[128,8,256]{2,1,0:T(8,128)(2,1)S(1)} %get-tuple-element.255) | copy-start | bytes 1572868
  85.0 29.2 %collective-permute-start.4 = (bf16[128,8,256]{2,1,0:T(8,128)(2,1)S(1)}, bf16[128,8,256]{2,1,0:T(8,128)(2,1)S(1)}, u32[]{:S(2)}, u32[]{:S(2)}) collective-permute-start(bf16[128,8,256]{2,1,0:T(8,128)(2,1)S(1)} %get-tuple-element.255), channel_id=1, source_target_pairs={{16,0},{17,1},{18,2},{19,3},{20,4},{21,5},{22,6},{23,7},{24,8},{25... | collective-permute-start | bytes 1572872 | tf_op jit(solution)/shard_map/ppermute | solution.py:20
  115.2 13.3 %collective-permute-start.6 = (bf16[128,8,256]{2,1,0:T(8,128)(2,1)}, bf16[128,8,256]{2,1,0:T(8,128)(2,1)}, u32[]{:S(2)}, u32[]{:S(2)}) collective-permute-start(bf16[128,8,256]{2,1,0:T(8,128)(2,1)} %bitcast_select_fusion.4), channel_id=1, source_target_pairs={{0,8},{8,0},{4,12},{12,4},{1,9},{9,1},{5,13},{13,5},{2,10},{10,2},... | collective-permute-start | bytes 1572872 | tf_op jit(solution)/shard_map/ppermute | solution.py:14
  115.7 12.7 %collective-permute-start.5 = (bf16[128,8,256]{2,1,0:T(8,128)(2,1)}, bf16[128,8,256]{2,1,0:T(8,128)(2,1)}, u32[]{:S(2)}, u32[]{:S(2)}) collective-permute-start(bf16[128,8,256]{2,1,0:T(8,128)(2,1)} %bitcast_select_fusion.4), channel_id=1, source_target_pairs={{0,4},{4,0},{8,12},{12,8},{1,5},{5,1},{9,13},{13,9},{2,6},{6,2},{1... | collective-permute-start | bytes 1572872 | tf_op jit(solution)/shard_map/ppermute | solution.py:14
  140.4 2.4 copy-start.32
  140.4 9.0 %slice-start.2 = ((s8[6291456]{0:T(1024)(128)(4,1)}), s8[4194304]{0:T(1024)(128)(4,1)S(1)}, s32[]{:S(2)}) async-start(s8[6291456]{0:T(1024)(128)(4,1)} %bitcast.315), calls=%async_computation.6 | async-start | bytes 8388608 | tf_op jit(solution)/shard_map/cond
  142.8 6.6 %copy-start.5 = (bf16[3,128,16,256]{3,1,2,0:T(8,128)(2,1)}, bf16[3,128,16,256]{3,1,2,0:T(8,128)(2,1)S(1)}, u32[]{:S(2)}) copy-start(bf16[3,128,16,256]{3,1,2,0:T(8,128)(2,1)S(1)} %select_bitcast_fusion.1) | copy-start | bytes 9437188 | tf_op jit(solution)/shard_map/cond
  142.8 6.6 %slice-start.3 = ((s8[6291456]{0:T(1024)(128)(4,1)}), s8[2097152]{0:T(1024)(128)(4,1)S(1)}, s32[]{:S(2)}) async-start(s8[6291456]{0:T(1024)(128)(4,1)} %bitcast.315), calls=%async_computation.7 | async-start | bytes 4194304 | tf_op jit(solution)/shard_map/cond
  149.4 2.2 copy-start.9
  169.1 12.2 %copy-start.28 = (bf16[128,8,256]{2,1,0:T(8,128)(2,1)S(1)}, bf16[128,8,256]{2,1,0:T(8,128)(2,1)}, u32[]{:S(2)}) copy-start(bf16[128,8,256]{2,1,0:T(8,128)(2,1)} %copy-done.27) | copy-start | bytes 1572868
  169.2 15.7 %copy-start.29 = (bf16[1,128,2048]{2,1,0:T(8,128)(2,1)S(1)}, bf16[1,128,2048]{2,1,0:T(8,128)(2,1)}, u32[]{:S(2)}) copy-start(bf16[1,128,2048]{2,1,0:T(8,128)(2,1)} %get-tuple-element.266) | copy-start | bytes 1572868
  169.2 12.1 %collective-permute-start.8 = (bf16[128,8,256]{2,1,0:T(8,128)(2,1)S(1)}, bf16[128,8,256]{2,1,0:T(8,128)(2,1)S(1)}, u32[]{:S(2)}, u32[]{:S(2)}) collective-permute-start(bf16[128,8,256]{2,1,0:T(8,128)(2,1)S(1)} %get-tuple-element.270), channel_id=1, source_target_pairs={{0,8},{8,0},{4,12},{12,4},{1,9},{9,1},{5,13},{13,5},{2,10},{10,2},... | collective-permute-start | bytes 1572872 | tf_op jit(solution)/shard_map/ppermute | solution.py:14
  169.8 11.5 %collective-permute-start.7 = (bf16[128,8,256]{2,1,0:T(8,128)(2,1)S(1)}, bf16[128,8,256]{2,1,0:T(8,128)(2,1)S(1)}, u32[]{:S(2)}, u32[]{:S(2)}) collective-permute-start(bf16[128,8,256]{2,1,0:T(8,128)(2,1)S(1)} %get-tuple-element.269), channel_id=1, source_target_pairs={{0,4},{4,0},{8,12},{12,8},{1,5},{5,1},{9,13},{13,9},{2,6},{6,2},{1... | collective-permute-start | bytes 1572872 | tf_op jit(solution)/shard_map/ppermute | solution.py:14
  183.6 13.0 %collective-permute-start.9 = (bf16[128,8,256]{2,1,0:T(8,128)(2,1)S(1)}, bf16[128,8,256]{2,1,0:T(8,128)(2,1)S(1)}, u32[]{:S(2)}, u32[]{:S(2)}) collective-permute-start(bf16[128,8,256]{2,1,0:T(8,128)(2,1)S(1)} %get-tuple-element.253), channel_id=1, source_target_pairs={{16,0},{17,1},{18,2},{19,3},{20,4},{21,5},{22,6},{23,7},{24,8},{25... | collective-permute-start | bytes 1572872 | tf_op jit(solution)/shard_map/ppermute | solution.py:20
  185.1 11.6 %copy-start.18 = (bf16[16,8,8,256]{3,2,1,0:T(8,128)(2,1)}, bf16[16,8,8,256]{3,2,1,0:T(8,128)(2,1)S(1)}, u32[]{:S(2)}) copy-start(bf16[16,8,8,256]{3,2,1,0:T(8,128)(2,1)S(1)} %copy.198) | copy-start | bytes 1572868
  197.6 10.5 %collective-permute-start.11 = (bf16[128,8,256]{2,1,0:T(8,128)(2,1)}, bf16[128,8,256]{2,1,0:T(8,128)(2,1)}, u32[]{:S(2)}, u32[]{:S(2)}) collective-permute-start(bf16[128,8,256]{2,1,0:T(8,128)(2,1)} %bitcast_select_fusion.3), channel_id=1, source_target_pairs={{0,8},{8,0},{4,12},{12,4},{1,9},{9,1},{5,13},{13,5},{2,10},{10,2},... | collective-permute-start | bytes 1572872 | tf_op jit(solution)/shard_map/ppermute | solution.py:14
  198.1 10.0 %collective-permute-start.10 = (bf16[128,8,256]{2,1,0:T(8,128)(2,1)}, bf16[128,8,256]{2,1,0:T(8,128)(2,1)}, u32[]{:S(2)}, u32[]{:S(2)}) collective-permute-start(bf16[128,8,256]{2,1,0:T(8,128)(2,1)} %bitcast_select_fusion.3), channel_id=1, source_target_pairs={{0,4},{4,0},{8,12},{12,8},{1,5},{5,1},{9,13},{13,9},{2,6},{6,2},{1... | collective-permute-start | bytes 1572872 | tf_op jit(solution)/shard_map/ppermute | solution.py:14
  216.3 10.6 %collective-permute-start.13 = (bf16[128,8,256]{2,1,0:T(8,128)(2,1)}, bf16[128,8,256]{2,1,0:T(8,128)(2,1)}, u32[]{:S(2)}, u32[]{:S(2)}) collective-permute-start(bf16[128,8,256]{2,1,0:T(8,128)(2,1)} %get-tuple-element.265), channel_id=1, source_target_pairs={{0,8},{8,0},{4,12},{12,4},{1,9},{9,1},{5,13},{13,5},{2,10},{10,2},... | collective-permute-start | bytes 1572872 | tf_op jit(solution)/shard_map/ppermute | solution.py:14
  216.9 10.0 %collective-permute-start.12 = (bf16[128,8,256]{2,1,0:T(8,128)(2,1)}, bf16[128,8,256]{2,1,0:T(8,128)(2,1)}, u32[]{:S(2)}, u32[]{:S(2)}) collective-permute-start(bf16[128,8,256]{2,1,0:T(8,128)(2,1)} %get-tuple-element.264), channel_id=1, source_target_pairs={{0,4},{4,0},{8,12},{12,8},{1,5},{5,1},{9,13},{13,9},{2,6},{6,2},{1... | collective-permute-start | bytes 1572872 | tf_op jit(solution)/shard_map/ppermute | solution.py:14
  221.4 27.0 %collective-permute-start.20 = (bf16[2,128,8,256]{3,1,2,0:T(8,128)(2,1)}, bf16[2,128,8,256]{3,1,2,0:T(8,128)(2,1)}, u32[]{:S(2)}, u32[]{:S(2)}) collective-permute-start(bf16[2,128,8,256]{3,1,2,0:T(8,128)(2,1)} %copy.164), channel_id=1, source_target_pairs={{0,8},{8,0},{4,12},{12,4},{1,9},{9,1},{5,13},{13,5},{2,10},{10,2},... | collective-permute-start | bytes 3145736 | tf_op jit(solution)/shard_map/ppermute | solution.py:14
  222.8 25.5 %collective-permute-start.19 = (bf16[2,128,8,256]{3,1,2,0:T(8,128)(2,1)}, bf16[2,128,8,256]{3,1,2,0:T(8,128)(2,1)}, u32[]{:S(2)}, u32[]{:S(2)}) collective-permute-start(bf16[2,128,8,256]{3,1,2,0:T(8,128)(2,1)} %copy.164), channel_id=1, source_target_pairs={{0,4},{4,0},{8,12},{12,8},{1,5},{5,1},{9,13},{13,9},{2,6},{6,2},{1... | collective-permute-start | bytes 3145736 | tf_op jit(solution)/shard_map/ppermute | solution.py:14
  225.5 6.0 %copy-start.3 = (bf16[128,16,256]{2,0,1:T(8,128)(2,1)S(1)}, bf16[128,16,256]{2,0,1:T(8,128)(2,1)}, u32[]{:S(2)}) copy-start(bf16[128,16,256]{2,0,1:T(8,128)(2,1)} %get-tuple-element.102) | copy-start | bytes 3145732
  230.0 18.3 %copy-start.24 = (bf16[1,2,128,8,256]{4,2,3,1,0:T(8,128)(2,1)S(1)}, bf16[1,2,128,8,256]{4,2,3,1,0:T(8,128)(2,1)}, u32[]{:S(2)}) copy-start(bf16[1,2,128,8,256]{4,2,3,1,0:T(8,128)(2,1)} %copy.166) | copy-start | bytes 3145732
  230.0 40.5 %collective-permute-start.14 = (bf16[128,8,256]{2,1,0:T(8,128)(2,1)}, bf16[128,8,256]{2,1,0:T(8,128)(2,1)}, u32[]{:S(2)}, u32[]{:S(2)}) collective-permute-start(bf16[128,8,256]{2,1,0:T(8,128)(2,1)} %get-tuple-element.251), channel_id=1, source_target_pairs={{16,0},{17,1},{18,2},{19,3},{20,4},{21,5},{22,6},{23,7},{24,8},{25... | collective-permute-start | bytes 1572872 | tf_op jit(solution)/shard_map/ppermute | solution.py:20
  259.0 11.5 %copy-start.19 = (bf16[16,8,8,256]{3,2,1,0:T(8,128)(2,1)S(1)}, bf16[16,8,8,256]{3,2,1,0:T(8,128)(2,1)}, u32[]{:S(2)}) copy-start(bf16[16,8,8,256]{3,2,1,0:T(8,128)(2,1)} %copy-done.18) | copy-start | bytes 1572868
  261.6 12.0 %copy-start.15 = (bf16[2,128,16,256]{3,1,2,0:T(8,128)(2,1)S(1)}, bf16[2,128,16,256]{3,1,2,0:T(8,128)(2,1)}, u32[]{:S(2)}) copy-start(bf16[2,128,16,256]{3,1,2,0:T(8,128)(2,1)} %bitcast_dynamic-update-slice_fusion.5) | copy-start | bytes 6291460
  271.6 13.5 %copy-start.20 = (bf16[128,8,256]{2,1,0:T(8,128)(2,1)}, bf16[128,8,256]{2,1,0:T(8,128)(2,1)S(1)}, u32[]{:S(2)}) copy-start(bf16[128,8,256]{2,1,0:T(8,128)(2,1)S(1)} %bitcast_select_fusion.2) | copy-start | bytes 1572868
  271.6 12.2 %collective-permute-start.16 = (bf16[128,8,256]{2,1,0:T(8,128)(2,1)S(1)}, bf16[128,8,256]{2,1,0:T(8,128)(2,1)S(1)}, u32[]{:S(2)}, u32[]{:S(2)}) collective-permute-start(bf16[128,8,256]{2,1,0:T(8,128)(2,1)S(1)} %bitcast_select_fusion.2), channel_id=1, source_target_pairs={{0,8},{8,0},{4,12},{12,4},{1,9},{9,1},{5,13},{13,5},{2,10},{10,2},... | collective-permute-start | bytes 1572872 | tf_op jit(solution)/shard_map/ppermute | solution.py:14
  272.3 11.6 %collective-permute-start.15 = (bf16[128,8,256]{2,1,0:T(8,128)(2,1)S(1)}, bf16[128,8,256]{2,1,0:T(8,128)(2,1)S(1)}, u32[]{:S(2)}, u32[]{:S(2)}) collective-permute-start(bf16[128,8,256]{2,1,0:T(8,128)(2,1)S(1)} %bitcast_select_fusion.2), channel_id=1, source_target_pairs={{0,4},{4,0},{8,12},{12,8},{1,5},{5,1},{9,13},{13,9},{2,6},{6,2},{1... | collective-permute-start | bytes 1572872 | tf_op jit(solution)/shard_map/ppermute | solution.py:14
  273.6 11.5 %copy-start.8 = (bf16[128,16,256]{2,0,1:T(8,128)(2,1)}, bf16[128,16,256]{2,0,1:T(8,128)(2,1)S(1)}, u32[]{:S(2)}) copy-start(bf16[128,16,256]{2,0,1:T(8,128)(2,1)S(1)} %fusion.111) | copy-start | bytes 3145732
  273.7 11.4 %copy-start.16 = (bf16[2,128,16,256]{3,1,2,0:T(8,128)(2,1)}, bf16[2,128,16,256]{3,1,2,0:T(8,128)(2,1)S(1)}, u32[]{:S(2)}) copy-start(bf16[2,128,16,256]{3,1,2,0:T(8,128)(2,1)S(1)} %bitcast_dynamic-update-slice_fusion.4) | copy-start | bytes 6291460
  294.6 4.1 copy-start.34
  294.6 10.6 %slice-start.6 = ((s8[6291456]{0:T(1024)(128)(4,1)}), s8[4194304]{0:T(1024)(128)(4,1)S(1)}, s32[]{:S(2)}) async-start(s8[6291456]{0:T(1024)(128)(4,1)} %bitcast.319), calls=%async_computation.10 | async-start | bytes 8388608 | tf_op jit(solution)/shard_map/cond
  298.7 6.5 %slice-start.7 = ((s8[6291456]{0:T(1024)(128)(4,1)}), s8[2097152]{0:T(1024)(128)(4,1)S(1)}, s32[]{:S(2)}) async-start(s8[6291456]{0:T(1024)(128)(4,1)} %bitcast.319), calls=%async_computation.11 | async-start | bytes 4194304 | tf_op jit(solution)/shard_map/cond
  305.2 2.2 copy-start.10
  314.5 1.2 copy-start.11
  316.2 1.6 copy-start.22
  316.2 1.7 copy-start.25
  335.0 224.7 %reduce-scatter.5.cloned.1.call-start = ((), (), s32[]{:S(2)}) async-start(), calls=%async_computation.3 | async-start | bytes 7864320 | tf_op jit(solution)/shard_map/reduce_scatter | solution.py:131
  339.7 2.2 copy-start.6
  346.9 2.7 copy-start.4
  361.4 0.7 copy-start.38
  361.4 1.3 copy-start.23
  361.4 2.7 copy-start.17
  361.4 13.6 %copy-start.21 = (bf16[128,8,256]{2,1,0:T(8,128)(2,1)S(1)}, bf16[128,8,256]{2,1,0:T(8,128)(2,1)}, u32[]{:S(2)}) copy-start(bf16[128,8,256]{2,1,0:T(8,128)(2,1)} %copy-done.20) | copy-start | bytes 1572868
  361.4 13.6 %copy-start.26 = (f32[128,8,256]{2,1,0:T(8,128)S(1)}, f32[128,8,256]{2,1,0:T(8,128)}, u32[]{:S(2)}) copy-start(f32[128,8,256]{2,1,0:T(8,128)} %copy-done.25) | copy-start | bytes 3145732
  362.7 12.3 %collective-permute-start.18 = (bf16[128,8,256]{2,1,0:T(8,128)(2,1)S(1)}, bf16[128,8,256]{2,1,0:T(8,128)(2,1)S(1)}, u32[]{:S(2)}, u32[]{:S(2)}) collective-permute-start(bf16[128,8,256]{2,1,0:T(8,128)(2,1)S(1)} %get-tuple-element.263), channel_id=1, source_target_pairs={{0,8},{8,0},{4,12},{12,4},{1,9},{9,1},{5,13},{13,5},{2,10},{10,2},... | collective-permute-start | bytes 1572872 | tf_op jit(solution)/shard_map/ppermute | solution.py:14
  364.0 11.0 %collective-permute-start.17 = (bf16[128,8,256]{2,1,0:T(8,128)(2,1)S(1)}, bf16[128,8,256]{2,1,0:T(8,128)(2,1)S(1)}, u32[]{:S(2)}, u32[]{:S(2)}) collective-permute-start(bf16[128,8,256]{2,1,0:T(8,128)(2,1)S(1)} %get-tuple-element.262), channel_id=1, source_target_pairs={{0,4},{4,0},{8,12},{12,8},{1,5},{5,1},{9,13},{13,9},{2,6},{6,2},{1... | collective-permute-start | bytes 1572872 | tf_op jit(solution)/shard_map/ppermute | solution.py:14
Sparse Core Ops, SparseCore 0:
  335.2 110.9 reduce-scatter.2
  448.5 111.2 reduce-scatter.4
where the time goes:
time: 576 us; the launch traced here: 575 us
  waiting for transfers between devices  300 us (52%)
  local copies, waits for them, and re-layouts  112 us (19%)
  other arithmetic  65.8 us (11%)
  matrix products  48.3 us (8%)
  loops' own time  21.1 us (4%)
  between operations  14.8 us (3%)
  starting transfers between devices  13.8 us (2%)
    reduce_scatter x1, waiting for transfers between devices, local(): lax.psum_scatter(acc_down.astype(jnp.bfloat16), 'dp', scatter_dimension=3...  103 us
    ppermute x18, waiting for transfers between devices, from_partner(): return lax.ppermute(block, axis, route)  80.5 us
    reduce_scatter x1, waiting for transfers between devices, local(): lax.psum_scatter(acc_up.astype(jnp.bfloat16), 'dp', scatter_dimension=2,...  67.5 us
    ppermute x3, waiting for transfers between devices, shifted(): lax.ppermute(value, axis, [(source, source + steps) for source in range(f...  48.4 us
    another operation x4, loops' own time, local(): lax.cond(running, do_work, skip_work, (g_stack, pre_now))  21.1 us
    unnamed x64, local copies, waits for them, and re-layouts  19.4 us
    another operation x12, local copies, waits for them, and re-layouts  16.4 us
    dot_general x2, matrix products, do_work(): jnp.einsum('ftjc,fje->ftec', product, onehot_up, precision=highest)  14.2 us
  transfers between devices with their start and end apart: 23, of which 13 were waited for; matrix products, arithmetic and copies ran while one was open for 19% of the time, Pallas kernels for 0%

commit v1 on v0

v1 whole, which is shorter than its diff:
```python
import functools
import itertools

import jax
import jax.numpy as jnp
from jax import lax
from jax.experimental import pallas as pl
from jax.experimental.pallas import tpu as pltpu
from jax.sharding import PartitionSpec as P

AXES = ("section", "hid", "dp")
VMEM_LIMIT = 52 * 1024 * 1024
ROOT = 0.7978845608028654
CUBE = 0.044715
F32 = jnp.float32
BF16 = jnp.bfloat16


def send(value, target):
    sizes = [lax.axis_size(axis) for axis in AXES]

    def flat(at):
        return (at[0] * sizes[1] + at[1]) * sizes[2] + at[2]

    route = []
    for at in itertools.product(*(range(size) for size in sizes)):
        to = target(*at)
        if to is not None:
            route.append((flat(at), flat(to)))
    return lax.ppermute(value, AXES, route)


def end_to_near(value):
    return send(value, lambda s, h, z: {0: (s, h, 1), 3: (s, h, 2)}.get(z))


def end_to_far(value):
    return send(value, lambda s, h, z: {0: (s, h, 2), 3: (s, h, 1)}.get(z))


def near_to_end(value):
    return send(value, lambda s, h, z: {1: (s, h, 0), 2: (s, h, 3)}.get(z))


def mid_to_far(value):
    return send(value, lambda s, h, z: {1: (s, h, 3), 2: (s, h, 0)}.get(z))


def mid_swap(value):
    return send(value, lambda s, h, z: {1: (s, h, 2), 2: (s, h, 1)}.get(z))


def mid_partner(value, bit):
    return send(value, lambda s, h, z: (s, h ^ 1 << bit, z) if z in (1, 2) else None)


def section_partner(value, bit, active):
    return send(value, lambda s, h, z: (s, h ^ 1 << bit, z) if s == active else None)


def section_down(value, active):
    return send(value, lambda s, h, z: (s - 1, h, z) if s == active else None)


def chain_body(factors, steps, per_step, blk, fgroup, info, pick_up, pick_down, *refs):
    g_refs, refs = refs[:factors], refs[factors:]
    pre_ref, refs = refs[0], refs[1:]
    down_refs, refs = refs[:factors], refs[factors:]
    up_refs, refs = refs[:factors], refs[factors:]
    du_old, gm_old, go_old = refs[:3]
    du_ref, gm_ref, go_ref, own_ref = refs[3:7]
    cross_refs, total = refs[7:-1], refs[-1]
    hgroup = steps * per_step
    half_width = blk // 2
    step = pl.program_id(0)
    active = info[0] == 1

    @pl.when(jnp.logical_not(active))
    def _():
        du_ref[...] = du_old[...]

        @pl.when(step == 0)
        def _():
            gm_ref[...] = gm_old[...]
            go_ref[...] = go_old[...]

    @pl.when(active)
    def _():
        @pl.when(step == 0)
        def _():
            total[...] = jnp.zeros_like(total)
            half = info[1]
            for b in range(fgroup):
                mine = pl.ds(pl.multiple_of(b * blk + half * half_width, half_width), half_width)
                other = pl.ds(
                    pl.multiple_of(b * blk + (1 - half) * half_width, half_width), half_width
                )
                place = slice(b * half_width, (b + 1) * half_width)
                for f in range(factors):
                    gm_ref[f, :, place] = g_refs[f][:, mine]
                go_ref[:, place] = g_refs[0][:, other]

        for k in range(per_step):
            j = step * per_step + k
            columns = slice(k * blk, (k + 1) * blk)
            da = None
            for f in range(factors):
                pick = pick_down[info[2 + f] * hgroup + j]
                chosen = g_refs[f][:, pl.ds(pl.multiple_of(pick * blk, blk), blk)]
                part = lax.dot_general(
                    chosen, down_refs[f][0, 0, k], (((1,), (1,)), ((), ())), preferred_element_type=F32
                )
                da = part if da is None else da + part
            v = pre_ref[0, 0, :, columns].astype(F32)
            square = v * v
            t = jnp.tanh(ROOT * v * (1.0 + CUBE * square))
            slope = 0.5 * (1.0 + t) + 0.5 * ROOT * v * (1.0 - t * t) * (1.0 + 3.0 * CUBE * square)
            du = (slope * da).astype(BF16)
            du_ref[0, :, columns] = du
            for f in range(factors):
                pick = pick_up[info[2 + f] * hgroup + j]
                place = pl.ds(pl.multiple_of(pick * blk, blk), blk)
                total[f, :, place] += lax.dot_general(
                    du, up_refs[f][0, 0, k], (((1,), (1,)), ((), ())), preferred_element_type=F32
                )

        @pl.when(step == steps - 1)
        def _():
            own_ref[...] = g_refs[0][...].astype(F32) + total[0]
            for f in range(1, factors):
                cross_refs[f - 1][...] = total[f].astype(BF16)


def chain(info, pick_up, pick_down, g_list, pre_act, down_weight, up_weight, du, gm, go, micro, chunks):
    factors = len(g_list)
    tokens, width = g_list[0].shape
    hgroup, blk = up_weight.shape[2], up_weight.shape[-1]
    fgroup = width // blk
    per_step = hgroup // chunks
    wide = per_step * blk
    whole = pl.BlockSpec((tokens, width), lambda j, *s: (0, 0))

    def weight_spec(f):
        return pl.BlockSpec(
            (1, 1, per_step, blk, blk), lambda j, info, *s: (0, info[2 + f], j * info[0], 0, 0)
        )

    du_spec = pl.BlockSpec((1, tokens, wide), lambda j, *s: (j, micro, 0))
    gm_spec = pl.BlockSpec((factors, tokens, width // 2), lambda j, *s: (0, micro, 0))
    go_spec = pl.BlockSpec((tokens, width // 2), lambda j, *s: (micro, 0))
    pre_spec = pl.BlockSpec((1, 1, tokens, wide), lambda j, info, *s: (0, micro, 0, j * info[0]))
    first_alias = 3 + factors + 1 + 2 * factors
    flat = jax.ShapeDtypeStruct((tokens, width), BF16)
    macs = tokens * hgroup * blk * blk * factors * 2
    return pl.pallas_call(
        functools.partial(chain_body, factors, chunks, per_step, blk, fgroup),
        grid_spec=pltpu.PrefetchScalarGridSpec(
            num_scalar_prefetch=3,
            grid=(chunks,),
            in_specs=[whole] * factors
            + [pre_spec]
            + [weight_spec(f) for f in range(factors)] * 2
            + [du_spec, gm_spec, go_spec],
            out_specs=[du_spec, gm_spec, go_spec, whole] + [whole] * (factors - 1),
            scratch_shapes=[pltpu.VMEM((factors, tokens, width), F32)],
        ),
        out_shape=[
            jax.ShapeDtypeStruct(du.shape, BF16),
            jax.ShapeDtypeStruct(gm.shape, BF16),
            jax.ShapeDtypeStruct(go.shape, BF16),
            jax.ShapeDtypeStruct((tokens, width), F32),
        ]
        + [flat] * (factors - 1),
        input_output_aliases={first_alias: 0, first_alias + 1: 1, first_alias + 2: 2},
        compiler_params=pltpu.CompilerParams(vmem_limit_bytes=VMEM_LIMIT),
        cost_estimate=pl.CostEstimate(
            flops=2 * macs, bytes_accessed=4 * factors * hgroup * blk * blk, transcendentals=0
        ),
        name="chain",
    )(
        info,
        pick_up,
        pick_down,
        *g_list,
        pre_act,
        *[down_weight] * factors,
        *[up_weight] * factors,
        du,
        gm,
        go,
    )


def up_body(factors, count, hgroup, blk, first, info, pick_up, *refs):
    own_x, near_x = refs[:factors], refs[factors : 2 * factors]
    du_own, du_near, mine_ref, near_ref, mid_ref, far_ref, held = refs[2 * factors :]
    quarter = blk // 4
    z = info[0]

    def rows(at):
        return pl.ds(pl.multiple_of(at * quarter, quarter), quarter)

    for k in range(count):
        columns = slice(k * blk, (k + 1) * blk)
        for f in range(factors):
            slot = info[1 + f]
            place = pl.ds(pl.multiple_of(pick_up[slot * hgroup + first + k] * blk, blk), blk)
            held[...] = jnp.dot(
                own_x[f][place, :], du_own[0, :, columns], preferred_element_type=F32
            ) + jnp.dot(near_x[f][place, :], du_near[:, columns], preferred_element_type=F32)
            mine_ref[slot, k] = held[rows(z), :]
            near_ref[slot, k] = held[rows(z ^ 1), :].astype(BF16)
            mid_ref[slot, k] = held[rows(3 - z), :].astype(BF16)
            far_ref[slot, k] = held[rows(z ^ 2), :].astype(BF16)


def up_products(info, pick_up, own_x, near_x, du_own, du_near, hgroup, blk, chunk):
    factors = len(own_x)
    width, tokens = own_x[0].shape
    count = du_near.shape[1] // blk
    x_spec = pl.BlockSpec((width, tokens), lambda i, *s: (0, 0))
    shape = (factors, count, blk // 4, blk)
    out_spec = pl.BlockSpec(shape, lambda i, *s: (0, 0, 0, 0))
    return pl.pallas_call(
        functools.partial(up_body, factors, count, hgroup, blk, chunk * count),
        grid_spec=pltpu.PrefetchScalarGridSpec(
            num_scalar_prefetch=2,
            grid=(1,),
            in_specs=[x_spec] * (2 * factors)
            + [
                pl.BlockSpec((1, tokens, count * blk), lambda i, *s: (chunk, 0, 0)),
                pl.BlockSpec((tokens, count * blk), lambda i, *s: (0, 0)),
            ],
            out_specs=[out_spec] * 4,
            scratch_shapes=[pltpu.VMEM((blk, blk), F32)],
        ),
        out_shape=[jax.ShapeDtypeStruct(shape, F32)] + [jax.ShapeDtypeStruct(shape, BF16)] * 3,
        compiler_params=pltpu.CompilerParams(vmem_limit_bytes=VMEM_LIMIT),
        cost_estimate=pl.CostEstimate(
            flops=4 * factors * count * blk * blk * tokens,
            bytes_accessed=4 * factors * width * tokens,
            transcendentals=0,
        ),
        name="up_products",
    )(info, pick_up, *own_x, *near_x, du_own, du_near)


def down_body(factors, per_step, hgroup, blk, first, info, pick_down, *refs):
    acts, refs = refs[:4], refs[4:]
    gm_own, refs = refs[0], refs[1:]
    others = [refs[factors * i : factors * (i + 1)] for i in range(3)]
    mine_ref, end_ref = refs[3 * factors :]
    half = blk // 2
    quarter = blk // 4
    odd = info[0] % 2 == 1
    for k in range(per_step):
        j = first + pl.program_id(0) * per_step + k
        rows = slice(k * blk, (k + 1) * blk)
        for f in range(factors):
            slot = info[1 + f]
            place = pl.ds(pl.multiple_of(pick_down[slot * hgroup + j] * half, half), half)
            acc = jnp.dot(acts[0][0, rows, :], gm_own[f, :, place], preferred_element_type=F32)
            for i in range(3):
                acc += jnp.dot(
                    acts[1 + i][rows, :], others[i][f][:, place], preferred_element_type=F32
                )
            low, high = acc[:, :quarter], acc[:, quarter:]
            mine, end = jnp.where(odd, high, low), jnp.where(odd, low, high)
            mine_ref[slot, k] = jnp.concatenate([mine[:half], mine[half:]], axis=1)
            end_ref[slot, k] = jnp.concatenate([end[:half], end[half:]], axis=1).astype(BF16)


def down_products(info, pick_down, act_own, act_others, gm_own, g_others, hgroup, blk, part):
    factors = gm_own.shape[0]
    tokens, half_width = gm_own.shape[1:]
    depth = act_own.shape[1]
    count = depth // blk
    per_step = min(2, count)
    out_shape = (factors, count, blk // 2, blk // 2)
    out_spec = pl.BlockSpec((factors, per_step) + out_shape[2:], lambda i, *s: (0, i, 0, 0))
    g_spec = pl.BlockSpec((tokens, half_width), lambda i, *s: (0, 0))
    return pl.pallas_call(
        functools.partial(down_body, factors, per_step, hgroup, blk, part * count),
        grid_spec=pltpu.PrefetchScalarGridSpec(
            num_scalar_prefetch=2,
            grid=(count // per_step,),
            in_specs=[pl.BlockSpec((1, per_step * blk, tokens), lambda i, *s: (part, i, 0))]
            + [pl.BlockSpec((per_step * blk, tokens), lambda i, *s: (i, 0))] * 3
            + [pl.BlockSpec((factors, tokens, half_width), lambda i, *s: (0, 0, 0))]
            + [g_spec] * (3 * factors),
            out_specs=[out_spec] * 2,
        ),
        out_shape=[jax.ShapeDtypeStruct(out_shape, F32), jax.ShapeDtypeStruct(out_shape, BF16)],
        compiler_params=pltpu.CompilerParams(vmem_limit_bytes=VMEM_LIMIT),
        cost_estimate=pl.CostEstimate(
            flops=4 * factors * count * blk * blk * tokens,
            bytes_accessed=8 * depth * tokens + 8 * factors * tokens * half_width,
            transcendentals=0,
        ),
        name="down_products",
    )(info, pick_down, act_own, *act_others, gm_own, *itertools.chain(*g_others))


def down_finish_body(parts, info, *refs):
    mine, given, out = refs[:parts], refs[parts : 2 * parts], refs[-1]
    middle = info[0] == 1
    quarter = out.shape[-1]
    part = pl.program_id(1)
    for p in range(parts):

        @pl.when(part == p)
        def _():
            value = jnp.where(middle, mine[p][...], given[p][...].astype(F32))
            out[0, :, :, : 2 * quarter, :] = value[:, :, :, :quarter]
            out[0, :, :, 2 * quarter :, :] = value[:, :, :, quarter:]


def down_finish(info, mine, given, blk):
    parts = len(mine)
    factors, count, half, _ = mine[0].shape
    out = (1, factors, parts * count, blk, blk // 4)
    spec = pl.BlockSpec((1, count, half, half), lambda f, p, *s: (f, 0, 0, 0))
    return pl.pallas_call(
        functools.partial(down_finish_body, parts),
        grid_spec=pltpu.PrefetchScalarGridSpec(
            num_scalar_prefetch=1,
            grid=(factors, parts),
            in_specs=[spec] * (2 * parts),
            out_specs=pl.BlockSpec((1, 1, count, blk, blk // 4), lambda f, p, *s: (0, f, p, 0, 0)),
        ),
        out_shape=jax.ShapeDtypeStruct(out, F32),
        compiler_params=pltpu.CompilerParams(vmem_limit_bytes=VMEM_LIMIT),
        name="down_finish",
    )(info, *mine, *given)


def gelu_tanh(values):
    return jax.nn.gelu(values, approximate=True)


def local(acts_in, pre_act, out_grad, up_weight, down_weight, up_pick, down_pick, factor_order):
    bits = lax.axis_size("hid").bit_length() - 1
    factors = bits + 1
    sections = lax.axis_size("section")
    section = lax.axis_index("section")
    z = lax.axis_index("dp")
    middle = jnp.logical_or(z == 1, z == 2)
    micros, tokens, width = acts_in.shape[1:]
    hgroup, blk = up_weight.shape[2], up_weight.shape[-1]
    hidden = hgroup * blk
    rows = micros * tokens
    chunks, parts = 4, 2
    order = factor_order[0]
    pick_up = up_pick.reshape(-1)
    pick_down = down_pick.reshape(-1)
    place = jnp.concatenate([z[None].astype(jnp.int32), order])

    x_own = acts_in[0].reshape(rows, width).T
    x_near = end_to_near(x_own)
    act = gelu_tanh(pre_act[0].astype(F32)).astype(BF16).reshape(rows, hidden).T
    act = act.reshape(parts, hidden // parts, rows)
    act_mid = [mid_swap(act[p]) for p in range(parts)]
    act_near = [end_to_near(act[p]) for p in range(parts)]
    act_far = [mid_swap(act_near[p]) for p in range(parts)]

    du = jnp.zeros((chunks, rows, hidden // chunks), BF16)
    gm = jnp.zeros((factors, rows, width // 2), BF16)
    go = jnp.zeros((rows, width // 2), BF16)
    g_now = [out_grad[m] for m in range(micros)]
    grad = [None] * micros
    x_groups = None
    for step in range(sections):
        active = sections - 1 - step
        here = section == active
        info = jnp.concatenate(
            [jnp.stack([here.astype(jnp.int32), (z // 2).astype(jnp.int32)]), order]
        )
        g_all = [
            [g_now[m]] + [section_partner(g_now[m], bit, active) for bit in range(bits)]
            for m in range(micros)
        ]
        results = []
        for m in range(micros):
            du, gm, go, own, *cross = chain(
                info, pick_up, pick_down, g_all[m], pre_act, down_weight, up_weight, du, gm, go, m, chunks
            )
            total = own
            for bit in range(bits):
                total = total + section_partner(cross[bit], bit, active).astype(F32)
            results.append(total.astype(BF16))
        for m in range(micros):
            grad[m] = results[m] if step == 0 else jnp.where(here, results[m], grad[m])
        if step + 1 < sections:
            g_now = [section_down(results[m], active) for m in range(micros)]
        if x_groups is None:
            x_groups = [
                [value] + [mid_partner(value, bit) for bit in range(bits)] for value in (x_own, x_near)
            ]

    g_near, g_mid, g_far = end_to_near(gm[0]), mid_swap(go), end_to_far(go)
    g_others = [
        [value] + [mid_partner(value, bit) for bit in range(bits)] for value in (g_near, g_mid, g_far)
    ]
    down_mine, down_given = [], []
    for p in range(parts):
        mine, end = down_products(
            place, pick_down, act, (act_near[p], act_mid[p], act_far[p]), gm, g_others, hgroup, blk, p
        )
        down_mine.append(mine)
        down_given.append(near_to_end(end))
    down_grad = down_finish(middle.astype(jnp.int32)[None], down_mine, down_given, blk)

    up_parts = []
    for q in range(chunks):
        du_near = end_to_near(du[q])
        mine, near, mid, far = up_products(
            place, pick_up, x_groups[0], x_groups[1], du, du_near, hgroup, blk, q
        )
        from_near, from_mid, from_far = near_to_end(near), mid_swap(mid), mid_to_far(far)
        up_parts.append(
            jnp.where(
                middle,
                mine + from_mid.astype(F32),
                from_near.astype(F32) + from_far.astype(F32),
            )
        )
    up_grad = jnp.concatenate(up_parts, axis=1)[None]
    grad_in = jnp.stack(grad)[None]
    return grad_in, up_grad, down_grad


def solution(mesh):
    placed = (
        P("section", None, "dp", "hid"),
        P("section", None, "dp", "hid"),
        P(None, "dp", "hid"),
        P("section", None, "hid", None, None),
        P("section", None, "hid", None, None),
        P("section", None, "hid"),
        P("section", None, "hid"),
        P("section", None),
    )
    return jax.shard_map(
        local,
        mesh=mesh,
        in_specs=placed,
        out_specs=(
            P("section", None, "dp", "hid"),
            P("section", None, "hid", "dp", None),
            P("section", None, "hid", None, "dp"),
        ),
        check_vma=False,
    )
```

time: 576 us -> 411 us (0.71)
  waiting for transfers between devices: 300 us -> 167 us
  starting transfers between devices: 13.8 us -> 112 us
  local copies, waits for them, and re-layouts: 112 us -> 25.7 us
  Pallas kernels: 0 us -> 84.9 us
  other arithmetic: 65.8 us -> 13.8 us
  matrix products: 48.3 us -> 0 us
  loops' own time: 21.1 us -> 0 us
  between operations: 14.8 us -> 1.74 us
    reduce_scatter x2 -> x0, waiting for transfers between devices: 171 us -> none  [the longest x1 103 us: local(): lax.psum_scatter(acc_down.astype(jnp.bfloat16), 'dp', scatter_dimension=3...]
    ppermute x21 -> x56, starting transfers between devices: 13.5 us -> 112 us  [send(): return lax.ppermute(value, AXES, route)]
    pallas_call x0 -> x11, Pallas kernels: none -> 84.9 us  [the longest x4 36.4 us: chain(): pl.pallas_call(functools.partial(chain_body, factors, chunks, per_step, b...]
    dot_general x8 -> x0, matrix products: 48.3 us -> none  [the longest x2 14.2 us: do_work(): jnp.einsum('ftjc,fje->ftec', product, onehot_up, precision=highest)]
    gather x16 -> x0, local copies, waits for them, and re-layouts: 45.5 us -> none  [the longest x3 12.1 us: local(): w_up = jnp.take(up_weight[0], weight_index, axis=0)]
    ppermute x21 -> x56, waiting for transfers between devices: 129 us -> 167 us  [send(): return lax.ppermute(value, AXES, route)]
    select_n x15 -> x4, other arithmetic: 30.6 us -> 1.94 us  [local(): jnp.where(middle, mine + from_mid.astype(F32), from_near.astype(F32) + fr...]
    another operation x4 -> x0, loops' own time: 21.1 us -> none  [local(): lax.cond(running, do_work, skip_work, (g_stack, pre_now))]
  transfers between devices with their start and end apart: 23 -> 56, of which waited for: 13 -> 15; matrix products, arithmetic and copies ran while one was open for 19% -> 8% of each run, Pallas kernels for 0% -> 19%
where the time goes in v1:
time: 411 us; the launch traced here: 405 us
  waiting for transfers between devices  167 us (41%)
  starting transfers between devices  112 us (27%)
  Pallas kernels  84.9 us (21%)
  local copies, waits for them, and re-layouts  25.7 us (6%)
  other arithmetic  13.8 us (3%)
    ppermute x56, waiting for transfers between devices, send(): return lax.ppermute(value, AXES, route)  167 us
    ppermute x56, starting transfers between devices, send(): return lax.ppermute(value, AXES, route)  112 us
    pallas_call x4, Pallas kernels, chain(): pl.pallas_call(functools.partial(chain_body, factors, chunks, per_step, b...  36.4 us
    pallas_call x4, Pallas kernels, up_products(): pl.pallas_call(functools.partial(up_body, factors, count, hgroup, blk, ch...  22.2 us
    pallas_call x2, Pallas kernels, down_products(): pl.pallas_call(functools.partial(down_body, factors, per_step, hgroup, bl...  19.2 us
  transfers between devices with their start and end apart: 56, of which 15 were waited for; matrix products, arithmetic and copies ran while one was open for 8% of the time, Pallas kernels for 19%

profile of v1, /device:TPU:0, one launch (start us, length us, event | category | flops | bytes accessed | tf_op | source)
XLA Modules:
  0.0 404.9 jit_solution(13005692260895595396)
XLA Ops:
  0.6 2.4 slice_bitcast_fusion.6
  3.1 1.5 collective-permute-start.7
  4.5 1.5 collective-permute-start.8
  6.0 1.5 collective-permute-start
  7.5 1.5 collective-permute-start.1
  9.0 2.3 copy.26
  12.0 2.7 bitcast_convert_fusion
  14.8 5.7 %copy.27 = f32[256,4096]{0,1:T(8,128)} copy(f32[256,4096]{1,0:T(8,128)} %bitcast_convert_fusion) | data formatting | bytes 8388608 | tf_op jit(solution)/shard_map/convert_element_type | solution.py:360
  21.3 8.9 %collective-permute-start.20 = (bf16[2048,256]{1,0:T(8,128)(2,1)}, bf16[2048,256]{1,0:T(8,128)(2,1)S(1)}, u32[]{:S(2)}, u32[]{:S(2)}) collective-permute-start(bf16[2048,256]{1,0:T(8,128)(2,1)} %bitcast.11.refs_0_), channel_id=1, source_target_pairs={{0,1},{3,2},{4,5},{7,6},{8,9},{11,10},{12,13},{15,14},{16,17},{19,... | collective-permute-start | bytes 3145736 | tf_op jit(solution)/shard_map/ppermute | solution.py:30
  30.2 1.6 broadcast_in_dim.23.refs_10_
  31.8 1.4 broadcast_in_dim.24.refs_11_
  33.2 6.5 %chain.4 = (bf16[4,256,1024]{2,1,0:T(8,128)(2,1)}, bf16[3,256,1024]{2,1,0:T(8,128)(2,1)}, bf16[256,1024]{1,0:T(8,128)(2,1)S(1)}, f32[128,2048]{1,0:T(8,128)}, bf...) custom-call(s32[5]{0:T(128)S(1)} %get-tuple-element.103.info, ...), custom_call_target="tpu_custom_call", output_to_operand_aliasing={{0}: (13, {}), {1}: (14, {}), {2}: (15, {})} | custom-call | flops 1610612736 | bytes 12582912 | tf_op jit(solution)/shard_map/chain/pallas_call | solution.py:155
  39.7 6.8 %chain.5 = (bf16[4,256,1024]{2,1,0:T(8,128)(2,1)}, bf16[3,256,1024]{2,1,0:T(8,128)(2,1)}, bf16[256,1024]{1,0:T(8,128)(2,1)S(1)}, f32[128,2048]{1,0:T(8,128)}, bf...) custom-call(s32[5]{0:T(128)S(1)} %get-tuple-element.103.info, ...), custom_call_target="tpu_custom_call", output_to_operand_aliasing={{0}: (13, {}), {1}: (14, {}), {2}: (15, {})} | custom-call | flops 1610612736 | bytes 12582912 | tf_op jit(solution)/shard_map/chain/pallas_call | solution.py:155
  52.1 2.3 collective-permute-start.39
  55.1 4.0 collective-permute-start.51
  62.2 54.5 %collective-permute-done.13.refs_0_ = bf16[128,2048]{1,0:T(8,128)(2,1)S(1)} collective-permute-done((bf16[128,2048]{1,0:T(8,128)(2,1)S(1)}, bf16[128,2048]{1,0:T(8,128)(2,1)S(1)}, u32[]{:S(2)}, u32[]{:S(2)}) %collective-permute-start.13) | collective-permute-done | bytes 524320 | tf_op jit(solution)/shard_map/ppermute | solution.py:30
  116.7 1.9 collective-permute-start.14
  118.6 3.4 collective-permute-start.15
  122.0 2.1 collective-permute-done.4.refs_0_
  124.1 1.9 collective-permute-start.5
  126.0 3.4 collective-permute-start.6
  129.4 1.7 collective-permute-start.52
  131.8 3.4 collective-permute-done.15.refs_2_
  136.0 1.6 collective-permute-start.41
  137.6 8.5 %collective-permute-done.6.refs_2_ = bf16[128,2048]{1,0:T(8,128)(2,1)S(1)} collective-permute-done((bf16[128,2048]{1,0:T(8,128)(2,1)S(1)}, bf16[128,2048]{1,0:T(8,128)(2,1)S(1)}, u32[]{:S(2)}, u32[]{:S(2)}) %collective-permute-start.6) | collective-permute-done | bytes 524320 | tf_op jit(solution)/shard_map/ppermute | solution.py:30
  146.0 1.7 collective-permute-start.53
  147.8 11.6 %chain.6 = (bf16[4,256,1024]{2,1,0:T(8,128)(2,1)}, bf16[3,256,1024]{2,1,0:T(8,128)(2,1)}, bf16[256,1024]{1,0:T(8,128)(2,1)S(1)}, f32[128,2048]{1,0:T(8,128)}, bf...) custom-call(s32[5]{0:T(128)S(1)} %get-tuple-element.102.info, ...), custom_call_target="tpu_custom_call", output_to_operand_aliasing={{0}: (13, {}), {1}: (14, {}), {2}: (15, {})} | custom-call | flops 1610612736 | bytes 12582912 | tf_op jit(solution)/shard_map/chain/pallas_call | solution.py:155
  159.4 11.6 %chain.7 = (bf16[4,256,1024]{2,1,0:T(8,128)(2,1)}, bf16[3,256,1024]{2,1,0:T(8,128)(2,1)}, bf16[256,1024]{1,0:T(8,128)(2,1)S(1)}, f32[128,2048]{1,0:T(8,128)}, bf...) custom-call(s32[5]{0:T(128)S(1)} %get-tuple-element.102.info, ...), custom_call_target="tpu_custom_call", output_to_operand_aliasing={{0}: (13, {}), {1}: (14, {}), {2}: (15, {})} | custom-call | flops 1610612736 | bytes 12582912 | tf_op jit(solution)/shard_map/chain/pallas_call | solution.py:155
  171.0 3.4 collective-permute-start.17
  174.4 2.7 slice_bitcast_fusion.4
  177.1 1.9 collective-permute-start.16
  179.1 2.5 collective-permute-start.10
  181.6 2.1 collective-permute-start.9
  183.7 18.8 %collective-permute-start.35 = (bf16[256,1024]{1,0:T(8,128)(2,1)S(1)}, bf16[256,1024]{1,0:T(8,128)(2,1)S(1)}, u32[]{:S(2)}, u32[]{:S(2)}) collective-permute-start(bf16[256,1024]{1,0:T(8,128)(2,1)S(1)} %get-tuple-element.97), channel_id=1, source_target_pairs={{0,1},{3,2},{4,5},{7,6},{8,9},{11,10},{12,13},{15,14},{16,17},{19,... | collective-permute-start | bytes 1572872 | tf_op jit(solution)/shard_map/ppermute | solution.py:30
  202.5 1.3 collective-permute-start.31
  203.9 1.9 slice_bitcast_fusion
  205.7 1.5 collective-permute-start.45
  207.2 3.9 collective-permute-start.48
  212.5 2.4 collective-permute-done.35.refs_7_
  214.8 4.4 %collective-permute-start.23 = (bf16[256,1024]{1,0:T(8,128)(2,1)}, bf16[256,1024]{1,0:T(8,128)(2,1)S(1)}, u32[]{:S(2)}, u32[]{:S(2)}) collective-permute-start(bf16[256,1024]{1,0:T(8,128)(2,1)} %get-tuple-element.96), channel_id=1, source_target_pairs={{0,1},{3,2},{4,5},{7,6},{8,9},{11,10},{12,13},{15,14},{16,17},{19,... | collective-permute-start | bytes 1572872 | tf_op jit(solution)/shard_map/ppermute | solution.py:30
  219.3 6.8 %collective-permute-done.31.refs_7_ = bf16[256,1024]{1,0:T(8,128)(2,1)S(1)} collective-permute-done((bf16[256,1024]{1,0:T(8,128)(2,1)S(1)}, bf16[256,1024]{1,0:T(8,128)(2,1)S(1)}, u32[]{:S(2)}, u32[]{:S(2)}) %collective-permute-start.31) | collective-permute-done | bytes 524320 | tf_op jit(solution)/shard_map/ppermute | solution.py:30
  226.1 4.4 %collective-permute-start.42 = (bf16[256,1024]{1,0:T(8,128)(2,1)}, bf16[256,1024]{1,0:T(8,128)(2,1)S(1)}, u32[]{:S(2)}, u32[]{:S(2)}) collective-permute-start(bf16[256,1024]{1,0:T(8,128)(2,1)} %slice_bitcast_fusion), channel_id=1, source_target_pairs={{0,1},{3,2},{4,5},{7,6},{8,9},{11,10},{12,13},{15,14},{16,17},{19,... | collective-permute-start | bytes 1572872 | tf_op jit(solution)/shard_map/ppermute | solution.py:30
  230.5 2.6 fusion.7
  233.2 5.5 %up_products.7 = (f32[3,4,64,256]{3,2,1,0:T(8,128)}, bf16[3,4,64,256]{3,2,1,0:T(8,128)(2,1)S(1)}, bf16[3,4,64,256]{3,2,1,0:T(8,128)(2,1)S(1)}, bf16[3,4,64,256]{3,2,1,0:T(8,128)(2,1)S(1)}) custom-call(s32[4]{0:T(128)S(1)} %pad_add_fusion.info, s32[48]{0:T(128)S(1)} %reshape.23.pick_up, bf16[2048,256]{1,0:T(8,128)(2,1)} %bitcast.11.refs_0_, ...), custom_call_target="tpu_custom_call" | custom-call | flops 805306368 | bytes 6291456 | tf_op jit(solution)/shard_map/up_products/pallas_call | solution.py:224
  238.7 5.8 %up_products.6 = (f32[3,4,64,256]{3,2,1,0:T(8,128)}, bf16[3,4,64,256]{3,2,1,0:T(8,128)(2,1)S(1)}, bf16[3,4,64,256]{3,2,1,0:T(8,128)(2,1)S(1)}, bf16[3,4,64,256]{3,2,1,0:T(8,128)(2,1)S(1)}) custom-call(s32[4]{0:T(128)S(1)} %pad_add_fusion.info, s32[48]{0:T(128)S(1)} %reshape.23.pick_up, bf16[2048,256]{1,0:T(8,128)(2,1)} %bitcast.11.refs_0_, ...), custom_call_target="tpu_custom_call" | custom-call | flops 805306368 | bytes 6291456 | tf_op jit(solution)/shard_map/up_products/pallas_call | solution.py:224
  244.5 4.2 %collective-permute-done.27.refs_7_ = bf16[256,1024]{1,0:T(8,128)(2,1)S(1)} collective-permute-done((bf16[256,1024]{1,0:T(8,128)(2,1)}, bf16[256,1024]{1,0:T(8,128)(2,1)S(1)}, u32[]{:S(2)}, u32[]{:S(2)}) %collective-permute-start.27) | collective-permute-done | bytes 524320 | tf_op jit(solution)/shard_map/ppermute | solution.py:30
  249.9 9.9 %collective-permute-done.23.refs_7_ = bf16[256,1024]{1,0:T(8,128)(2,1)S(1)} collective-permute-done((bf16[256,1024]{1,0:T(8,128)(2,1)}, bf16[256,1024]{1,0:T(8,128)(2,1)S(1)}, u32[]{:S(2)}, u32[]{:S(2)}) %collective-permute-start.23) | collective-permute-done | bytes 524320 | tf_op jit(solution)/shard_map/ppermute | solution.py:30
  261.2 8.3 %collective-permute-done.42.refs_5_ = bf16[256,1024]{1,0:T(8,128)(2,1)S(1)} collective-permute-done((bf16[256,1024]{1,0:T(8,128)(2,1)}, bf16[256,1024]{1,0:T(8,128)(2,1)S(1)}, u32[]{:S(2)}, u32[]{:S(2)}) %collective-permute-start.42) | collective-permute-done | bytes 524320 | tf_op jit(solution)/shard_map/ppermute | solution.py:30
  274.8 16.3 %collective-permute-done.34 = bf16[3,4,64,256]{3,2,1,0:T(8,128)(2,1)S(1)} collective-permute-done((bf16[3,4,64,256]{3,2,1,0:T(8,128)(2,1)S(1)}, bf16[3,4,64,256]{3,2,1,0:T(8,128)(2,1)S(1)}, u32[]{:S(2)}, u32[]{:S(2)}) %collective-permute-start.34) | collective-permute-done | bytes 393248 | tf_op jit(solution)/shard_map/ppermute | solution.py:30
  292.7 1.5 fusion.9
  294.3 5.5 %up_products.5 = (f32[3,4,64,256]{3,2,1,0:T(8,128)}, bf16[3,4,64,256]{3,2,1,0:T(8,128)(2,1)S(1)}, bf16[3,4,64,256]{3,2,1,0:T(8,128)(2,1)S(1)}, bf16[3,4,64,256]{3,2,1,0:T(8,128)(2,1)S(1)}) custom-call(s32[4]{0:T(128)S(1)} %pad_add_fusion.info, s32[48]{0:T(128)S(1)} %reshape.23.pick_up, bf16[2048,256]{1,0:T(8,128)(2,1)} %bitcast.11.refs_0_, ...), custom_call_target="tpu_custom_call" | custom-call | flops 805306368 | bytes 6291456 | tf_op jit(solution)/shard_map/up_products/pallas_call | solution.py:224
  299.7 5.5 %up_products.4 = (f32[3,4,64,256]{3,2,1,0:T(8,128)}, bf16[3,4,64,256]{3,2,1,0:T(8,128)(2,1)S(1)}, bf16[3,4,64,256]{3,2,1,0:T(8,128)(2,1)S(1)}, bf16[3,4,64,256]{3,2,1,0:T(8,128)(2,1)S(1)}) custom-call(s32[4]{0:T(128)S(1)} %pad_add_fusion.info, s32[48]{0:T(128)S(1)} %reshape.23.pick_up, bf16[2048,256]{1,0:T(8,128)(2,1)} %bitcast.11.refs_0_, ...), custom_call_target="tpu_custom_call" | custom-call | flops 805306368 | bytes 6291456 | tf_op jit(solution)/shard_map/up_products/pallas_call | solution.py:224
  310.9 1.4 collective-permute-start.28
  312.6 9.6 %down_products.2 = (f32[3,8,128,128]{3,2,1,0:T(8,128)}, bf16[3,8,128,128]{3,2,1,0:T(8,128)(2,1)}) custom-call(s32[4]{0:T(128)S(1)} %pad_add_fusion.info, s32[48]{0:T(128)S(1)} %reshape.24.pick_down, bf16[2,2048,256]{2,1,0:T(8,128)(2,1)} %bitcast.37, bf16[2048,256]{1,0:T(8,128)(2,1)} %collective-permute-done.39.refs_1_, bf16[2048,256]{1,0:T(8,128)(2,1)} %copy-done.15, ...), custom_call_target="tpu_custom_call" | custom-call | flops 1610612736 | bytes 10485760 | tf_op jit(solution)/shard_map/down_products/pallas_call | solution.py:282
  322.2 9.6 %down_products.3 = (f32[3,8,128,128]{3,2,1,0:T(8,128)}, bf16[3,8,128,128]{3,2,1,0:T(8,128)(2,1)}) custom-call(s32[4]{0:T(128)S(1)} %pad_add_fusion.info, s32[48]{0:T(128)S(1)} %reshape.24.pick_down, bf16[2,2048,256]{2,1,0:T(8,128)(2,1)} %bitcast.38, bf16[2048,256]{1,0:T(8,128)(2,1)} %collective-permute-done.51.refs_1_, ...), custom_call_target="tpu_custom_call" | custom-call | flops 1610612736 | bytes 10485760 | tf_op jit(solution)/shard_map/down_products/pallas_call | solution.py:282
  331.9 1.4 collective-permute-start.26
  338.3 1.3 add_select_fusion.2
  339.6 11.2 %collective-permute-done.26 = bf16[3,4,64,256]{3,2,1,0:T(8,128)(2,1)S(1)} collective-permute-done((bf16[3,4,64,256]{3,2,1,0:T(8,128)(2,1)S(1)}, bf16[3,4,64,256]{3,2,1,0:T(8,128)(2,1)S(1)}, u32[]{:S(2)}, u32[]{:S(2)}) %collective-permute-start.26) | collective-permute-done | bytes 393248 | tf_op jit(solution)/shard_map/ppermute | solution.py:30
  350.9 7.2 %collective-permute-done.25 = bf16[3,4,64,256]{3,2,1,0:T(8,128)(2,1)S(1)} collective-permute-done((bf16[3,4,64,256]{3,2,1,0:T(8,128)(2,1)S(1)}, bf16[3,4,64,256]{3,2,1,0:T(8,128)(2,1)S(1)}, u32[]{:S(2)}, u32[]{:S(2)}) %collective-permute-start.25) | collective-permute-done | bytes 393248 | tf_op jit(solution)/shard_map/ppermute | solution.py:30
  358.3 1.9 maximum_bitcast_fusion
  360.1 14.8 %collective-permute-done.54.refs_2_ = bf16[3,8,128,128]{3,2,1,0:T(8,128)(2,1)S(1)} collective-permute-done((bf16[3,8,128,128]{3,2,1,0:T(8,128)(2,1)S(1)}, bf16[3,8,128,128]{3,2,1,0:T(8,128)(2,1)S(1)}, u32[]{:S(2)}, u32[]{:S(2)}) %collective-permute-start.54) | collective-permute-done | bytes 786464 | tf_op jit(solution)/shard_map/ppermute | solution.py:30
  374.9 16.8 %collective-permute-done.55.refs_3_ = bf16[3,8,128,128]{3,2,1,0:T(8,128)(2,1)S(1)} collective-permute-done((bf16[3,8,128,128]{3,2,1,0:T(8,128)(2,1)}, bf16[3,8,128,128]{3,2,1,0:T(8,128)(2,1)S(1)}, u32[]{:S(2)}, u32[]{:S(2)}) %collective-permute-start.55) | collective-permute-done | bytes 786464 | tf_op jit(solution)/shard_map/ppermute | solution.py:30
  391.7 7.1 %down_finish.1 = f32[1,3,16,256,64]{4,3,2,1,0:T(8,128)} custom-call(s32[1]{0:T(128)} %bitcast.17.info, f32[3,8,128,128]{3,2,1,0:T(8,128)} %get-tuple-element.87.refs_0_, f32[3,8,128,128]{3,2,1,0:T(8,128)} %get-tuple-element.88.refs_1_, bf16[3,8,128,128]{3,2,1,0:T(8,128)(2,1)S(1)} %collective-permute-done.54.refs_2_, ...), custom_call_target="tpu_custom_call" | custom-call | tf_op jit(solution)/shard_map/down_finish/pallas_call | solution.py:323
  398.8 6.1 %copy.25 = f32[1,3,16,256,64]{3,4,2,1,0:T(8,128)} copy(f32[1,3,16,256,64]{4,3,2,1,0:T(8,128)} %down_finish.1) | data formatting | bytes 6291456
  (172 shorter events, 34.3 us)
Async XLA Ops:
  3.1 36.6 %collective-permute-start.7 = (bf16[128,2048]{1,0:T(8,128)(2,1)}, bf16[128,2048]{1,0:T(8,128)(2,1)}, u32[]{:S(2)}, u32[]{:S(2)}) collective-permute-start(bf16[128,2048]{1,0:T(8,128)(2,1)} %get-tuple-element.101.refs_0_), channel_id=1, source_target_pairs={{16,20},{17,21},{18,22},{19,23},{20,16},{21,17},{22,18},{23,19},{2... | collective-permute-start | bytes 1572872 | tf_op jit(solution)/shard_map/ppermute | solution.py:30
  4.5 35.2 %collective-permute-start.8 = (bf16[128,2048]{1,0:T(8,128)(2,1)}, bf16[128,2048]{1,0:T(8,128)(2,1)}, u32[]{:S(2)}, u32[]{:S(2)}) collective-permute-start(bf16[128,2048]{1,0:T(8,128)(2,1)} %get-tuple-element.101.refs_0_), channel_id=1, source_target_pairs={{16,24},{17,25},{18,26},{19,27},{20,28},{21,29},{22,30},{23,31},{2... | collective-permute-start | bytes 1572872 | tf_op jit(solution)/shard_map/ppermute | solution.py:30
  6.0 14.6 %collective-permute-start = (bf16[128,2048]{1,0:T(8,128)(2,1)}, bf16[128,2048]{1,0:T(8,128)(2,1)}, u32[]{:S(2)}, u32[]{:S(2)}) collective-permute-start(bf16[128,2048]{1,0:T(8,128)(2,1)} %get-tuple-element.100.refs_0_), channel_id=1, source_target_pairs={{16,20},{17,21},{18,22},{19,23},{20,16},{21,17},{22,18},{23,19},{2... | collective-permute-start | bytes 1572872 | tf_op jit(solution)/shard_map/ppermute | solution.py:30
  7.5 13.8 %collective-permute-start.1 = (bf16[128,2048]{1,0:T(8,128)(2,1)}, bf16[128,2048]{1,0:T(8,128)(2,1)}, u32[]{:S(2)}, u32[]{:S(2)}) collective-permute-start(bf16[128,2048]{1,0:T(8,128)(2,1)} %get-tuple-element.100.refs_0_), channel_id=1, source_target_pairs={{16,24},{17,25},{18,26},{19,27},{20,28},{21,29},{22,30},{23,31},{2... | collective-permute-start | bytes 1572872 | tf_op jit(solution)/shard_map/ppermute | solution.py:30
  11.2 43.9 %collective-permute-start.18 = (bf16[2048,256]{1,0:T(8,128)(2,1)}, bf16[2048,256]{1,0:T(8,128)(2,1)S(1)}, u32[]{:S(2)}, u32[]{:S(2)}) collective-permute-start(bf16[2048,256]{1,0:T(8,128)(2,1)} %bitcast.11.refs_0_), channel_id=1, source_target_pairs={{1,5},{2,6},{5,1},{6,2},{9,13},{10,14},{13,9},{14,10},{17,21},{18,... | collective-permute-start | bytes 3145736 | tf_op jit(solution)/shard_map/ppermute | solution.py:30
  20.6 38.7 %collective-permute-start.19 = (bf16[2048,256]{1,0:T(8,128)(2,1)}, bf16[2048,256]{1,0:T(8,128)(2,1)S(1)}, u32[]{:S(2)}, u32[]{:S(2)}) collective-permute-start(bf16[2048,256]{1,0:T(8,128)(2,1)} %bitcast.11.refs_0_), channel_id=1, source_target_pairs={{1,9},{2,10},{5,13},{6,14},{9,1},{10,2},{13,5},{14,6},{17,25},{18,... | collective-permute-start | bytes 3145736 | tf_op jit(solution)/shard_map/ppermute | solution.py:30
  21.3 39.5 %collective-permute-start.20 = (bf16[2048,256]{1,0:T(8,128)(2,1)}, bf16[2048,256]{1,0:T(8,128)(2,1)S(1)}, u32[]{:S(2)}, u32[]{:S(2)}) collective-permute-start(bf16[2048,256]{1,0:T(8,128)(2,1)} %bitcast.11.refs_0_), channel_id=1, source_target_pairs={{0,1},{3,2},{4,5},{7,6},{8,9},{11,10},{12,13},{15,14},{16,17},{19,... | collective-permute-start | bytes 3145736 | tf_op jit(solution)/shard_map/ppermute | solution.py:30
  46.5 2.9 collective-permute-start.12
  47.2 3.0 collective-permute-start.11
  49.4 2.7 collective-permute-start.3
  50.2 4.1 %collective-permute-start.2 = (bf16[128,2048]{1,0:T(8,128)(2,1)S(1)}, bf16[128,2048]{1,0:T(8,128)(2,1)S(1)}, u32[]{:S(2)}, u32[]{:S(2)}) collective-permute-start(bf16[128,2048]{1,0:T(8,128)(2,1)S(1)} %get-tuple-element.48), channel_id=1, source_target_pairs={{16,20},{17,21},{18,22},{19,23},{20,16},{21,17},{22,18},{23,19},{2... | collective-permute-start | bytes 1572872 | tf_op jit(solution)/shard_map/ppermute | solution.py:30
  52.1 66.5 %collective-permute-start.39 = (bf16[2048,256]{1,0:T(8,128)(2,1)S(1)}, bf16[2048,256]{1,0:T(8,128)(2,1)}, u32[]{:S(2)}, u32[]{:S(2)}) collective-permute-start(bf16[2048,256]{1,0:T(8,128)(2,1)S(1)} %get-tuple-element.95), channel_id=1, source_target_pairs={{0,1},{3,2},{4,5},{7,6},{8,9},{11,10},{12,13},{15,14},{16,17},{19,... | collective-permute-start | bytes 3145736 | tf_op jit(solution)/shard_map/ppermute | solution.py:30
  54.4 71.6 %collective-permute-start.40 = (bf16[2048,256]{1,0:T(8,128)(2,1)S(1)}, bf16[2048,256]{1,0:T(8,128)(2,1)S(1)}, u32[]{:S(2)}, u32[]{:S(2)}) collective-permute-start(bf16[2048,256]{1,0:T(8,128)(2,1)S(1)} %get-tuple-element.95), channel_id=1, source_target_pairs={{1,2},{2,1},{5,6},{6,5},{9,10},{10,9},{13,14},{14,13},{17,18},{18,... | collective-permute-start | bytes 3145736 | tf_op jit(solution)/shard_map/ppermute | solution.py:30
  55.1 104.3 %copy-start.2 = (bf16[2048,256]{1,0:T(8,128)(2,1)}, bf16[2048,256]{1,0:T(8,128)(2,1)S(1)}, u32[]{:S(2)}) copy-start(bf16[2048,256]{1,0:T(8,128)(2,1)S(1)} %collective-permute-done.18.refs_1_) | copy-start | bytes 3145732
  55.1 74.3 %collective-permute-start.51 = (bf16[2048,256]{1,0:T(8,128)(2,1)}, bf16[2048,256]{1,0:T(8,128)(2,1)}, u32[]{:S(2)}, u32[]{:S(2)}) collective-permute-start(bf16[2048,256]{1,0:T(8,128)(2,1)} %get-tuple-element.94), channel_id=1, source_target_pairs={{0,1},{3,2},{4,5},{7,6},{8,9},{11,10},{12,13},{15,14},{16,17},{19,... | collective-permute-start | bytes 3145736 | tf_op jit(solution)/shard_map/ppermute | solution.py:30
  59.3 72.5 %copy-start.13 = (bf16[128,2048]{1,0:T(8,128)(2,1)}, bf16[128,2048]{1,0:T(8,128)(2,1)S(1)}, u32[]{:S(2)}) copy-start(bf16[128,2048]{1,0:T(8,128)(2,1)S(1)} %add_convert_fusion.1) | copy-start | bytes 1572868
  59.3 100.1 %copy-start.3 = (bf16[2048,256]{1,0:T(8,128)(2,1)}, bf16[2048,256]{1,0:T(8,128)(2,1)S(1)}, u32[]{:S(2)}) copy-start(bf16[2048,256]{1,0:T(8,128)(2,1)S(1)} %collective-permute-done.19.refs_2_) | copy-start | bytes 3145732
  59.3 57.3 %collective-permute-start.13 = (bf16[128,2048]{1,0:T(8,128)(2,1)S(1)}, bf16[128,2048]{1,0:T(8,128)(2,1)S(1)}, u32[]{:S(2)}, u32[]{:S(2)}) collective-permute-start(bf16[128,2048]{1,0:T(8,128)(2,1)S(1)} %add_convert_fusion.1), channel_id=1, source_target_pairs={{16,0},{17,1},{18,2},{19,3},{20,4},{21,5},{22,6},{23,7},{24,8},{25... | collective-permute-start | bytes 1572872 | tf_op jit(solution)/shard_map/ppermute | solution.py:30
  60.8 71.0 %copy-start.11 = (bf16[128,2048]{1,0:T(8,128)(2,1)}, bf16[128,2048]{1,0:T(8,128)(2,1)S(1)}, u32[]{:S(2)}) copy-start(bf16[128,2048]{1,0:T(8,128)(2,1)S(1)} %add_convert_fusion.3) | copy-start | bytes 1572868
  60.9 98.5 %copy-start.4 = (bf16[2048,256]{1,0:T(8,128)(2,1)}, bf16[2048,256]{1,0:T(8,128)(2,1)S(1)}, u32[]{:S(2)}) copy-start(bf16[2048,256]{1,0:T(8,128)(2,1)S(1)} %collective-permute-done.20.refs_3_) | copy-start | bytes 3145732
  60.9 63.2 %collective-permute-start.4 = (bf16[128,2048]{1,0:T(8,128)(2,1)S(1)}, bf16[128,2048]{1,0:T(8,128)(2,1)S(1)}, u32[]{:S(2)}, u32[]{:S(2)}) collective-permute-start(bf16[128,2048]{1,0:T(8,128)(2,1)S(1)} %add_convert_fusion.3), channel_id=1, source_target_pairs={{16,0},{17,1},{18,2},{19,3},{20,4},{21,5},{22,6},{23,7},{24,8},{25... | collective-permute-start | bytes 1572872 | tf_op jit(solution)/shard_map/ppermute | solution.py:30
  116.7 14.4 %collective-permute-start.14 = (bf16[128,2048]{1,0:T(8,128)(2,1)S(1)}, bf16[128,2048]{1,0:T(8,128)(2,1)S(1)}, u32[]{:S(2)}, u32[]{:S(2)}) collective-permute-start(bf16[128,2048]{1,0:T(8,128)(2,1)S(1)} %collective-permute-done.13.refs_0_), channel_id=1, source_target_pairs={{0,4},{1,5},{2,6},{3,7},{4,0},{5,1},{6,2},{7,3},{8,12},{9,13},{10,... | collective-permute-start | bytes 1572872 | tf_op jit(solution)/shard_map/ppermute | solution.py:30
  118.6 16.6 %collective-permute-start.15 = (bf16[128,2048]{1,0:T(8,128)(2,1)S(1)}, bf16[128,2048]{1,0:T(8,128)(2,1)S(1)}, u32[]{:S(2)}, u32[]{:S(2)}) collective-permute-start(bf16[128,2048]{1,0:T(8,128)(2,1)S(1)} %collective-permute-done.13.refs_0_), channel_id=1, source_target_pairs={{0,8},{1,9},{2,10},{3,11},{4,12},{5,13},{6,14},{7,15},{8,0},{9,1},... | collective-permute-start | bytes 1572872 | tf_op jit(solution)/shard_map/ppermute | solution.py:30
  124.1 11.9 %collective-permute-start.5 = (bf16[128,2048]{1,0:T(8,128)(2,1)S(1)}, bf16[128,2048]{1,0:T(8,128)(2,1)S(1)}, u32[]{:S(2)}, u32[]{:S(2)}) collective-permute-start(bf16[128,2048]{1,0:T(8,128)(2,1)S(1)} %collective-permute-done.4.refs_0_), channel_id=1, source_target_pairs={{0,4},{1,5},{2,6},{3,7},{4,0},{5,1},{6,2},{7,3},{8,12},{9,13},{10,... | collective-permute-start | bytes 1572872 | tf_op jit(solution)/shard_map/ppermute | solution.py:30
  126.0 20.1 %collective-permute-start.6 = (bf16[128,2048]{1,0:T(8,128)(2,1)S(1)}, bf16[128,2048]{1,0:T(8,128)(2,1)S(1)}, u32[]{:S(2)}, u32[]{:S(2)}) collective-permute-start(bf16[128,2048]{1,0:T(8,128)(2,1)S(1)} %collective-permute-done.4.refs_0_), channel_id=1, source_target_pairs={{0,8},{1,9},{2,10},{3,11},{4,12},{5,13},{6,14},{7,15},{8,0},{9,1},... | collective-permute-start | bytes 1572872 | tf_op jit(solution)/shard_map/ppermute | solution.py:30
  129.4 41.6 %collective-permute-start.52 = (bf16[2048,256]{1,0:T(8,128)(2,1)}, bf16[2048,256]{1,0:T(8,128)(2,1)}, u32[]{:S(2)}, u32[]{:S(2)}) collective-permute-start(bf16[2048,256]{1,0:T(8,128)(2,1)} %get-tuple-element.94), channel_id=1, source_target_pairs={{1,2},{2,1},{5,6},{6,5},{9,10},{10,9},{13,14},{14,13},{17,18},{18,... | collective-permute-start | bytes 3145736 | tf_op jit(solution)/shard_map/ppermute | solution.py:30
  131.1 46.0 %collective-permute-start.21 = (bf16[2048,256]{1,0:T(8,128)(2,1)S(1)}, bf16[2048,256]{1,0:T(8,128)(2,1)S(1)}, u32[]{:S(2)}, u32[]{:S(2)}) collective-permute-start(bf16[2048,256]{1,0:T(8,128)(2,1)S(1)} %collective-permute-done.20.refs_3_), channel_id=1, source_target_pairs={{1,5},{2,6},{5,1},{6,2},{9,13},{10,14},{13,9},{14,10},{17,21},{18,... | collective-permute-start | bytes 3145736 | tf_op jit(solution)/shard_map/ppermute | solution.py:30
  135.2 43.9 %collective-permute-start.22 = (bf16[2048,256]{1,0:T(8,128)(2,1)S(1)}, bf16[2048,256]{1,0:T(8,128)(2,1)S(1)}, u32[]{:S(2)}, u32[]{:S(2)}) collective-permute-start(bf16[2048,256]{1,0:T(8,128)(2,1)S(1)} %collective-permute-done.20.refs_3_), channel_id=1, source_target_pairs={{1,9},{2,10},{5,13},{6,14},{9,1},{10,2},{13,5},{14,6},{17,25},{18,... | collective-permute-start | bytes 3145736 | tf_op jit(solution)/shard_map/ppermute | solution.py:30
  136.0 45.6 %collective-permute-start.41 = (bf16[2048,256]{1,0:T(8,128)(2,1)}, bf16[2048,256]{1,0:T(8,128)(2,1)}, u32[]{:S(2)}, u32[]{:S(2)}) collective-permute-start(bf16[2048,256]{1,0:T(8,128)(2,1)} %collective-permute-done.39.refs_1_), channel_id=1, source_target_pairs={{1,2},{2,1},{5,6},{6,5},{9,10},{10,9},{13,14},{14,13},{17,18},{18,... | collective-permute-start | bytes 3145736 | tf_op jit(solution)/shard_map/ppermute | solution.py:30
  146.0 37.7 %collective-permute-start.53 = (bf16[2048,256]{1,0:T(8,128)(2,1)}, bf16[2048,256]{1,0:T(8,128)(2,1)}, u32[]{:S(2)}, u32[]{:S(2)}) collective-permute-start(bf16[2048,256]{1,0:T(8,128)(2,1)} %collective-permute-done.51.refs_1_), channel_id=1, source_target_pairs={{1,2},{2,1},{5,6},{6,5},{9,10},{10,9},{13,14},{14,13},{17,18},{18,... | collective-permute-start | bytes 3145736 | tf_op jit(solution)/shard_map/ppermute | solution.py:30
  171.0 31.5 %collective-permute-start.17 = (bf16[128,2048]{1,0:T(8,128)(2,1)S(1)}, bf16[128,2048]{1,0:T(8,128)(2,1)S(1)}, u32[]{:S(2)}, u32[]{:S(2)}) collective-permute-start(bf16[128,2048]{1,0:T(8,128)(2,1)S(1)} %get-tuple-element.67), channel_id=1, source_target_pairs={{0,8},{1,9},{2,10},{3,11},{4,12},{5,13},{6,14},{7,15},{8,0},{9,1},... | collective-permute-start | bytes 1572872 | tf_op jit(solution)/shard_map/ppermute | solution.py:30
  177.1 28.6 %collective-permute-start.16 = (bf16[128,2048]{1,0:T(8,128)(2,1)S(1)}, bf16[128,2048]{1,0:T(8,128)(2,1)S(1)}, u32[]{:S(2)}, u32[]{:S(2)}) collective-permute-start(bf16[128,2048]{1,0:T(8,128)(2,1)S(1)} %get-tuple-element.66), channel_id=1, source_target_pairs={{0,4},{1,5},{2,6},{3,7},{4,0},{5,1},{6,2},{7,3},{8,12},{9,13},{10,... | collective-permute-start | bytes 1572872 | tf_op jit(solution)/shard_map/ppermute | solution.py:30
  179.1 51.4 %copy-start.6 = (bf16[2048,256]{1,0:T(8,128)(2,1)}, bf16[2048,256]{1,0:T(8,128)(2,1)S(1)}, u32[]{:S(2)}) copy-start(bf16[2048,256]{1,0:T(8,128)(2,1)S(1)} %collective-permute-done.22.refs_5_) | copy-start | bytes 3145732
  179.1 28.1 %collective-permute-start.10 = (bf16[128,2048]{1,0:T(8,128)(2,1)S(1)}, bf16[128,2048]{1,0:T(8,128)(2,1)}, u32[]{:S(2)}, u32[]{:S(2)}) collective-permute-start(bf16[128,2048]{1,0:T(8,128)(2,1)S(1)} %get-tuple-element.58), channel_id=1, source_target_pairs={{0,8},{1,9},{2,10},{3,11},{4,12},{5,13},{6,14},{7,15},{8,0},{9,1},... | collective-permute-start | bytes 1572872 | tf_op jit(solution)/shard_map/ppermute | solution.py:30
  181.6 29.6 %collective-permute-start.9 = (bf16[128,2048]{1,0:T(8,128)(2,1)S(1)}, bf16[128,2048]{1,0:T(8,128)(2,1)}, u32[]{:S(2)}, u32[]{:S(2)}) collective-permute-start(bf16[128,2048]{1,0:T(8,128)(2,1)S(1)} %get-tuple-element.57), channel_id=1, source_target_pairs={{0,4},{1,5},{2,6},{3,7},{4,0},{5,1},{6,2},{7,3},{8,12},{9,13},{10,... | collective-permute-start | bytes 1572872 | tf_op jit(solution)/shard_map/ppermute | solution.py:30
  183.7 31.1 %collective-permute-start.35 = (bf16[256,1024]{1,0:T(8,128)(2,1)S(1)}, bf16[256,1024]{1,0:T(8,128)(2,1)S(1)}, u32[]{:S(2)}, u32[]{:S(2)}) collective-permute-start(bf16[256,1024]{1,0:T(8,128)(2,1)S(1)} %get-tuple-element.97), channel_id=1, source_target_pairs={{0,1},{3,2},{4,5},{7,6},{8,9},{11,10},{12,13},{15,14},{16,17},{19,... | collective-permute-start | bytes 1572872 | tf_op jit(solution)/shard_map/ppermute | solution.py:30
  202.5 23.5 %collective-permute-start.31 = (bf16[256,1024]{1,0:T(8,128)(2,1)S(1)}, bf16[256,1024]{1,0:T(8,128)(2,1)S(1)}, u32[]{:S(2)}, u32[]{:S(2)}) collective-permute-start(bf16[256,1024]{1,0:T(8,128)(2,1)S(1)} %get-tuple-element.98), channel_id=1, source_target_pairs={{0,1},{3,2},{4,5},{7,6},{8,9},{11,10},{12,13},{15,14},{16,17},{19,... | collective-permute-start | bytes 1572872 | tf_op jit(solution)/shard_map/ppermute | solution.py:30
  205.7 64.4 %collective-permute-start.45 = (bf16[256,1024]{1,0:T(8,128)(2,1)S(1)}, bf16[256,1024]{1,0:T(8,128)(2,1)}, u32[]{:S(2)}, u32[]{:S(2)}) collective-permute-start(bf16[256,1024]{1,0:T(8,128)(2,1)S(1)} %get-tuple-element.86), channel_id=1, source_target_pairs={{1,2},{2,1},{5,6},{6,5},{9,10},{10,9},{13,14},{14,13},{17,18},{18,... | collective-permute-start | bytes 1572872 | tf_op jit(solution)/shard_map/ppermute | solution.py:30
  207.2 64.3 %collective-permute-start.48 = (bf16[256,1024]{1,0:T(8,128)(2,1)S(1)}, bf16[256,1024]{1,0:T(8,128)(2,1)}, u32[]{:S(2)}, u32[]{:S(2)}) collective-permute-start(bf16[256,1024]{1,0:T(8,128)(2,1)S(1)} %get-tuple-element.86), channel_id=1, source_target_pairs={{0,2},{3,1},{4,6},{7,5},{8,10},{11,9},{12,14},{15,13},{16,18},{19,... | collective-permute-start | bytes 1572872 | tf_op jit(solution)/shard_map/ppermute | solution.py:30
  211.1 37.5 %collective-permute-start.27 = (bf16[256,1024]{1,0:T(8,128)(2,1)}, bf16[256,1024]{1,0:T(8,128)(2,1)S(1)}, u32[]{:S(2)}, u32[]{:S(2)}) collective-permute-start(bf16[256,1024]{1,0:T(8,128)(2,1)} %get-tuple-element.99), channel_id=1, source_target_pairs={{0,1},{3,2},{4,5},{7,6},{8,9},{11,10},{12,13},{15,14},{16,17},{19,... | collective-permute-start | bytes 1572872 | tf_op jit(solution)/shard_map/ppermute | solution.py:30
  214.8 45.0 %collective-permute-start.23 = (bf16[256,1024]{1,0:T(8,128)(2,1)}, bf16[256,1024]{1,0:T(8,128)(2,1)S(1)}, u32[]{:S(2)}, u32[]{:S(2)}) collective-permute-start(bf16[256,1024]{1,0:T(8,128)(2,1)} %get-tuple-element.96), channel_id=1, source_target_pairs={{0,1},{3,2},{4,5},{7,6},{8,9},{11,10},{12,13},{15,14},{16,17},{19,... | collective-permute-start | bytes 1572872 | tf_op jit(solution)/shard_map/ppermute | solution.py:30
  226.1 43.4 %collective-permute-start.42 = (bf16[256,1024]{1,0:T(8,128)(2,1)}, bf16[256,1024]{1,0:T(8,128)(2,1)S(1)}, u32[]{:S(2)}, u32[]{:S(2)}) collective-permute-start(bf16[256,1024]{1,0:T(8,128)(2,1)} %slice_bitcast_fusion), channel_id=1, source_target_pairs={{0,1},{3,2},{4,5},{7,6},{8,9},{11,10},{12,13},{15,14},{16,17},{19,... | collective-permute-start | bytes 1572872 | tf_op jit(solution)/shard_map/ppermute | solution.py:30
  238.7 54.0 %copy-start.12 = (bf16[128,2048]{1,0:T(8,128)(2,1)S(1)}, bf16[128,2048]{1,0:T(8,128)(2,1)}, u32[]{:S(2)}) copy-start(bf16[128,2048]{1,0:T(8,128)(2,1)} %copy-done.11) | copy-start | bytes 1572868
  238.7 54.0 %copy-start.16 = (f32[128,2048]{1,0:T(8,128)S(1)}, f32[128,2048]{1,0:T(8,128)}, u32[]{:S(2)}) copy-start(f32[128,2048]{1,0:T(8,128)} %get-tuple-element.56) | copy-start | bytes 3145732
  248.6 23.9 %collective-permute-start.38 = (bf16[3,4,64,256]{3,2,1,0:T(8,128)(2,1)S(1)}, bf16[3,4,64,256]{3,2,1,0:T(8,128)(2,1)S(1)}, u32[]{:S(2)}, u32[]{:S(2)}) collective-permute-start(bf16[3,4,64,256]{3,2,1,0:T(8,128)(2,1)S(1)} %get-tuple-element.84), channel_id=1, source_target_pairs={{1,3},{2,0},{5,7},{6,4},{9,11},{10,8},{13,15},{14,12},{17,19},{18,... | collective-permute-start | bytes 1179656 | tf_op jit(solution)/shard_map/ppermute | solution.py:30
  259.9 13.4 %collective-permute-start.37 = (bf16[3,4,64,256]{3,2,1,0:T(8,128)(2,1)S(1)}, bf16[3,4,64,256]{3,2,1,0:T(8,128)(2,1)S(1)}, u32[]{:S(2)}, u32[]{:S(2)}) collective-permute-start(bf16[3,4,64,256]{3,2,1,0:T(8,128)(2,1)S(1)} %get-tuple-element.83), channel_id=1, source_target_pairs={{1,0},{2,3},{5,4},{6,7},{9,8},{10,11},{13,12},{14,15},{17,16},{18,... | collective-permute-start | bytes 1179656 | tf_op jit(solution)/shard_map/ppermute | solution.py:30
  269.5 4.5 %collective-permute-start.36 = (bf16[3,4,64,256]{3,2,1,0:T(8,128)(2,1)S(1)}, bf16[3,4,64,256]{3,2,1,0:T(8,128)(2,1)S(1)}, u32[]{:S(2)}, u32[]{:S(2)}) collective-permute-start(bf16[3,4,64,256]{3,2,1,0:T(8,128)(2,1)S(1)} %get-tuple-element.82), channel_id=1, source_target_pairs={{1,2},{2,1},{5,6},{6,5},{9,10},{10,9},{13,14},{14,13},{17,18},{18,... | collective-permute-start | bytes 1179656 | tf_op jit(solution)/shard_map/ppermute | solution.py:30
  270.2 20.9 %collective-permute-start.34 = (bf16[3,4,64,256]{3,2,1,0:T(8,128)(2,1)S(1)}, bf16[3,4,64,256]{3,2,1,0:T(8,128)(2,1)S(1)}, u32[]{:S(2)}, u32[]{:S(2)}) collective-permute-start(bf16[3,4,64,256]{3,2,1,0:T(8,128)(2,1)S(1)} %get-tuple-element.80), channel_id=1, source_target_pairs={{1,3},{2,0},{5,7},{6,4},{9,11},{10,8},{13,15},{14,12},{17,19},{18,... | collective-permute-start | bytes 1179656 | tf_op jit(solution)/shard_map/ppermute | solution.py:30
  271.5 20.3 %collective-permute-start.43 = (bf16[256,1024]{1,0:T(8,128)(2,1)S(1)}, bf16[256,1024]{1,0:T(8,128)(2,1)S(1)}, u32[]{:S(2)}, u32[]{:S(2)}) collective-permute-start(bf16[256,1024]{1,0:T(8,128)(2,1)S(1)} %collective-permute-done.42.refs_5_), channel_id=1, source_target_pairs={{1,5},{2,6},{5,1},{6,2},{9,13},{10,14},{13,9},{14,10},{17,21},{18,... | collective-permute-start | bytes 1572872 | tf_op jit(solution)/shard_map/ppermute | solution.py:30
  272.5 33.7 %collective-permute-start.44 = (bf16[256,1024]{1,0:T(8,128)(2,1)S(1)}, bf16[256,1024]{1,0:T(8,128)(2,1)S(1)}, u32[]{:S(2)}, u32[]{:S(2)}) collective-permute-start(bf16[256,1024]{1,0:T(8,128)(2,1)S(1)} %collective-permute-done.42.refs_5_), channel_id=1, source_target_pairs={{1,9},{2,10},{5,13},{6,14},{9,1},{10,2},{13,5},{14,6},{17,25},{18,... | collective-permute-start | bytes 1572872 | tf_op jit(solution)/shard_map/ppermute | solution.py:30
  273.3 34.3 %collective-permute-start.46 = (bf16[256,1024]{1,0:T(8,128)(2,1)}, bf16[256,1024]{1,0:T(8,128)(2,1)S(1)}, u32[]{:S(2)}, u32[]{:S(2)}) collective-permute-start(bf16[256,1024]{1,0:T(8,128)(2,1)} %collective-permute-done.45.refs_8_), channel_id=1, source_target_pairs={{1,5},{2,6},{5,1},{6,2},{9,13},{10,14},{13,9},{14,10},{17,21},{18,... | collective-permute-start | bytes 1572872 | tf_op jit(solution)/shard_map/ppermute | solution.py:30
  274.0 34.3 %collective-permute-start.47 = (bf16[256,1024]{1,0:T(8,128)(2,1)}, bf16[256,1024]{1,0:T(8,128)(2,1)S(1)}, u32[]{:S(2)}, u32[]{:S(2)}) collective-permute-start(bf16[256,1024]{1,0:T(8,128)(2,1)} %collective-permute-done.45.refs_8_), channel_id=1, source_target_pairs={{1,9},{2,10},{5,13},{6,14},{9,1},{10,2},{13,5},{14,6},{17,25},{18,... | collective-permute-start | bytes 1572872 | tf_op jit(solution)/shard_map/ppermute | solution.py:30
  291.1 18.5 %collective-permute-start.49 = (bf16[256,1024]{1,0:T(8,128)(2,1)}, bf16[256,1024]{1,0:T(8,128)(2,1)S(1)}, u32[]{:S(2)}, u32[]{:S(2)}) collective-permute-start(bf16[256,1024]{1,0:T(8,128)(2,1)} %collective-permute-done.48.refs_11_), channel_id=1, source_target_pairs={{1,5},{2,6},{5,1},{6,2},{9,13},{10,14},{13,9},{14,10},{17,21},{18,... | collective-permute-start | bytes 1572872 | tf_op jit(solution)/shard_map/ppermute | solution.py:30
  291.8 19.1 %collective-permute-start.50 = (bf16[256,1024]{1,0:T(8,128)(2,1)}, bf16[256,1024]{1,0:T(8,128)(2,1)S(1)}, u32[]{:S(2)}, u32[]{:S(2)}) collective-permute-start(bf16[256,1024]{1,0:T(8,128)(2,1)} %collective-permute-done.48.refs_11_), channel_id=1, source_target_pairs={{1,9},{2,10},{5,13},{6,14},{9,1},{10,2},{13,5},{14,6},{17,25},{18,... | collective-permute-start | bytes 1572872 | tf_op jit(solution)/shard_map/ppermute | solution.py:30
  306.3 25.6 %collective-permute-start.33 = (bf16[3,4,64,256]{3,2,1,0:T(8,128)(2,1)S(1)}, bf16[3,4,64,256]{3,2,1,0:T(8,128)(2,1)S(1)}, u32[]{:S(2)}, u32[]{:S(2)}) collective-permute-start(bf16[3,4,64,256]{3,2,1,0:T(8,128)(2,1)S(1)} %get-tuple-element.79), channel_id=1, source_target_pairs={{1,0},{2,3},{5,4},{6,7},{9,8},{10,11},{13,12},{14,15},{17,16},{18,... | collective-permute-start | bytes 1179656 | tf_op jit(solution)/shard_map/ppermute | solution.py:30
  307.6 25.7 %collective-permute-start.32 = (bf16[3,4,64,256]{3,2,1,0:T(8,128)(2,1)S(1)}, bf16[3,4,64,256]{3,2,1,0:T(8,128)(2,1)S(1)}, u32[]{:S(2)}, u32[]{:S(2)}) collective-permute-start(bf16[3,4,64,256]{3,2,1,0:T(8,128)(2,1)S(1)} %get-tuple-element.78), channel_id=1, source_target_pairs={{1,2},{2,1},{5,6},{6,5},{9,10},{10,9},{13,14},{14,13},{17,18},{18,... | collective-permute-start | bytes 1179656 | tf_op jit(solution)/shard_map/ppermute | solution.py:30
  308.3 26.3 %collective-permute-start.30 = (bf16[3,4,64,256]{3,2,1,0:T(8,128)(2,1)S(1)}, bf16[3,4,64,256]{3,2,1,0:T(8,128)(2,1)S(1)}, u32[]{:S(2)}, u32[]{:S(2)}) collective-permute-start(bf16[3,4,64,256]{3,2,1,0:T(8,128)(2,1)S(1)} %get-tuple-element.76), channel_id=1, source_target_pairs={{1,3},{2,0},{5,7},{6,4},{9,11},{10,8},{13,15},{14,12},{17,19},{18,... | collective-permute-start | bytes 1179656 | tf_op jit(solution)/shard_map/ppermute | solution.py:30
  309.6 25.9 %collective-permute-start.29 = (bf16[3,4,64,256]{3,2,1,0:T(8,128)(2,1)S(1)}, bf16[3,4,64,256]{3,2,1,0:T(8,128)(2,1)}, u32[]{:S(2)}, u32[]{:S(2)}) collective-permute-start(bf16[3,4,64,256]{3,2,1,0:T(8,128)(2,1)S(1)} %get-tuple-element.75), channel_id=1, source_target_pairs={{1,0},{2,3},{5,4},{6,7},{9,8},{10,11},{13,12},{14,15},{17,16},{18,... | collective-permute-start | bytes 1179656 | tf_op jit(solution)/shard_map/ppermute | solution.py:30
  310.9 25.8 %collective-permute-start.28 = (bf16[3,4,64,256]{3,2,1,0:T(8,128)(2,1)S(1)}, bf16[3,4,64,256]{3,2,1,0:T(8,128)(2,1)}, u32[]{:S(2)}, u32[]{:S(2)}) collective-permute-start(bf16[3,4,64,256]{3,2,1,0:T(8,128)(2,1)S(1)} %get-tuple-element.74), channel_id=1, source_target_pairs={{1,2},{2,1},{5,6},{6,5},{9,10},{10,9},{13,14},{14,13},{17,18},{18,... | collective-permute-start | bytes 1179656 | tf_op jit(solution)/shard_map/ppermute | solution.py:30
  331.9 19.0 %collective-permute-start.26 = (bf16[3,4,64,256]{3,2,1,0:T(8,128)(2,1)S(1)}, bf16[3,4,64,256]{3,2,1,0:T(8,128)(2,1)S(1)}, u32[]{:S(2)}, u32[]{:S(2)}) collective-permute-start(bf16[3,4,64,256]{3,2,1,0:T(8,128)(2,1)S(1)} %get-tuple-element.72), channel_id=1, source_target_pairs={{1,3},{2,0},{5,7},{6,4},{9,11},{10,8},{13,15},{14,12},{17,19},{18,... | collective-permute-start | bytes 1179656 | tf_op jit(solution)/shard_map/ppermute | solution.py:30
  333.3 24.7 %collective-permute-start.25 = (bf16[3,4,64,256]{3,2,1,0:T(8,128)(2,1)S(1)}, bf16[3,4,64,256]{3,2,1,0:T(8,128)(2,1)S(1)}, u32[]{:S(2)}, u32[]{:S(2)}) collective-permute-start(bf16[3,4,64,256]{3,2,1,0:T(8,128)(2,1)S(1)} %get-tuple-element.71), channel_id=1, source_target_pairs={{1,0},{2,3},{5,4},{6,7},{9,8},{10,11},{13,12},{14,15},{17,16},{18,... | collective-permute-start | bytes 1179656 | tf_op jit(solution)/shard_map/ppermute | solution.py:30
  334.6 23.4 %collective-permute-start.24 = (bf16[3,4,64,256]{3,2,1,0:T(8,128)(2,1)S(1)}, bf16[3,4,64,256]{3,2,1,0:T(8,128)(2,1)S(1)}, u32[]{:S(2)}, u32[]{:S(2)}) collective-permute-start(bf16[3,4,64,256]{3,2,1,0:T(8,128)(2,1)S(1)} %get-tuple-element.70), channel_id=1, source_target_pairs={{1,2},{2,1},{5,6},{6,5},{9,10},{10,9},{13,14},{14,13},{17,18},{18,... | collective-permute-start | bytes 1179656 | tf_op jit(solution)/shard_map/ppermute | solution.py:30
  335.5 39.4 %collective-permute-start.54 = (bf16[3,8,128,128]{3,2,1,0:T(8,128)(2,1)S(1)}, bf16[3,8,128,128]{3,2,1,0:T(8,128)(2,1)S(1)}, u32[]{:S(2)}, u32[]{:S(2)}) collective-permute-start(bf16[3,8,128,128]{3,2,1,0:T(8,128)(2,1)S(1)} %copy-done.41), channel_id=1, source_target_pairs={{1,0},{2,3},{5,4},{6,7},{9,8},{10,11},{13,12},{14,15},{17,16},{18,... | collective-permute-start | bytes 2359304 | tf_op jit(solution)/shard_map/ppermute | solution.py:30
  336.8 54.9 %collective-permute-start.55 = (bf16[3,8,128,128]{3,2,1,0:T(8,128)(2,1)}, bf16[3,8,128,128]{3,2,1,0:T(8,128)(2,1)S(1)}, u32[]{:S(2)}, u32[]{:S(2)}) collective-permute-start(bf16[3,8,128,128]{3,2,1,0:T(8,128)(2,1)} %get-tuple-element.90), channel_id=1, source_target_pairs={{1,0},{2,3},{5,4},{6,7},{9,8},{10,11},{13,12},{14,15},{17,16},{18,... | collective-permute-start | bytes 2359304 | tf_op jit(solution)/shard_map/ppermute | solution.py:30
  (34 other events, 536.2 us)

commit v2 on v1

v2 whole, which is shorter than its diff:
```python
import functools
import itertools

import jax
import jax.numpy as jnp
from jax import lax
from jax.experimental import pallas as pl
from jax.experimental.pallas import tpu as pltpu
from jax.sharding import PartitionSpec as P

AXES = ("section", "hid", "dp")
VMEM_LIMIT = 52 * 1024 * 1024
ROOT = 0.7978845608028654
CUBE = 0.044715
F32 = jnp.float32
BF16 = jnp.bfloat16


def send(value, target):
    sizes = [lax.axis_size(axis) for axis in AXES]

    def flat(at):
        return (at[0] * sizes[1] + at[1]) * sizes[2] + at[2]

    route = []
    for at in itertools.product(*(range(size) for size in sizes)):
        to = target(*at)
        if to is not None:
            route.append((flat(at), flat(to)))
    return lax.ppermute(value, AXES, route)


def along_dp(value, apart):
    return send(value, lambda s, h, z: (s, h, z ^ apart))


def partner(value, bit):
    return send(value, lambda s, h, z: (s, h ^ 1 << bit, z))


def section_partner(value, bit, active):
    return send(value, lambda s, h, z: (s, h ^ 1 << bit, z) if s == active else None)


def section_down(value, active):
    return send(value, lambda s, h, z: (s - 1, h, z) if s == active else None)


def chain_body(factors, steps, per_step, blk, fgroup, info, pick_up, pick_down, *refs):
    g_refs, refs = refs[:factors], refs[factors:]
    pre_ref, refs = refs[0], refs[1:]
    down_refs, refs = refs[:factors], refs[factors:]
    up_refs, refs = refs[:factors], refs[factors:]
    du_old, keep_old, give_old = refs[:3]
    du_ref, keep_ref, give_ref, own_ref = refs[3:7]
    cross_refs, total = refs[7:-1], refs[-1]
    hgroup = steps * per_step
    half, quarter = blk // 2, blk // 4
    step = pl.program_id(0)
    active = info[0] == 1

    @pl.when(jnp.logical_not(active))
    def _():
        du_ref[...] = du_old[...]

        @pl.when(step == 0)
        def _():
            keep_ref[...] = keep_old[...]
            give_ref[...] = give_old[...]

    @pl.when(active)
    def _():
        @pl.when(step == 0)
        def _():
            total[...] = jnp.zeros_like(total)

            def quarters(ref, at):
                odd = at % 2 == 1
                found = []
                for b in range(fgroup):
                    start = pl.multiple_of(b * blk + at // 2 * half, half)
                    wide = ref[:, pl.ds(start, half)]
                    found.append(jnp.where(odd, wide[:, quarter:], wide[:, :quarter]))
                return jnp.concatenate(found, axis=1)

            for f in range(factors):
                keep_ref[f] = quarters(g_refs[f], info[1])
            for k in range(1, 4):
                give_ref[k - 1] = quarters(g_refs[0], info[1] ^ k)

        for k in range(per_step):
            j = step * per_step + k
            columns = slice(k * blk, (k + 1) * blk)
            da = None
            for f in range(factors):
                pick = pick_down[info[2 + f] * hgroup + j]
                chosen = g_refs[f][:, pl.ds(pl.multiple_of(pick * blk, blk), blk)]
                part = lax.dot_general(
                    chosen, down_refs[f][0, 0, k], (((1,), (1,)), ((), ())), preferred_element_type=F32
                )
                da = part if da is None else da + part
            v = pre_ref[0, 0, :, columns].astype(F32)
            square = v * v
            t = jnp.tanh(ROOT * v * (1.0 + CUBE * square))
            slope = 0.5 * (1.0 + t) + 0.5 * ROOT * v * (1.0 - t * t) * (1.0 + 3.0 * CUBE * square)
            du = (slope * da).astype(BF16)
            du_ref[:, columns] = du
            for f in range(factors):
                pick = pick_up[info[2 + f] * hgroup + j]
                place = pl.ds(pl.multiple_of(pick * blk, blk), blk)
                total[f, :, place] += lax.dot_general(
                    du, up_refs[f][0, 0, k], (((1,), (1,)), ((), ())), preferred_element_type=F32
                )

        @pl.when(step == steps - 1)
        def _():
            own_ref[...] = g_refs[0][...].astype(F32) + total[0]
            for f in range(1, factors):
                cross_refs[f - 1][...] = total[f].astype(BF16)


def chain(info, pick_up, pick_down, g_list, pre_act, down_weight, up_weight, du, keep, give, micro):
    factors = len(g_list)
    tokens, width = g_list[0].shape
    hgroup, blk = up_weight.shape[2], up_weight.shape[-1]
    fgroup = width // blk
    per_step = min(4, hgroup)
    steps = hgroup // per_step
    wide = per_step * blk
    whole = pl.BlockSpec((tokens, width), lambda j, *s: (0, 0))

    def weight_spec(f):
        return pl.BlockSpec(
            (1, 1, per_step, blk, blk), lambda j, info, *s: (0, info[2 + f], j * info[0], 0, 0)
        )

    du_spec = pl.BlockSpec((tokens, wide), lambda j, *s: (micro, j))
    keep_spec = pl.BlockSpec((factors, tokens, width // 4), lambda j, *s: (0, micro, 0))
    give_spec = pl.BlockSpec((3, tokens, width // 4), lambda j, *s: (0, micro, 0))
    pre_spec = pl.BlockSpec((1, 1, tokens, wide), lambda j, info, *s: (0, micro, 0, j * info[0]))
    first_alias = 3 + factors + 1 + 2 * factors
    flat = jax.ShapeDtypeStruct((tokens, width), BF16)
    macs = tokens * hgroup * blk * blk * factors * 2
    return pl.pallas_call(
        functools.partial(chain_body, factors, steps, per_step, blk, fgroup),
        grid_spec=pltpu.PrefetchScalarGridSpec(
            num_scalar_prefetch=3,
            grid=(steps,),
            in_specs=[whole] * factors
            + [pre_spec]
            + [weight_spec(f) for f in range(factors)] * 2
            + [du_spec, keep_spec, give_spec],
            out_specs=[du_spec, keep_spec, give_spec, whole] + [whole] * (factors - 1),
            scratch_shapes=[pltpu.VMEM((factors, tokens, width), F32)],
        ),
        out_shape=[
            jax.ShapeDtypeStruct(du.shape, BF16),
            jax.ShapeDtypeStruct(keep.shape, BF16),
            jax.ShapeDtypeStruct(give.shape, BF16),
            jax.ShapeDtypeStruct((tokens, width), F32),
        ]
        + [flat] * (factors - 1),
        input_output_aliases={first_alias: 0, first_alias + 1: 1, first_alias + 2: 2},
        compiler_params=pltpu.CompilerParams(vmem_limit_bytes=VMEM_LIMIT),
        cost_estimate=pl.CostEstimate(
            flops=2 * macs, bytes_accessed=4 * factors * hgroup * blk * blk, transcendentals=0
        ),
        name="chain",
    )(
        info,
        pick_up,
        pick_down,
        *g_list,
        pre_act,
        *[down_weight] * factors,
        *[up_weight] * factors,
        du,
        keep,
        give,
    )


def up_body(factors, per_step, hgroup, blk, info, pick_up, *refs):
    x_refs, du_ref, out_ref = refs[:factors], refs[factors], refs[factors + 1]
    for k in range(per_step):
        j = pl.program_id(0) * per_step + k
        for f in range(factors):
            slot = info[1 + f]
            place = pl.ds(pl.multiple_of(pick_up[slot * hgroup + j] * blk, blk), blk)
            product = jnp.dot(
                x_refs[f][place, :],
                du_ref[:, k * blk : (k + 1) * blk],
                preferred_element_type=F32,
            )
            out_ref[slot, k] = product.astype(BF16)


def up_products(info, pick_up, x_groups, du, blk):
    factors = len(x_groups)
    width, tokens = x_groups[0].shape
    hgroup = du.shape[1] // blk
    per_step = min(4, hgroup)
    x_spec = pl.BlockSpec((width, tokens), lambda i, *s: (0, 0))
    return pl.pallas_call(
        functools.partial(up_body, factors, per_step, hgroup, blk),
        grid_spec=pltpu.PrefetchScalarGridSpec(
            num_scalar_prefetch=2,
            grid=(hgroup // per_step,),
            in_specs=[x_spec] * factors
            + [pl.BlockSpec((tokens, per_step * blk), lambda i, *s: (0, i))],
            out_specs=pl.BlockSpec((factors, per_step, blk, blk), lambda i, *s: (0, i, 0, 0)),
        ),
        out_shape=jax.ShapeDtypeStruct((factors, hgroup, blk, blk), BF16),
        compiler_params=pltpu.CompilerParams(vmem_limit_bytes=VMEM_LIMIT),
        cost_estimate=pl.CostEstimate(
            flops=2 * factors * hgroup * blk * blk * tokens,
            bytes_accessed=2 * factors * hgroup * blk * blk,
            transcendentals=0,
        ),
        name="up_products",
    )(info, pick_up, *x_groups, du)


def down_body(factors, per_step, hgroup, blk, info, pick_down, act_ref, keep_ref, *refs):
    given, out_ref, turned = refs[:-2], refs[-2], refs[-1]
    quarter = blk // 4
    tokens = act_ref.shape[1]

    @pl.when(pl.program_id(0) == 0)
    def _():
        for f in range(factors):
            for k in range(4):
                source = keep_ref[f] if k == 0 else given[f][k - 1]
                start = pl.multiple_of((info[0] ^ k) * tokens, tokens)
                turned[f, :, pl.ds(start, tokens)] = source.T

    for k in range(per_step):
        j = pl.program_id(0) * per_step + k
        rows = []
        for f in range(factors):
            pick = pick_down[info[1 + f] * hgroup + j]
            rows.append(turned[f, pl.ds(pl.multiple_of(pick * quarter, quarter), quarter), :])
        act = act_ref[:, :, k * blk : (k + 1) * blk].reshape(-1, blk)
        total = jnp.dot(jnp.concatenate(rows, axis=0), act, preferred_element_type=F32)
        for f in range(factors):
            out_ref[0, info[1 + f], k] = total[f * quarter : (f + 1) * quarter]


def down_products(info, pick_down, act_all, keep, given, blk):
    factors = keep.shape[0]
    devices, tokens, hidden = act_all.shape
    quarter_width = keep.shape[-1]
    hgroup = hidden // blk
    per_step = min(2, hgroup)
    return pl.pallas_call(
        functools.partial(down_body, factors, per_step, hgroup, blk),
        grid_spec=pltpu.PrefetchScalarGridSpec(
            num_scalar_prefetch=2,
            grid=(hgroup // per_step,),
            in_specs=[
                pl.BlockSpec((devices, tokens, per_step * blk), lambda i, *s: (0, 0, i)),
                pl.BlockSpec(keep.shape, lambda i, *s: (0, 0, 0)),
            ]
            + [pl.BlockSpec(given[0].shape, lambda i, *s: (0, 0, 0))] * factors,
            out_specs=pl.BlockSpec(
                (1, factors, per_step, blk // 4, blk), lambda i, *s: (0, 0, i, 0, 0)
            ),
            scratch_shapes=[pltpu.VMEM((factors, quarter_width, devices * tokens), BF16)],
        ),
        out_shape=jax.ShapeDtypeStruct((1, factors, hgroup, blk // 4, blk), F32),
        compiler_params=pltpu.CompilerParams(vmem_limit_bytes=VMEM_LIMIT),
        cost_estimate=pl.CostEstimate(
            flops=2 * factors * hgroup * blk * blk * tokens,
            bytes_accessed=2 * devices * tokens * hidden + factors * hgroup * blk * blk,
            transcendentals=0,
        ),
        name="down_products",
    )(info, pick_down, act_all, keep, *given)


def gelu_tanh(values):
    return jax.nn.gelu(values, approximate=True)


def local(acts_in, pre_act, out_grad, up_weight, down_weight, up_pick, down_pick, factor_order):
    bits = lax.axis_size("hid").bit_length() - 1
    factors = bits + 1
    sections = lax.axis_size("section")
    section = lax.axis_index("section")
    z = lax.axis_index("dp").astype(jnp.int32)
    micros, tokens, width = acts_in.shape[1:]
    hgroup, blk = up_weight.shape[2], up_weight.shape[-1]
    hidden = hgroup * blk
    rows = micros * tokens
    order = factor_order[0]
    pick_up = up_pick.reshape(-1)
    pick_down = down_pick.reshape(-1)
    place = jnp.concatenate([z[None], order])

    act = gelu_tanh(pre_act[0].astype(F32)).astype(BF16).reshape(rows, hidden)
    act_all = lax.all_gather(act, "dp")
    x_own = acts_in[0].reshape(rows, width).T

    du = jnp.zeros((rows, hidden), BF16)
    keep = jnp.zeros((factors, rows, width // 4), BF16)
    give = jnp.zeros((3, rows, width // 4), BF16)
    g_now = [out_grad[m] for m in range(micros)]
    grad = [None] * micros
    x_groups = None
    for step in range(sections):
        active = sections - 1 - step
        here = section == active
        info = jnp.concatenate([jnp.stack([here.astype(jnp.int32), z]), order])
        g_all = [
            [g_now[m]] + [section_partner(g_now[m], bit, active) for bit in range(bits)]
            for m in range(micros)
        ]
        results = []
        for m in range(micros):
            du, keep, give, own, *cross = chain(
                info, pick_up, pick_down, g_all[m], pre_act, down_weight, up_weight, du, keep, give, m
            )
            total = own
            for bit in range(bits):
                total = total + section_partner(cross[bit], bit, active).astype(F32)
            results.append(total.astype(BF16))
        for m in range(micros):
            grad[m] = results[m] if step == 0 else jnp.where(here, results[m], grad[m])
        if step + 1 < sections:
            g_now = [section_down(results[m], active) for m in range(micros)]
        if x_groups is None:
            x_groups = [x_own] + [partner(x_own, bit) for bit in range(bits)]

    up_part = up_products(place, pick_up, x_groups, du, blk)
    up_grad = lax.psum_scatter(up_part, "dp", scatter_dimension=2, tiled=True).astype(F32)[None]

    given = jnp.stack([along_dp(give[k - 1], k) for k in range(1, 4)])
    given = [given] + [partner(given, bit) for bit in range(bits)]
    down_grad = down_products(place, pick_down, act_all, keep, given, blk).swapaxes(3, 4)

    return jnp.stack(grad)[None], up_grad, down_grad


def solution(mesh):
    placed = (
        P("section", None, "dp", "hid"),
        P("section", None, "dp", "hid"),
        P(None, "dp", "hid"),
        P("section", None, "hid", None, None),
        P("section", None, "hid", None, None),
        P("section", None, "hid"),
        P("section", None, "hid"),
        P("section", None),
    )
    return jax.shard_map(
        local,
        mesh=mesh,
        in_specs=placed,
        out_specs=(
            P("section", None, "dp", "hid"),
            P("section", None, "hid", "dp", None),
            P("section", None, "hid", None, "dp"),
        ),
        check_vma=False,
    )
```

time: 411 us -> 310 us (0.75); the launches traced: 405 us -> 309 us
  starting transfers between devices: 112 us -> 34.2 us
  Pallas kernels: 84.9 us -> 55.1 us
  local copies, waits for them, and re-layouts: 25.7 us -> 12 us
  waiting for transfers between devices: 167 us -> 180 us
  between operations: 1.74 us -> 14.6 us
    ppermute x56 -> x25, starting transfers between devices: 112 us -> 34.1 us  [send(): return lax.ppermute(value, AXES, route)]
    reduce_scatter x0 -> x1, waiting for transfers between devices: none -> 69.8 us  [local(): lax.psum_scatter(up_part, 'dp', scatter_dimension=2, tiled=True).astype(F32)]
    ppermute x56 -> x25, waiting for transfers between devices: 167 us -> 111 us  [send(): return lax.ppermute(value, AXES, route)]
    pallas_call x9 -> x5, Pallas kernels: 65.7 us -> 44.5 us  [the longest x4 37.5 us: chain(): pl.pallas_call(functools.partial(chain_body, factors, steps, per_step, bl...]
    pallas_call x2 -> x1, Pallas kernels: 19.2 us -> 10.6 us  [down_products(): pl.pallas_call(functools.partial(down_body, factors, per_step, hgroup, bl...]
    convert_element_type x1 -> x0, local copies, waits for them, and re-layouts: 5.66 us -> none  [local(): act = gelu_tanh(pre_act[0].astype(F32)).astype(BF16).reshape(rows, hidden).T]
    squeeze x2 -> x1, local copies, waits for them, and re-layouts: 4.61 us -> 0.05 us  [local(): given = jnp.stack([along_dp(give[k - 1], k) for k in range(1, 4)])]
  transfers between devices with their start and end apart: 56 -> 27, of which waited for: 15 -> 7; matrix products, arithmetic and copies ran while one was open for 8% -> 3% of each run, Pallas kernels for 19% -> 18%
where the time goes in v2:
time: 310 us; the launch traced here: 309 us
  waiting for transfers between devices  180 us (58%)
  Pallas kernels  55.1 us (18%)
  starting transfers between devices  34.2 us (11%)
  between operations  14.6 us (5%)
  other arithmetic  12.7 us (4%)
  local copies, waits for them, and re-layouts  12 us (4%)
    ppermute x25, waiting for transfers between devices, send(): return lax.ppermute(value, AXES, route)  111 us
    reduce_scatter x1, waiting for transfers between devices, local(): lax.psum_scatter(up_part, 'dp', scatter_dimension=2, tiled=True).astype(F32)  69.8 us
    pallas_call x4, Pallas kernels, chain(): pl.pallas_call(functools.partial(chain_body, factors, steps, per_step, bl...  37.5 us
    ppermute x25, starting transfers between devices, send(): return lax.ppermute(value, AXES, route)  34.1 us
    pallas_call x1, Pallas kernels, down_products(): pl.pallas_call(functools.partial(down_body, factors, per_step, hgroup, bl...  10.6 us
    pallas_call x1, Pallas kernels, up_products(): pl.pallas_call(functools.partial(up_body, factors, per_step, hgroup, blk)...  6.96 us
    unnamed x48, local copies, waits for them, and re-layouts  6.67 us
  transfers between devices with their start and end apart: 27, of which 7 were waited for; matrix products, arithmetic and copies ran while one was open for 3% of the time, Pallas kernels for 18%

profile of v2, /device:TPU:0, one launch (start us, length us, event | category | flops | bytes accessed | tf_op | source)
XLA Modules:
  0.0 309.0 jit_solution(3448960330600742215)
XLA Ops:
  7.3 4.4 %fusion.5 = bf16[1,256,4096]{2,1,0:T(8,128)(2,1)} fusion(bf16[1,2,128,4096]{3,2,1,0:T(8,128)(2,1)} %refs_3_.7), kind=kLoop, calls=%fused_computation.9 | loop fusion | flops 10485760 | bytes 4194304 | tf_op jit(solution)/shard_map/convert_element_type | solution.py:300
  11.7 0.1 slice_bitcast_fusion.1
  11.8 0.7 collective-permute-start
  12.6 0.7 collective-permute-start.1
  13.3 0.7 collective-permute-start.7
  14.0 0.7 collective-permute-start.8
  14.7 0.1 reshape.54.pick_up
  14.8 0.1 reshape.55.pick_down
  14.9 0.1 add_add_fusion
  15.0 1.6 broadcast_in_dim.13.refs_10_
  16.6 1.0 broadcast_1_refs_11__refs_12_.2.refs_11_
  17.6 0.9 broadcast_1_refs_11__refs_12_.2.clone.refs_12_
  18.5 6.7 %chain.4 = (bf16[256,4096]{1,0:T(8,128)(2,1)}, bf16[3,256,512]{2,1,0:T(8,128)(2,1)}, bf16[3,256,512]{2,1,0:T(8,128)(2,1)}, f32[128,2048]{1,0:T(8,128)}, bf16[128...) custom-call(s32[5]{0:T(128)S(1)} %get-tuple-element.57.info, ...), custom_call_target="tpu_custom_call", output_to_operand_aliasing={{0}: (13, {}), {1}: (14, {}), {2}: (15, {})} | custom-call | flops 1610612736 | bytes 12582912 | tf_op jit(solution)/shard_map/chain/pallas_call | solution.py:144
  25.2 0.7 collective-permute-start.3
  25.9 0.7 collective-permute-start.2
  26.7 0.8 copy-done.14
  27.4 0.2 copy-done.15
  27.6 6.2 %chain.5 = (bf16[256,4096]{1,0:T(8,128)(2,1)}, bf16[3,256,512]{2,1,0:T(8,128)(2,1)}, bf16[3,256,512]{2,1,0:T(8,128)(2,1)}, f32[128,2048]{1,0:T(8,128)}, bf16[128...) custom-call(s32[5]{0:T(128)S(1)} %get-tuple-element.57.info, ...), custom_call_target="tpu_custom_call", output_to_operand_aliasing={{0}: (13, {}), {1}: (14, {}), {2}: (15, {})} | custom-call | flops 1610612736 | bytes 12582912 | tf_op jit(solution)/shard_map/chain/pallas_call | solution.py:144
  33.9 0.7 collective-permute-start.12
  34.6 0.7 collective-permute-start.11
  35.3 0.2 add_convert_fusion.3
  35.5 1.3 collective-permute-start.4
  36.8 1.4 add_convert_fusion.1
  38.3 1.3 collective-permute-start.13
  39.6 46.7 %collective-permute-done.4.refs_0_ = bf16[128,2048]{1,0:T(8,128)(2,1)S(1)} collective-permute-done((bf16[128,2048]{1,0:T(8,128)(2,1)S(1)}, bf16[128,2048]{1,0:T(8,128)(2,1)S(1)}, u32[]{:S(2)}, u32[]{:S(2)}) %collective-permute-start.4) | collective-permute-done | bytes 524320 | tf_op jit(solution)/shard_map/ppermute | solution.py:30
  86.2 1.9 collective-permute-start.5
  88.1 1.5 copy.25
  89.6 0.6 collective-permute-start.18
  90.2 1.5 collective-permute-start.19
  91.7 2.4 collective-permute-start.6
  94.1 4.6 %collective-permute-done.13.refs_0_ = bf16[128,2048]{1,0:T(8,128)(2,1)S(1)} collective-permute-done((bf16[128,2048]{1,0:T(8,128)(2,1)S(1)}, bf16[128,2048]{1,0:T(8,128)(2,1)S(1)}, u32[]{:S(2)}, u32[]{:S(2)}) %collective-permute-start.13) | collective-permute-done | bytes 524320 | tf_op jit(solution)/shard_map/ppermute | solution.py:30
  98.7 1.9 collective-permute-start.14
  100.7 2.5 collective-permute-start.15
  103.2 0.1 pad_add_fusion.info
  103.3 24.2 %collective-permute-done.6.refs_2_ = bf16[128,2048]{1,0:T(8,128)(2,1)S(1)} collective-permute-done((bf16[128,2048]{1,0:T(8,128)(2,1)S(1)}, bf16[128,2048]{1,0:T(8,128)(2,1)S(1)}, u32[]{:S(2)}, u32[]{:S(2)}) %collective-permute-start.6) | collective-permute-done | bytes 524320 | tf_op jit(solution)/shard_map/ppermute | solution.py:30
  127.5 0.8 copy-done.20
  128.2 12.3 %chain.6 = (bf16[256,4096]{1,0:T(8,128)(2,1)}, bf16[3,256,512]{2,1,0:T(8,128)(2,1)}, bf16[3,256,512]{2,1,0:T(8,128)(2,1)}, f32[128,2048]{1,0:T(8,128)}, bf16[128...) custom-call(s32[5]{0:T(128)S(1)} %get-tuple-element.56.info, ...), custom_call_target="tpu_custom_call", output_to_operand_aliasing={{0}: (13, {}), {1}: (14, {}), {2}: (15, {})} | custom-call | flops 1610612736 | bytes 12582912 | tf_op jit(solution)/shard_map/chain/pallas_call | solution.py:144
  140.6 0.8 copy-done.18
  141.3 0.2 copy-done.19
  141.5 12.3 %chain.7 = (bf16[256,4096]{1,0:T(8,128)(2,1)}, bf16[3,256,512]{2,1,0:T(8,128)(2,1)}, bf16[3,256,512]{2,1,0:T(8,128)(2,1)}, f32[128,2048]{1,0:T(8,128)}, bf16[128...) custom-call(s32[5]{0:T(128)S(1)} %get-tuple-element.56.info, ...), custom_call_target="tpu_custom_call", output_to_operand_aliasing={{0}: (13, {}), {1}: (14, {}), {2}: (15, {})} | custom-call | flops 1610612736 | bytes 12582912 | tf_op jit(solution)/shard_map/chain/pallas_call | solution.py:144
  153.8 0.8 copy-done.1
  154.6 1.0 copy-done.8
  155.6 0.3 copy-done.9
  155.9 7.0 %up_products.1 = bf16[3,16,256,256]{3,2,1,0:T(8,128)(2,1)} custom-call(s32[4]{0:T(128)S(1)} %pad_add_fusion.info, s32[48]{0:T(128)S(1)} %reshape.54.pick_up, bf16[2048,256]{1,0:T(8,128)(2,1)S(1)} %bitcast.34, bf16[2048,256]{1,0:T(8,128)(2,1)} %copy-done.8, bf16[2048,256]{1,0:T(8,128)(2,1)} %copy-done.9, bf16[256,4096]{1,0:T(8,128)(2,1)} %get-tuple-element.48.refs_3_), custom_call_target="tpu_custom_call" | custom-call | flops 1610612736 | bytes 6291456 | tf_op jit(solution)/shard_map/up_products/pallas_call | solution.py:204
  162.9 1.0 copy-done.2
  163.9 3.4 %collective-permute-start.17 = (bf16[128,2048]{1,0:T(8,128)(2,1)S(1)}, bf16[128,2048]{1,0:T(8,128)(2,1)S(1)}, u32[]{:S(2)}, u32[]{:S(2)}) collective-permute-start(bf16[128,2048]{1,0:T(8,128)(2,1)S(1)} %copy-done.2), channel_id=1, source_target_pairs={{0,8},{1,9},{2,10},{3,11},{4,12},{5,13},{6,14},{7,15},{8,0},{9,1},... | collective-permute-start | bytes 1572872 | tf_op jit(solution)/shard_map/ppermute | solution.py:30
  167.3 1.9 collective-permute-start.16
  169.3 3.7 %collective-permute-start.22 = (bf16[256,512]{1,0:T(8,128)(2,1)S(1)}, bf16[256,512]{1,0:T(8,128)(2,1)S(1)}, u32[]{:S(2)}, u32[]{:S(2)}) collective-permute-start(bf16[256,512]{1,0:T(8,128)(2,1)S(1)} %get-tuple-element.54), channel_id=1, source_target_pairs={{0,3},{1,2},{2,1},{3,0},{4,7},{5,6},{6,5},{7,4},{8,11},{9,10},{10,... | collective-permute-start | bytes 786440 | tf_op jit(solution)/shard_map/ppermute | solution.py:30
  173.0 0.7 collective-permute-start.20
  173.8 6.6 %collective-permute-done.22 = bf16[256,512]{1,0:T(8,128)(2,1)S(1)} collective-permute-done((bf16[256,512]{1,0:T(8,128)(2,1)S(1)}, bf16[256,512]{1,0:T(8,128)(2,1)S(1)}, u32[]{:S(2)}, u32[]{:S(2)}) %collective-permute-start.22) | collective-permute-done | bytes 262176 | tf_op jit(solution)/shard_map/ppermute | solution.py:30
  180.4 2.4 collective-permute-start.10
  182.9 13.2 %collective-permute-done.21 = bf16[256,512]{1,0:T(8,128)(2,1)S(1)} collective-permute-done((bf16[256,512]{1,0:T(8,128)(2,1)S(1)}, bf16[256,512]{1,0:T(8,128)(2,1)S(1)}, u32[]{:S(2)}, u32[]{:S(2)}) %collective-permute-start.21) | collective-permute-done | bytes 262176 | tf_op jit(solution)/shard_map/ppermute | solution.py:30
  196.0 1.9 collective-permute-start.9
  198.0 0.1 pad_maximum_fusion.refs_0_
  198.1 0.6 collective-permute-start.23
  198.6 0.4 collective-permute-start.24
  199.1 1.6 fusion.9
  200.7 0.3 fusion.7
  201.0 1.1 maximum_bitcast_fusion
  202.1 0.9 copy-done.13
  203.0 15.3 %collective-permute-done.24.refs_2_ = bf16[3,256,512]{2,1,0:T(8,128)(2,1)} collective-permute-done((bf16[3,256,512]{2,1,0:T(8,128)(2,1)S(1)}, bf16[3,256,512]{2,1,0:T(8,128)(2,1)}, u32[]{:S(2)}, u32[]{:S(2)}) %collective-permute-start.24) | collective-permute-done | bytes 786464 | tf_op jit(solution)/shard_map/ppermute | solution.py:30
  218.3 10.6 %down_products.1 = f32[1,3,16,64,256]{4,3,2,1,0:T(8,128)} custom-call(s32[4]{0:T(128)S(1)} %pad_add_fusion.info, s32[48]{0:T(128)S(1)} %reshape.55.pick_down, bf16[4,256,4096]{2,1,0:T(8,128)(2,1)} %all-gather.2.cloned.1.call-done.act_ref, bf16[3,256,512]{2,1,0:T(8,128)(2,1)S(1)} %copy-done, bf16[3,256,512]{2,1,0:T(8,128)(2,1)S(1)} %pad_maximum_fusion.refs_0_, ...), custom_call_target="tpu_custom_call" | custom-call | flops 1610612736 | bytes 11534336 | tf_op jit(solution)/shard_map/down_products/pallas_call | solution.py:255
  228.9 69.8 %reduce-scatter.2.cloned.1.call-done = bf16[3,16,64,256]{3,2,1,0:T(8,128)(2,1)} async-done(((bf16[3,16,256,256]{3,2,1,0:T(8,128)(2,1)}), bf16[3,16,64,256]{3,2,1,0:T(8,128)(2,1)}) %reduce-scatter.2.cloned.1.call-update) | async-done | bytes 1572880 | tf_op jit(solution)/shard_map/reduce_scatter | solution.py:335
  298.7 3.5 %bitcast_convert_fusion = f32[1,3,16,64,256]{4,3,2,1,0:T(8,128)} fusion(bf16[3,16,64,256]{3,2,1,0:T(8,128)(2,1)} %reduce-scatter.2.cloned.1.call-done), kind=kLoop, calls=%fused_computation.10 | loop fusion | flops 786432 | bytes 4718592 | tf_op jit(solution)/shard_map/broadcast_in_dim | solution.py:335
  (66 shorter events, 0.3 us)
Async XLA Ops:
  7.2 4.6 %copy-start.10 = (bf16[2,128,2048]{2,1,0:T(8,128)(2,1)S(1)}, bf16[2,128,2048]{2,1,0:T(8,128)(2,1)}, u32[]{:S(2)}) copy-start(bf16[2,128,2048]{2,1,0:T(8,128)(2,1)} %param.10) | copy-start | bytes 3145732
  7.2 7.5 %copy-start.21 = (s32[1,3,16]{2,0,1:T(1,128)S(1)}, s32[1,3,16]{2,0,1:T(1,128)}, u32[]{:S(2)}) copy-start(s32[1,3,16]{2,0,1:T(1,128)} %param.13) | copy-start | bytes 580
  7.2 7.6 %copy-start.22 = (s32[1,3,16]{2,0,1:T(1,128)S(1)}, s32[1,3,16]{2,0,1:T(1,128)}, u32[]{:S(2)}) copy-start(s32[1,3,16]{2,0,1:T(1,128)} %param.14) | copy-start | bytes 580
  7.2 7.7 %copy-start.23 = (s32[1,3]{1,0:T(1,128)S(1)}, s32[1,3]{1,0:T(1,128)}, u32[]{:S(2)}) copy-start(s32[1,3]{1,0:T(1,128)} %param.15) | copy-start | bytes 40
  7.2 211.1 %all-gather.2.cloned.1.call-start = ((), (), s32[]{:S(2)}) async-start(), calls=%async_computation.2 | async-start | bytes 10485760 | tf_op jit(solution)/shard_map/all_gather | solution.py:301
  11.7 287.0 %reduce-scatter.2.cloned.1.call-start = ((), (), s32[]{:S(2)}) async-start(), calls=%async_computation.1 | async-start | bytes 7864320 | tf_op jit(solution)/shard_map/reduce_scatter | solution.py:335
  11.8 3.1 %collective-permute-start = (bf16[128,2048]{1,0:T(8,128)(2,1)S(1)}, bf16[128,2048]{1,0:T(8,128)(2,1)S(1)}, u32[]{:S(2)}, u32[]{:S(2)}) collective-permute-start(bf16[128,2048]{1,0:T(8,128)(2,1)S(1)} %get-tuple-element.51.refs_0_), channel_id=1, source_target_pairs={{16,20},{17,21},{18,22},{19,23},{20,16},{21,17},{22,18},{23,19},{2... | collective-permute-start | bytes 1572872 | tf_op jit(solution)/shard_map/ppermute | solution.py:30
  12.6 2.4 collective-permute-start.1
  13.3 13.4 %collective-permute-start.7 = (bf16[128,2048]{1,0:T(8,128)(2,1)S(1)}, bf16[128,2048]{1,0:T(8,128)(2,1)S(1)}, u32[]{:S(2)}, u32[]{:S(2)}) collective-permute-start(bf16[128,2048]{1,0:T(8,128)(2,1)S(1)} %get-tuple-element.52.refs_0_), channel_id=1, source_target_pairs={{16,20},{17,21},{18,22},{19,23},{20,16},{21,17},{22,18},{23,19},{2... | collective-permute-start | bytes 1572872 | tf_op jit(solution)/shard_map/ppermute | solution.py:30
  14.0 12.7 %collective-permute-start.8 = (bf16[128,2048]{1,0:T(8,128)(2,1)S(1)}, bf16[128,2048]{1,0:T(8,128)(2,1)S(1)}, u32[]{:S(2)}, u32[]{:S(2)}) collective-permute-start(bf16[128,2048]{1,0:T(8,128)(2,1)S(1)} %get-tuple-element.52.refs_0_), channel_id=1, source_target_pairs={{16,24},{17,25},{18,26},{19,27},{20,28},{21,29},{22,30},{23,31},{2... | collective-permute-start | bytes 1572872 | tf_op jit(solution)/shard_map/ppermute | solution.py:30
  15.0 3.6 %copy-start.16 = (bf16[128,2048]{1,0:T(8,128)(2,1)}, bf16[128,2048]{1,0:T(8,128)(2,1)S(1)}, u32[]{:S(2)}) copy-start(bf16[128,2048]{1,0:T(8,128)(2,1)S(1)} %collective-permute-done.refs_1_) | copy-start | bytes 1572868
  15.0 3.5 %copy-start.17 = (bf16[128,2048]{1,0:T(8,128)(2,1)}, bf16[128,2048]{1,0:T(8,128)(2,1)S(1)}, u32[]{:S(2)}) copy-start(bf16[128,2048]{1,0:T(8,128)(2,1)S(1)} %collective-permute-done.1.refs_2_) | copy-start | bytes 1572868
  25.2 10.0 %collective-permute-start.3 = (bf16[128,2048]{1,0:T(8,128)(2,1)S(1)}, bf16[128,2048]{1,0:T(8,128)(2,1)S(1)}, u32[]{:S(2)}, u32[]{:S(2)}) collective-permute-start(bf16[128,2048]{1,0:T(8,128)(2,1)S(1)} %get-tuple-element.29), channel_id=1, source_target_pairs={{16,24},{17,25},{18,26},{19,27},{20,28},{21,29},{22,30},{23,31},{2... | collective-permute-start | bytes 1572872 | tf_op jit(solution)/shard_map/ppermute | solution.py:30
  25.9 9.4 %collective-permute-start.2 = (bf16[128,2048]{1,0:T(8,128)(2,1)S(1)}, bf16[128,2048]{1,0:T(8,128)(2,1)S(1)}, u32[]{:S(2)}, u32[]{:S(2)}) collective-permute-start(bf16[128,2048]{1,0:T(8,128)(2,1)S(1)} %get-tuple-element.28), channel_id=1, source_target_pairs={{16,20},{17,21},{18,22},{19,23},{20,16},{21,17},{22,18},{23,19},{2... | collective-permute-start | bytes 1572872 | tf_op jit(solution)/shard_map/ppermute | solution.py:30
  26.6 0.8 copy-start.14
  26.6 1.0 copy-start.15
  27.6 7.7 %copy-start.12 = (f32[128,2048]{1,0:T(8,128)S(1)}, f32[128,2048]{1,0:T(8,128)}, u32[]{:S(2)}) copy-start(f32[128,2048]{1,0:T(8,128)} %get-tuple-element.27) | copy-start | bytes 3145732
  33.9 2.9 collective-permute-start.12
  34.6 2.3 collective-permute-start.11
  35.5 52.7 %copy-start.4 = (bf16[128,2048]{1,0:T(8,128)(2,1)}, bf16[128,2048]{1,0:T(8,128)(2,1)S(1)}, u32[]{:S(2)}) copy-start(bf16[128,2048]{1,0:T(8,128)(2,1)S(1)} %add_convert_fusion.3) | copy-start | bytes 1572868
  35.5 50.7 %collective-permute-start.4 = (bf16[128,2048]{1,0:T(8,128)(2,1)S(1)}, bf16[128,2048]{1,0:T(8,128)(2,1)S(1)}, u32[]{:S(2)}, u32[]{:S(2)}) collective-permute-start(bf16[128,2048]{1,0:T(8,128)(2,1)S(1)} %add_convert_fusion.3), channel_id=1, source_target_pairs={{16,0},{17,1},{18,2},{19,3},{20,4},{21,5},{22,6},{23,7},{24,8},{25... | collective-permute-start | bytes 1572872 | tf_op jit(solution)/shard_map/ppermute | solution.py:30
  38.3 89.2 %copy-start.6 = (bf16[128,2048]{1,0:T(8,128)(2,1)}, bf16[128,2048]{1,0:T(8,128)(2,1)S(1)}, u32[]{:S(2)}) copy-start(bf16[128,2048]{1,0:T(8,128)(2,1)S(1)} %add_convert_fusion.1) | copy-start | bytes 1572868
  38.3 60.5 %collective-permute-start.13 = (bf16[128,2048]{1,0:T(8,128)(2,1)S(1)}, bf16[128,2048]{1,0:T(8,128)(2,1)S(1)}, u32[]{:S(2)}, u32[]{:S(2)}) collective-permute-start(bf16[128,2048]{1,0:T(8,128)(2,1)S(1)} %add_convert_fusion.1), channel_id=1, source_target_pairs={{16,0},{17,1},{18,2},{19,3},{20,4},{21,5},{22,6},{23,7},{24,8},{25... | collective-permute-start | bytes 1572872 | tf_op jit(solution)/shard_map/ppermute | solution.py:30
  86.2 14.4 %collective-permute-start.5 = (bf16[128,2048]{1,0:T(8,128)(2,1)S(1)}, bf16[128,2048]{1,0:T(8,128)(2,1)}, u32[]{:S(2)}, u32[]{:S(2)}) collective-permute-start(bf16[128,2048]{1,0:T(8,128)(2,1)S(1)} %collective-permute-done.4.refs_0_), channel_id=1, source_target_pairs={{0,4},{1,5},{2,6},{3,7},{4,0},{5,1},{6,2},{7,3},{8,12},{9,13},{10,... | collective-permute-start | bytes 1572872 | tf_op jit(solution)/shard_map/ppermute | solution.py:30
  89.6 65.0 %collective-permute-start.18 = (bf16[2048,256]{1,0:T(8,128)(2,1)S(1)}, bf16[2048,256]{1,0:T(8,128)(2,1)S(1)}, u32[]{:S(2)}, u32[]{:S(2)}) collective-permute-start(bf16[2048,256]{1,0:T(8,128)(2,1)S(1)} %bitcast.32), channel_id=1, source_target_pairs={{0,4},{1,5},{2,6},{3,7},{4,0},{5,1},{6,2},{7,3},{8,12},{9,13},{10,... | collective-permute-start | bytes 3145736 | tf_op jit(solution)/shard_map/ppermute | solution.py:30
  90.2 64.4 %collective-permute-start.19 = (bf16[2048,256]{1,0:T(8,128)(2,1)S(1)}, bf16[2048,256]{1,0:T(8,128)(2,1)S(1)}, u32[]{:S(2)}, u32[]{:S(2)}) collective-permute-start(bf16[2048,256]{1,0:T(8,128)(2,1)S(1)} %bitcast.33), channel_id=1, source_target_pairs={{0,8},{1,9},{2,10},{3,11},{4,12},{5,13},{6,14},{7,15},{8,0},{9,1},... | collective-permute-start | bytes 3145736 | tf_op jit(solution)/shard_map/ppermute | solution.py:30
  91.7 35.8 %collective-permute-start.6 = (bf16[128,2048]{1,0:T(8,128)(2,1)S(1)}, bf16[128,2048]{1,0:T(8,128)(2,1)S(1)}, u32[]{:S(2)}, u32[]{:S(2)}) collective-permute-start(bf16[128,2048]{1,0:T(8,128)(2,1)S(1)} %collective-permute-done.4.refs_0_), channel_id=1, source_target_pairs={{0,8},{1,9},{2,10},{3,11},{4,12},{5,13},{6,14},{7,15},{8,0},{9,1},... | collective-permute-start | bytes 1572872 | tf_op jit(solution)/shard_map/ppermute | solution.py:30
  98.7 41.8 %collective-permute-start.14 = (bf16[128,2048]{1,0:T(8,128)(2,1)S(1)}, bf16[128,2048]{1,0:T(8,128)(2,1)S(1)}, u32[]{:S(2)}, u32[]{:S(2)}) collective-permute-start(bf16[128,2048]{1,0:T(8,128)(2,1)S(1)} %collective-permute-done.13.refs_0_), channel_id=1, source_target_pairs={{0,4},{1,5},{2,6},{3,7},{4,0},{5,1},{6,2},{7,3},{8,12},{9,13},{10,... | collective-permute-start | bytes 1572872 | tf_op jit(solution)/shard_map/ppermute | solution.py:30
  100.7 39.9 %collective-permute-start.15 = (bf16[128,2048]{1,0:T(8,128)(2,1)S(1)}, bf16[128,2048]{1,0:T(8,128)(2,1)S(1)}, u32[]{:S(2)}, u32[]{:S(2)}) collective-permute-start(bf16[128,2048]{1,0:T(8,128)(2,1)S(1)} %collective-permute-done.13.refs_0_), channel_id=1, source_target_pairs={{0,8},{1,9},{2,10},{3,11},{4,12},{5,13},{6,14},{7,15},{8,0},{9,1},... | collective-permute-start | bytes 1572872 | tf_op jit(solution)/shard_map/ppermute | solution.py:30
  127.5 0.8 copy-start.20
  140.5 0.8 copy-start.18
  140.6 0.9 copy-start.19
  153.8 0.8 copy-start.1
  154.6 1.0 copy-start.8
  154.6 1.3 copy-start.9
  162.9 1.0 copy-start.2
  162.9 6.4 %copy-start.3 = (bf16[3,256,512]{2,1,0:T(8,128)(2,1)S(1)}, bf16[3,256,512]{2,1,0:T(8,128)(2,1)}, u32[]{:S(2)}) copy-start(bf16[3,256,512]{2,1,0:T(8,128)(2,1)} %get-tuple-element.50) | copy-start | bytes 2359300
  162.9 36.2 %copy-start.7 = (bf16[128,2048]{1,0:T(8,128)(2,1)S(1)}, bf16[128,2048]{1,0:T(8,128)(2,1)}, u32[]{:S(2)}) copy-start(bf16[128,2048]{1,0:T(8,128)(2,1)} %copy-done.6) | copy-start | bytes 1572868
  162.9 37.8 %copy-start.5 = (bf16[128,2048]{1,0:T(8,128)(2,1)S(1)}, bf16[128,2048]{1,0:T(8,128)(2,1)}, u32[]{:S(2)}) copy-start(bf16[128,2048]{1,0:T(8,128)(2,1)} %copy-done.4) | copy-start | bytes 1572868
  162.9 37.8 %copy-start.11 = (f32[128,2048]{1,0:T(8,128)S(1)}, f32[128,2048]{1,0:T(8,128)}, u32[]{:S(2)}) copy-start(f32[128,2048]{1,0:T(8,128)} %get-tuple-element.36) | copy-start | bytes 3145732
  163.9 34.7 %collective-permute-start.17 = (bf16[128,2048]{1,0:T(8,128)(2,1)S(1)}, bf16[128,2048]{1,0:T(8,128)(2,1)S(1)}, u32[]{:S(2)}, u32[]{:S(2)}) collective-permute-start(bf16[128,2048]{1,0:T(8,128)(2,1)S(1)} %copy-done.2), channel_id=1, source_target_pairs={{0,8},{1,9},{2,10},{3,11},{4,12},{5,13},{6,14},{7,15},{8,0},{9,1},... | collective-permute-start | bytes 1572872 | tf_op jit(solution)/shard_map/ppermute | solution.py:30
  167.3 31.8 %collective-permute-start.16 = (bf16[128,2048]{1,0:T(8,128)(2,1)S(1)}, bf16[128,2048]{1,0:T(8,128)(2,1)S(1)}, u32[]{:S(2)}, u32[]{:S(2)}) collective-permute-start(bf16[128,2048]{1,0:T(8,128)(2,1)S(1)} %get-tuple-element.46), channel_id=1, source_target_pairs={{0,4},{1,5},{2,6},{3,7},{4,0},{5,1},{6,2},{7,3},{8,12},{9,13},{10,... | collective-permute-start | bytes 1572872 | tf_op jit(solution)/shard_map/ppermute | solution.py:30
  169.3 11.1 %collective-permute-start.22 = (bf16[256,512]{1,0:T(8,128)(2,1)S(1)}, bf16[256,512]{1,0:T(8,128)(2,1)S(1)}, u32[]{:S(2)}, u32[]{:S(2)}) collective-permute-start(bf16[256,512]{1,0:T(8,128)(2,1)S(1)} %get-tuple-element.54), channel_id=1, source_target_pairs={{0,3},{1,2},{2,1},{3,0},{4,7},{5,6},{6,5},{7,4},{8,11},{9,10},{10,... | collective-permute-start | bytes 786440 | tf_op jit(solution)/shard_map/ppermute | solution.py:30
  173.0 23.0 %collective-permute-start.21 = (bf16[256,512]{1,0:T(8,128)(2,1)S(1)}, bf16[256,512]{1,0:T(8,128)(2,1)S(1)}, u32[]{:S(2)}, u32[]{:S(2)}) collective-permute-start(bf16[256,512]{1,0:T(8,128)(2,1)S(1)} %get-tuple-element.55), channel_id=1, source_target_pairs={{0,2},{1,3},{2,0},{3,1},{4,6},{5,7},{6,4},{7,5},{8,10},{9,11},{10,... | collective-permute-start | bytes 786440 | tf_op jit(solution)/shard_map/ppermute | solution.py:30
  173.0 24.9 %collective-permute-start.20 = (bf16[256,512]{1,0:T(8,128)(2,1)S(1)}, bf16[256,512]{1,0:T(8,128)(2,1)S(1)}, u32[]{:S(2)}, u32[]{:S(2)}) collective-permute-start(bf16[256,512]{1,0:T(8,128)(2,1)S(1)} %get-tuple-element.53), channel_id=1, source_target_pairs={{0,1},{1,0},{2,3},{3,2},{4,5},{5,4},{6,7},{7,6},{8,9},{9,8},{10,11... | collective-permute-start | bytes 786440 | tf_op jit(solution)/shard_map/ppermute | solution.py:30
  180.4 20.3 %collective-permute-start.10 = (bf16[128,2048]{1,0:T(8,128)(2,1)S(1)}, bf16[128,2048]{1,0:T(8,128)(2,1)S(1)}, u32[]{:S(2)}, u32[]{:S(2)}) collective-permute-start(bf16[128,2048]{1,0:T(8,128)(2,1)S(1)} %get-tuple-element.38), channel_id=1, source_target_pairs={{0,8},{1,9},{2,10},{3,11},{4,12},{5,13},{6,14},{7,15},{8,0},{9,1},... | collective-permute-start | bytes 1572872 | tf_op jit(solution)/shard_map/ppermute | solution.py:30
  196.0 4.6 %collective-permute-start.9 = (bf16[128,2048]{1,0:T(8,128)(2,1)S(1)}, bf16[128,2048]{1,0:T(8,128)(2,1)S(1)}, u32[]{:S(2)}, u32[]{:S(2)}) collective-permute-start(bf16[128,2048]{1,0:T(8,128)(2,1)S(1)} %get-tuple-element.37), channel_id=1, source_target_pairs={{0,4},{1,5},{2,6},{3,7},{4,0},{5,1},{6,2},{7,3},{8,12},{9,13},{10,... | collective-permute-start | bytes 1572872 | tf_op jit(solution)/shard_map/ppermute | solution.py:30
  198.1 4.0 %collective-permute-start.23 = (bf16[3,256,512]{2,1,0:T(8,128)(2,1)S(1)}, bf16[3,256,512]{2,1,0:T(8,128)(2,1)S(1)}, u32[]{:S(2)}, u32[]{:S(2)}) collective-permute-start(bf16[3,256,512]{2,1,0:T(8,128)(2,1)S(1)} %pad_maximum_fusion.refs_0_), channel_id=1, source_target_pairs={{0,4},{1,5},{2,6},{3,7},{4,0},{5,1},{6,2},{7,3},{8,12},{9,13},{10,... | collective-permute-start | bytes 2359304 | tf_op jit(solution)/shard_map/ppermute | solution.py:30
  198.6 19.6 %collective-permute-start.24 = (bf16[3,256,512]{2,1,0:T(8,128)(2,1)S(1)}, bf16[3,256,512]{2,1,0:T(8,128)(2,1)}, u32[]{:S(2)}, u32[]{:S(2)}) collective-permute-start(bf16[3,256,512]{2,1,0:T(8,128)(2,1)S(1)} %pad_maximum_fusion.refs_0_), channel_id=1, source_target_pairs={{0,8},{1,9},{2,10},{3,11},{4,12},{5,13},{6,14},{7,15},{8,0},{9,1},... | collective-permute-start | bytes 2359304 | tf_op jit(solution)/shard_map/ppermute | solution.py:30
  199.1 19.2 %copy-start = (bf16[3,256,512]{2,1,0:T(8,128)(2,1)S(1)}, bf16[3,256,512]{2,1,0:T(8,128)(2,1)}, u32[]{:S(2)}) copy-start(bf16[3,256,512]{2,1,0:T(8,128)(2,1)} %get-tuple-element.49.keep_ref) | copy-start | bytes 2359300
  202.1 0.9 copy-start.13
Sparse Core Ops, SparseCore 0:
  11.8 152.3 all-gather.1
  166.5 132.2 reduce-scatter.1

commit v3 on v0

v3 whole, which is shorter than its diff:
```python
import functools
import itertools

import jax
import jax.numpy as jnp
from jax import lax
from jax.experimental import pallas as pl
from jax.experimental.pallas import tpu as pltpu
from jax.sharding import PartitionSpec as P

AXES = ("section", "hid", "dp")
VMEM_LIMIT = 30 * 1024 * 1024
CHAIN_LIMIT = 24 * 1024 * 1024
SMALL_LIMIT = 16 * 1024 * 1024
ROOT = 0.7978845608028654
CUBE = 0.044715
F32 = jnp.float32
BF16 = jnp.bfloat16


def send(value, target):
    sizes = [lax.axis_size(axis) for axis in AXES]

    def flat(at):
        return (at[0] * sizes[1] + at[1]) * sizes[2] + at[2]

    route = []
    for at in itertools.product(*(range(size) for size in sizes)):
        to = target(*at)
        if to is not None:
            route.append((flat(at), flat(to)))
    return lax.ppermute(value, AXES, route)


def along_dp(value, apart):
    return send(value, lambda s, h, z: (s, h, z ^ apart))


def partner(value, bit):
    return send(value, lambda s, h, z: (s, h ^ 1 << bit, z))


def section_partner(value, bit, active):
    return send(value, lambda s, h, z: (s, h ^ 1 << bit, z) if s == active else None)


def section_down(value, active):
    return send(value, lambda s, h, z: (s - 1, h, z) if s == active else None)


def slope_of(v):
    square = v * v
    t = jnp.tanh(ROOT * v * (1.0 + CUBE * square))
    return 0.5 * (1.0 + t) + 0.5 * ROOT * v * (1.0 - t * t) * (1.0 + 3.0 * CUBE * square)


def block_of(index, size):
    return pl.ds(pl.multiple_of(index * size, size), size)


def chain_body(cfg, info, pick_up, pick_down, *refs):
    factors, chunks, blk, tokens, micro, terms = cfg
    refs = list(refs)

    def take(count):
        found = refs[:count]
        del refs[:count]
        return found

    g_hbm = take(factors)
    pre_hbm, down_hbm = take(2)
    up_hbm = take(1)[0] if terms else None
    take(1)
    du_hbm = take(1)[0]
    own_ref = take(1)[0] if terms else None
    cross_refs = take(factors - 1) if terms else None
    g_buf, pre_buf, down_buf, du_buf, g_sem, pre_sem, down_sem, du_sem = take(8)
    up_buf, total, up_sem = take(3) if terms else (None,) * 3
    per = down_buf.shape[1] // chunks
    hgroup = per * chunks
    active = info[0] == 1
    half = chunks // 2
    copy = pltpu.make_async_copy

    def g_copy(f):
        return copy(g_hbm[f], g_buf.at[f], g_sem.at[f])

    def weight_copy(hbm, buf, sem, f, c):
        rows = pl.ds(c * per, per)
        return copy(hbm.at[0, info[2 + f], rows], buf.at[f, rows], sem.at[f, c])

    def pre_copy():
        return copy(pre_hbm.at[0, micro], pre_buf, pre_sem)

    def du_copy(c):
        return copy(
            du_buf.at[:, block_of(c, per * blk)],
            du_hbm.at[c // half, pl.ds(micro * tokens, tokens), block_of(c % half, per * blk)],
            du_sem.at[c],
        )

    @pl.when(active)
    def _():
        for f in range(factors):
            g_copy(f).start()
        pre_copy().start()
        for c in range(chunks):
            for f in range(factors):
                weight_copy(down_hbm, down_buf, down_sem, f, c).start()
                if terms:
                    weight_copy(up_hbm, up_buf, up_sem, f, c).start()

    if terms:

        @pl.when(active)
        def _():
            total[...] = jnp.zeros_like(total)

    @pl.when(active)
    def _():
        for f in range(factors):
            g_copy(f).wait()
        pre_copy().wait()

    @pl.loop(0, chunks)
    def _(c):
        @pl.when(active)
        def _():
            for f in range(factors):
                weight_copy(down_hbm, down_buf, down_sem, f, c).wait()
                if terms:
                    weight_copy(up_hbm, up_buf, up_sem, f, c).wait()
            for k in range(per):
                j = c * per + k
                columns = block_of(j, blk)
                da = None
                for f in range(factors):
                    chosen = g_buf[f, :, block_of(pick_down[info[2 + f] * hgroup + j], blk)]
                    part = lax.dot_general(
                        chosen, down_buf[f, j], (((1,), (1,)), ((), ())), preferred_element_type=F32
                    )
                    da = part if da is None else da + part
                du = (slope_of(pre_buf[:, columns].astype(F32)) * da).astype(BF16)
                du_buf[:, columns] = du
                if terms:
                    for f in range(factors):
                        place = block_of(pick_up[info[2 + f] * hgroup + j], blk)
                        total[f, :, place] += lax.dot_general(
                            du, up_buf[f, j], (((1,), (1,)), ((), ())), preferred_element_type=F32
                        )
            du_copy(c).start()

    @pl.when(active)
    def _():
        if terms:
            own_ref[...] = g_buf[0].astype(F32) + total[0]
            for f in range(1, factors):
                cross_refs[f - 1][...] = total[f].astype(BF16)
        for c in range(chunks):
            du_copy(c).wait()


def chain(info, picks, g_list, pre_act, down_weight, up_weight, du, micro, terms):
    factors = len(g_list)
    tokens, width = g_list[0].shape
    hgroup, blk = up_weight.shape[2], up_weight.shape[-1]
    hidden = hgroup * blk
    chunks = min(4, hgroup)
    anywhere = pl.BlockSpec(memory_space=pl.ANY)
    inside = pl.BlockSpec(memory_space=pltpu.VMEM)
    dma = pltpu.SemaphoreType.DMA
    operands = [*g_list, pre_act, down_weight]
    out_shape = [jax.ShapeDtypeStruct(du.shape, BF16)]
    out_specs = [anywhere]
    scratch = [
        pltpu.VMEM((factors, tokens, width), BF16),
        pltpu.VMEM((tokens, hidden), BF16),
        pltpu.VMEM((factors, hgroup, blk, blk), BF16),
        pltpu.VMEM((tokens, hidden), BF16),
        dma((factors,)),
        dma,
        dma((factors, chunks)),
        dma((chunks,)),
    ]
    if terms:
        operands.append(up_weight)
        out_shape.append(jax.ShapeDtypeStruct((tokens, width), F32))
        out_shape += [jax.ShapeDtypeStruct((tokens, width), BF16)] * (factors - 1)
        out_specs += [inside] * factors
        scratch += [
            pltpu.VMEM((factors, hgroup, blk, blk), BF16),
            pltpu.VMEM((factors, tokens, width), F32),
            dma((factors, chunks)),
        ]
    operands.append(du)
    cfg = (factors, chunks, blk, tokens, micro, terms)
    macs = tokens * hgroup * blk * blk * factors * (1 + terms)
    return pl.pallas_call(
        functools.partial(chain_body, cfg),
        grid_spec=pltpu.PrefetchScalarGridSpec(
            num_scalar_prefetch=3,
            grid=(1,),
            in_specs=[anywhere] * len(operands),
            out_specs=out_specs,
            scratch_shapes=scratch,
        ),
        out_shape=out_shape,
        input_output_aliases={3 + len(operands) - 1: 0},
        compiler_params=pltpu.CompilerParams(vmem_limit_bytes=CHAIN_LIMIT),
        cost_estimate=pl.CostEstimate(
            flops=2 * macs,
            bytes_accessed=2 * factors * hgroup * blk * blk * (1 + terms),
            transcendentals=0,
        ),
        name="chain",
    )(info, *picks, *operands)


def terms_body(factors, per_step, hgroup, blk, info, pick_up, g_ref, du_ref, *refs):
    up_refs, own_ref = refs[:factors], refs[factors]
    cross_refs, total = refs[factors + 1 : -1], refs[-1]
    step = pl.program_id(0)

    @pl.when(info[0] == 1)
    def _():
        @pl.when(step == 0)
        def _():
            total[...] = jnp.zeros_like(total)

        for k in range(per_step):
            du = du_ref[0, :, k * blk : (k + 1) * blk]
            for f in range(factors):
                pick = pick_up[info[2 + f] * hgroup + step * per_step + k]
                total[f, :, block_of(pick, blk)] += lax.dot_general(
                    du, up_refs[f][0, 0, k], (((1,), (1,)), ((), ())), preferred_element_type=F32
                )

        @pl.when(step == pl.num_programs(0) - 1)
        def _():
            own_ref[...] = g_ref[...].astype(F32) + total[0]
            for f in range(1, factors):
                cross_refs[f - 1][...] = total[f].astype(BF16)


def last_terms(info, pick_up, g, du, up_weight):
    factors, hgroup, blk = up_weight.shape[1], up_weight.shape[2], up_weight.shape[-1]
    rows, width = g.shape
    per_step = min(4, hgroup // 2)
    half = hgroup // 2 // per_step
    whole = pl.BlockSpec((rows, width), lambda j, *s: (0, 0))

    def weight_spec(f):
        return pl.BlockSpec(
            (1, 1, per_step, blk, blk), lambda j, info, *s: (0, info[2 + f], j * info[0], 0, 0)
        )

    return pl.pallas_call(
        functools.partial(terms_body, factors, per_step, hgroup, blk),
        grid_spec=pltpu.PrefetchScalarGridSpec(
            num_scalar_prefetch=2,
            grid=(hgroup // per_step,),
            in_specs=[
                whole,
                pl.BlockSpec((1, rows, per_step * blk), lambda j, *s: (j // half, 0, j % half)),
            ]
            + [weight_spec(f) for f in range(factors)],
            out_specs=[whole] * factors,
            scratch_shapes=[pltpu.VMEM((factors, rows, width), F32)],
        ),
        out_shape=[jax.ShapeDtypeStruct((rows, width), F32)]
        + [jax.ShapeDtypeStruct((rows, width), BF16)] * (factors - 1),
        compiler_params=pltpu.CompilerParams(vmem_limit_bytes=VMEM_LIMIT),
        cost_estimate=pl.CostEstimate(
            flops=2 * rows * hgroup * blk * blk * factors,
            bytes_accessed=2 * factors * hgroup * blk * blk,
            transcendentals=0,
        ),
        name="last_terms",
    )(info, pick_up, g, du, *[up_weight] * factors)


def select_body(blk, tokens, info, *refs):
    quarter = blk // 4
    sources, keep_ref, give_ref, turned = refs[:-3], refs[-3], refs[-2], refs[-1]
    for m, ref in enumerate(sources):
        columns = slice(m * tokens, (m + 1) * tokens)
        for b in range(ref.shape[1] // blk):
            turned[...] = ref[:, b * blk : (b + 1) * blk].T
            for i, out in enumerate((keep_ref, keep_ref, give_ref, give_ref)):
                start = b * blk // 2 + i % 2 * quarter
                out[start : start + quarter, columns] = turned[block_of(info[i], quarter), :]


def select(wanted, sources, blk):
    tokens, width = sources[0].shape
    inside = pl.BlockSpec(memory_space=pltpu.VMEM)
    return pl.pallas_call(
        functools.partial(select_body, blk, tokens),
        grid_spec=pltpu.PrefetchScalarGridSpec(
            num_scalar_prefetch=1,
            grid=(1,),
            in_specs=[inside] * len(sources),
            out_specs=[inside] * 2,
            scratch_shapes=[pltpu.VMEM((blk, tokens), BF16)],
        ),
        out_shape=[jax.ShapeDtypeStruct((width // 2, len(sources) * tokens), BF16)] * 2,
        compiler_params=pltpu.CompilerParams(vmem_limit_bytes=SMALL_LIMIT),
        name="select",
    )(wanted, *sources)


def products_body(factors, per_step, hgroup, blk, first, info, picks, own_ref, other_ref, *refs):
    lefts, keep_ref, send_ref = refs[:factors], refs[factors], refs[factors + 1]
    half, quarter = blk // 2, blk // 4
    for k in range(per_step):
        j = first + pl.program_id(0) * per_step + k
        columns = slice(k * blk, (k + 1) * blk)
        rights = own_ref[0, :, columns], other_ref[0, :, columns]
        for f in range(factors):
            slot = info[1 + f]
            rows = block_of(picks[slot * hgroup + j], half)
            total = jnp.dot(lefts[f][0, rows, :], rights[0], preferred_element_type=F32)
            total += jnp.dot(lefts[f][1, rows, :], rights[1], preferred_element_type=F32)
            keep_ref[slot, k] = total[:quarter]
            send_ref[slot, k] = total[quarter:].astype(BF16)


def products(info, picks, lefts, own, part, pair, hgroup, blk, first):
    factors = len(lefts)
    tokens, hidden = own.shape[1:]
    count = hidden // blk
    per_step = min(4, count)
    shape = (factors, count, blk // 4, blk)
    out_spec = pl.BlockSpec((factors, per_step) + shape[2:], lambda i, *s: (0, i, 0, 0))
    return pl.pallas_call(
        functools.partial(products_body, factors, per_step, hgroup, blk, first),
        grid_spec=pltpu.PrefetchScalarGridSpec(
            num_scalar_prefetch=2,
            grid=(count // per_step,),
            in_specs=[
                pl.BlockSpec((1, tokens, per_step * blk), lambda i, *s: (part, 0, i)),
                pl.BlockSpec((1, tokens, per_step * blk), lambda i, info, *s: (info[0], 0, i)),
            ]
            + [pl.BlockSpec(lefts[0].shape, lambda i, *s: (0, 0, 0))] * factors,
            out_specs=[out_spec] * 2,
        ),
        out_shape=[jax.ShapeDtypeStruct(shape, F32), jax.ShapeDtypeStruct(shape, BF16)],
        compiler_params=pltpu.CompilerParams(vmem_limit_bytes=VMEM_LIMIT),
        cost_estimate=pl.CostEstimate(
            flops=2 * factors * count * blk * blk * tokens,
            bytes_accessed=4 * tokens * hidden + 3 * factors * count * blk * blk,
            transcendentals=0,
        ),
        name="products",
    )(info, picks, own, pair, *lefts)


def gelu_tanh(values):
    return jax.nn.gelu(values, approximate=True)


def after(value, *earlier):
    return lax.optimization_barrier((value, earlier))[0]


def local(acts_in, pre_act, out_grad, up_weight, down_weight, up_pick, down_pick, factor_order):
    bits = lax.axis_size("hid").bit_length() - 1
    sections = lax.axis_size("section")
    section = lax.axis_index("section")
    z = lax.axis_index("dp").astype(jnp.int32)
    micros, tokens, width = acts_in.shape[1:]
    hgroup, blk = up_weight.shape[2], up_weight.shape[-1]
    hidden = hgroup * blk
    rows = micros * tokens
    order = factor_order[0]
    picks = up_pick.reshape(-1), down_pick.reshape(-1)

    def exchanged(value, active):
        return [value] + [section_partner(value, bit, active) for bit in range(bits)]

    def groups(value):
        return [value] + [partner(value, bit) for bit in range(bits)]

    act = gelu_tanh(pre_act[0].astype(F32)).astype(BF16).reshape(1, rows, hidden)
    act_pair = lax.all_gather(act[0], "dp", axis_index_groups=[[0, 3], [1, 2]])
    x_keep, x_give = select(jnp.stack([z, z ^ 3, z ^ 1, z ^ 2]), [acts_in[0].reshape(rows, width)], blk)
    x_came = along_dp(x_give, 1)

    g_now = [out_grad[m] for m in range(micros)]
    g_layer = list(g_now)
    grad = [None] * micros
    du = jnp.zeros((2, rows, hidden // 2), BF16)
    for step in range(sections):
        active = sections - 1 - step
        here = section == active
        info = jnp.concatenate([jnp.stack([here.astype(jnp.int32), z]), order])
        g_all = [exchanged(g_now[m], active) for m in range(micros)]
        if step:
            g_layer = [jnp.where(here, g_now[m], g_layer[m]) for m in range(micros)]
        if step == sections - 1:
            break
        results = []
        for m in range(micros):
            du, own, *cross = chain(
                info, picks, g_all[m], pre_act, down_weight, up_weight, du, m, True
            )
            total = own
            for bit in range(bits):
                total = total + section_partner(cross[bit], bit, active).astype(F32)
            results.append(total.astype(BF16))
        grad = [results[m] if step == 0 else jnp.where(here, results[m], grad[m]) for m in range(micros)]
        g_now = [section_down(results[m], active) for m in range(micros)]
        if step == 0:
            x_groups = groups(after(jnp.stack([x_keep, x_came]), du))
    g_keep, g_give = select(jnp.stack([z, z ^ 1, z ^ 3, z ^ 2]), g_layer, blk)
    g_came = along_dp(g_give, 3)
    for m in range(micros):
        (du,) = chain(info, picks, g_all[m], pre_act, down_weight, up_weight, du, m, False)

    du, act_pair = lax.optimization_barrier((du, act_pair))
    place = jnp.concatenate([0 * z[None], order])
    up_grad = []
    for part in range(2):
        du_pair = along_dp(du[part], 1)[None]
        keep, give = products(
            place, picks[0], x_groups, du, part, du_pair, hgroup, blk, part * hgroup // 2
        )
        up_grad.append(keep + along_dp(give, 3).astype(F32))
    up_grad = jnp.concatenate(up_grad, axis=1)[None]

    g_groups = groups(after(jnp.stack([g_keep, g_came]), du))
    place = jnp.concatenate([1 - z[None] // 2, order])
    keep, give = products(place, picks[1], g_groups, act, 0, act_pair, hgroup, blk, 0)
    down_grad = (keep + along_dp(give, 1).astype(F32))[None].swapaxes(3, 4)

    own, *cross = last_terms(info, picks[0], jnp.concatenate(g_now, axis=0), du, up_weight)
    for bit in range(bits):
        own = own + section_partner(cross[bit], bit, active).astype(F32)
    result = own.astype(BF16).reshape(micros, tokens, width)
    grad_in = jnp.where(here, result, jnp.stack(grad))[None]
    return grad_in, up_grad, down_grad


def solution(mesh):
    placed = (
        P("section", None, "dp", "hid"),
        P("section", None, "dp", "hid"),
        P(None, "dp", "hid"),
        P("section", None, "hid", None, None),
        P("section", None, "hid", None, None),
        P("section", None, "hid"),
        P("section", None, "hid"),
        P("section", None),
    )
    return jax.shard_map(
        local,
        mesh=mesh,
        in_specs=placed,
        out_specs=(
            P("section", None, "dp", "hid"),
            P("section", None, "hid", "dp", None),
            P("section", None, "hid", None, "dp"),
        ),
        check_vma=False,
    )
```

time: 576 us -> 258 us (0.45)
  waiting for transfers between devices: 300 us -> 123 us
  local copies, waits for them, and re-layouts: 112 us -> 25.6 us
  other arithmetic: 65.8 us -> 14 us
  matrix products: 48.3 us -> 0 us
  starting transfers between devices: 13.8 us -> 49.2 us
  Pallas kernels: 0 us -> 30.4 us
  loops' own time: 21.1 us -> 0 us
    reduce_scatter x2 -> x0, waiting for transfers between devices: 171 us -> none  [the longest x1 103 us: local(): lax.psum_scatter(acc_down.astype(jnp.bfloat16), 'dp', scatter_dimension=3...]
    dot_general x8 -> x0, matrix products: 48.3 us -> none  [the longest x2 14.2 us: do_work(): jnp.einsum('ftjc,fje->ftec', product, onehot_up, precision=highest)]
    gather x16 -> x0, local copies, waits for them, and re-layouts: 45.5 us -> none  [the longest x3 12.1 us: local(): w_up = jnp.take(up_weight[0], weight_index, axis=0)]
    ppermute x21 -> x27, starting transfers between devices: 13.5 us -> 49.2 us  [send(): return lax.ppermute(value, AXES, route)]
    pallas_call x0 -> x10, Pallas kernels: none -> 30.4 us  [the longest x4 11.8 us: chain(): pl.pallas_call(functools.partial(chain_body, cfg), grid_spec=pltpu.Prefet...]
    select_n x15 -> x2, other arithmetic: 30.6 us -> 1.21 us  [the longest x1 1.11 us: local(): grad_in = jnp.where(here, result, jnp.stack(grad))[None]]
    another operation x4 -> x0, loops' own time: 21.1 us -> none  [local(): lax.cond(running, do_work, skip_work, (g_stack, pre_now))]
    another operation x14 -> x0, local copies, waits for them, and re-layouts: 21 us -> none
  transfers between devices with their start and end apart: 23 -> 28, of which waited for: 13 -> 10; matrix products, arithmetic and copies ran while one was open for 19% -> 3% of each run, Pallas kernels for 0% -> 12%
where the time goes in v3:
time: 258 us; the launch traced here: 257 us
  waiting for transfers between devices  123 us (48%)
  starting transfers between devices  49.2 us (19%)
  Pallas kernels  30.4 us (12%)
  local copies, waits for them, and re-layouts  25.6 us (10%)
  between operations  14.5 us (6%)
  other arithmetic  14 us (5%)
    ppermute x27, waiting for transfers between devices, send(): return lax.ppermute(value, AXES, route)  123 us
    ppermute x27, starting transfers between devices, send(): return lax.ppermute(value, AXES, route)  49.2 us
    unnamed x62, local copies, waits for them, and re-layouts  25 us
    pallas_call x4, Pallas kernels, chain(): pl.pallas_call(functools.partial(chain_body, cfg), grid_spec=pltpu.Prefet...  11.8 us
    pallas_call x3, Pallas kernels, products(): pl.pallas_call(functools.partial(products_body, factors, per_step, hgroup...  11.2 us
  transfers between devices with their start and end apart: 28, of which 10 were waited for; matrix products, arithmetic and copies ran while one was open for 3% of the time, Pallas kernels for 12%

profile of v3, /device:TPU:0, one launch (start us, length us, event | category | flops | bytes accessed | tf_op | source)
XLA Modules:
  0.0 256.9 jit_solution(6027535945594073621)
XLA Ops:
  7.2 4.3 %fusion.5.own_ref = bf16[1,256,4096]{2,1,0:T(8,128)(2,1)} fusion(bf16[1,2,128,4096]{3,2,1,0:T(8,128)(2,1)} %refs_3_.7), kind=kLoop, calls=%fused_computation.9 | loop fusion | flops 10485760 | bytes 4194304 | tf_op jit(solution)/shard_map/convert_element_type | solution.py:384
  11.6 1.2 copy-done.22
  12.9 0.7 collective-permute-start
  13.6 0.7 collective-permute-start.1
  14.3 1.5 collective-permute-start.5
  15.8 1.5 collective-permute-start.6
  17.5 0.8 copy-done.16
  18.3 0.8 copy-done.18
  19.4 0.8 copy-done.17
  20.4 3.6 %copy-done = bf16[1,3,16,256,256]{4,3,2,1,0:T(8,128)(2,1)S(1)} copy-done((bf16[1,3,16,256,256]{4,3,2,1,0:T(8,128)(2,1)S(1)}, bf16[1,3,16,256,256]{4,3,2,1,0:T(8,128)(2,1)}, u32[]{:S(2)}) %copy-start) | copy-done | bytes 6291480
  24.0 3.3 %copy-done.3 = bf16[1,3,16,256,256]{4,3,2,1,0:T(8,128)(2,1)S(1)} copy-done((bf16[1,3,16,256,256]{4,3,2,1,0:T(8,128)(2,1)S(1)}, bf16[1,3,16,256,256]{4,3,2,1,0:T(8,128)(2,1)}, u32[]{:S(2)}) %copy-start.3) | copy-done | bytes 6291480
  27.3 1.6 copy-done.5
  28.9 1.9 chain.4
  30.8 1.0 copy-done.14
  31.8 1.5 collective-permute-start.3
  33.2 1.4 collective-permute-start.2
  34.7 2.8 %copy-done.1 = bf16[1,3,16,256,256]{4,3,2,1,0:T(8,128)(2,1)S(1)} copy-done((bf16[1,3,16,256,256]{4,3,2,1,0:T(8,128)(2,1)S(1)}, bf16[1,3,16,256,256]{4,3,2,1,0:T(8,128)(2,1)}, u32[]{:S(2)}) %copy-start.1) | copy-done | bytes 6291480
  37.5 2.8 %copy-done.4 = bf16[1,3,16,256,256]{4,3,2,1,0:T(8,128)(2,1)S(1)} copy-done((bf16[1,3,16,256,256]{4,3,2,1,0:T(8,128)(2,1)S(1)}, bf16[1,3,16,256,256]{4,3,2,1,0:T(8,128)(2,1)}, u32[]{:S(2)}) %copy-start.4) | copy-done | bytes 6291480
  40.2 1.6 copy-done.6
  41.8 0.9 chain.5
  42.7 0.7 collective-permute-start.8
  43.4 0.7 collective-permute-start.7
  44.2 0.9 select.6
  45.1 3.0 %collective-permute-start.17 = (bf16[1024,256]{1,0:T(8,128)(2,1)S(1)}, bf16[1024,256]{1,0:T(8,128)(2,1)S(1)}, u32[]{:S(2)}, u32[]{:S(2)}) collective-permute-start(bf16[1024,256]{1,0:T(8,128)(2,1)S(1)} %get-tuple-element.41), channel_id=1, source_target_pairs={{0,1},{1,0},{2,3},{3,2},{4,5},{5,4},{6,7},{7,6},{8,9},{9,8},{10,11... | collective-permute-start | bytes 1572872 | tf_op jit(solution)/shard_map/ppermute | solution.py:32
  48.1 1.4 add_convert_fusion.2
  49.5 1.3 collective-permute-start.4
  51.1 1.4 collective-permute-start.9
  52.6 43.3 %collective-permute-done.4.refs_0_ = bf16[128,2048]{1,0:T(8,128)(2,1)S(1)} collective-permute-done((bf16[128,2048]{1,0:T(8,128)(2,1)S(1)}, bf16[128,2048]{1,0:T(8,128)(2,1)S(1)}, u32[]{:S(2)}, u32[]{:S(2)}) %collective-permute-start.4) | collective-permute-done | bytes 524320 | tf_op jit(solution)/shard_map/ppermute | solution.py:32
  95.9 1.9 collective-permute-start.12
  97.8 3.4 %collective-permute-start.13 = (bf16[128,2048]{1,0:T(8,128)(2,1)S(1)}, bf16[128,2048]{1,0:T(8,128)(2,1)S(1)}, u32[]{:S(2)}, u32[]{:S(2)}) collective-permute-start(bf16[128,2048]{1,0:T(8,128)(2,1)S(1)} %collective-permute-done.4.refs_0_), channel_id=1, source_target_pairs={{0,8},{1,9},{2,10},{3,11},{4,12},{5,13},{6,14},{7,15},{8,0},{9,1},... | collective-permute-start | bytes 1572872 | tf_op jit(solution)/shard_map/ppermute | solution.py:32
  101.6 4.9 %collective-permute-done.9.refs_0_ = bf16[128,2048]{1,0:T(8,128)(2,1)S(1)} collective-permute-done((bf16[128,2048]{1,0:T(8,128)(2,1)S(1)}, bf16[128,2048]{1,0:T(8,128)(2,1)S(1)}, u32[]{:S(2)}, u32[]{:S(2)}) %collective-permute-start.9) | collective-permute-done | bytes 524320 | tf_op jit(solution)/shard_map/ppermute | solution.py:32
  106.5 1.9 collective-permute-start.10
  108.4 3.4 %collective-permute-start.11 = (bf16[128,2048]{1,0:T(8,128)(2,1)S(1)}, bf16[128,2048]{1,0:T(8,128)(2,1)S(1)}, u32[]{:S(2)}, u32[]{:S(2)}) collective-permute-start(bf16[128,2048]{1,0:T(8,128)(2,1)S(1)} %collective-permute-done.9.refs_0_), channel_id=1, source_target_pairs={{0,8},{1,9},{2,10},{3,11},{4,12},{5,13},{6,14},{7,15},{8,0},{9,1},... | collective-permute-start | bytes 1572872 | tf_op jit(solution)/shard_map/ppermute | solution.py:32
  111.9 1.8 select.7
  113.8 0.8 copy-done.20
  114.6 0.5 collective-permute-start.19
  115.1 2.5 collective-permute-start.23
  117.6 4.4 %chain.6.refs_5_ = bf16[2,256,2048]{2,1,0:T(8,128)(2,1)S(1)} custom-call(s32[5]{0:T(128)S(1)} %get-tuple-element.62.info, s32[48]{0:T(128)S(1)} %reshape.100.pick_up.picks, s32[48]{0:T(128)S(1)} %reshape.101.pick_down.picks, bf16[128,2048]{1,0:T(8,128)(2,1)S(1)} %collective-permute-done.4.refs_0_, ...), custom_call_target="tpu_custom_call", output_to_operand_aliasing={{}: (8, {})} | custom-call | flops 805306368 | bytes 6291456 | tf_op jit(solution)/shard_map/chain/pallas_call | solution.py:198
  122.0 3.6 %collective-permute-done.11.refs_2_ = bf16[128,2048]{1,0:T(8,128)(2,1)S(1)} collective-permute-done((bf16[128,2048]{1,0:T(8,128)(2,1)S(1)}, bf16[128,2048]{1,0:T(8,128)(2,1)S(1)}, u32[]{:S(2)}, u32[]{:S(2)}) %collective-permute-start.11) | collective-permute-done | bytes 524320 | tf_op jit(solution)/shard_map/ppermute | solution.py:32
  125.6 4.6 %chain.7.du_ref.own_ref = bf16[2,256,2048]{2,1,0:T(8,128)(2,1)S(1)} custom-call(s32[5]{0:T(128)S(1)} %get-tuple-element.62.info, s32[48]{0:T(128)S(1)} %reshape.100.pick_up.picks, s32[48]{0:T(128)S(1)} %reshape.101.pick_down.picks, bf16[128,2048]{1,0:T(8,128)(2,1)S(1)} %collective-permute-done.9.refs_0_, ...), custom_call_target="tpu_custom_call", output_to_operand_aliasing={{}: (8, {})} | custom-call | flops 805306368 | bytes 6291456 | tf_op jit(solution)/shard_map/chain/pallas_call | solution.py:198
  130.5 0.5 collective-permute-start.21
  131.3 1.1 pad_maximum_fusion.2.refs_0_
  132.5 10.6 %collective-permute-start.16 = (bf16[256,2048]{1,0:T(8,128)(2,1)S(1)}, bf16[256,2048]{1,0:T(8,128)(2,1)S(1)}, u32[]{:S(2)}, u32[]{:S(2)}) collective-permute-start(bf16[256,2048]{1,0:T(8,128)(2,1)S(1)} %get-tuple-element.53), channel_id=1, source_target_pairs={{0,1},{1,0},{2,3},{3,2},{4,5},{5,4},{6,7},{7,6},{8,9},{9,8},{10,11... | collective-permute-start | bytes 3145736 | tf_op jit(solution)/shard_map/ppermute | solution.py:32
  143.2 1.6 collective-permute-start.25
  144.7 2.8 %copy-done.2 = bf16[1,3,16,256,256]{4,3,2,1,0:T(8,128)(2,1)S(1)} copy-done((bf16[1,3,16,256,256]{4,3,2,1,0:T(8,128)(2,1)S(1)}, bf16[1,3,16,256,256]{4,3,2,1,0:T(8,128)(2,1)}, u32[]{:S(2)}) %copy-start.2) | copy-done | bytes 6291480
  147.5 4.7 %last_terms.1 = (f32[256,2048]{1,0:T(8,128)S(1)}, bf16[256,2048]{1,0:T(8,128)(2,1)S(1)}, bf16[256,2048]{1,0:T(8,128)(2,1)S(1)}) custom-call(s32[5]{0:T(128)S(1)} %get-tuple-element.62.info, s32[48]{0:T(128)S(1)} %reshape.100.pick_up.picks, bf16[256,2048]{1,0:T(8,128)(2,1)S(1)} %pad_maximum_fusion.g_ref, bf16[2,256,2048]{2,1,0:T(8,128)(2,1)S(1)} %chain.7.du_ref.own_ref, ...), custom_call_target="tpu_custom_call" | custom-call | flops 1610612736 | bytes 6291456 | tf_op jit(solution)/shard_map/last_terms/pallas_call | solution.py:257
  152.3 2.4 collective-permute-start.15
  154.7 1.9 collective-permute-done.21
  156.6 1.9 collective-permute-start.14
  158.6 3.6 %products.4 = (f32[3,8,64,256]{3,2,1,0:T(8,128)S(1)}, bf16[3,8,64,256]{3,2,1,0:T(8,128)(2,1)S(1)}) custom-call(s32[4]{0:T(128)S(1)} %get-tuple-element.60.info, s32[48]{0:T(128)S(1)} %reshape.100.pick_up.picks, bf16[2,256,2048]{2,1,0:T(8,128)(2,1)S(1)} %chain.7.du_ref.own_ref, bf16[1,256,2048]{2,1,0:T(8,128)(2,1)S(1)} %bitcast.40, ...), custom_call_target="tpu_custom_call" | custom-call | flops 805306368 | bytes 6815744 | tf_op jit(solution)/shard_map/products/pallas_call | solution.py:335
  162.2 15.3 %collective-permute-done.16 = bf16[256,2048]{1,0:T(8,128)(2,1)S(1)} collective-permute-done((bf16[256,2048]{1,0:T(8,128)(2,1)S(1)}, bf16[256,2048]{1,0:T(8,128)(2,1)S(1)}, u32[]{:S(2)}, u32[]{:S(2)}) %collective-permute-start.16) | collective-permute-done | bytes 1048608 | tf_op jit(solution)/shard_map/ppermute | solution.py:32
  177.5 2.5 collective-permute-start.22
  179.9 3.9 %products.3 = (f32[3,8,64,256]{3,2,1,0:T(8,128)S(1)}, bf16[3,8,64,256]{3,2,1,0:T(8,128)(2,1)S(1)}) custom-call(s32[4]{0:T(128)S(1)} %get-tuple-element.60.info, s32[48]{0:T(128)S(1)} %reshape.100.pick_up.picks, bf16[2,256,2048]{2,1,0:T(8,128)(2,1)S(1)} %chain.7.du_ref.own_ref, bf16[1,256,2048]{2,1,0:T(8,128)(2,1)S(1)} %bitcast.39, ...), custom_call_target="tpu_custom_call" | custom-call | flops 805306368 | bytes 6815744 | tf_op jit(solution)/shard_map/products/pallas_call | solution.py:335
  183.8 1.4 collective-permute-start.20
  185.3 3.8 %products.5 = (f32[3,16,64,256]{3,2,1,0:T(8,128)S(1)}, bf16[3,16,64,256]{3,2,1,0:T(8,128)(2,1)S(1)}) custom-call(s32[4]{0:T(128)S(1)} %get-tuple-element.59.info, s32[48]{0:T(128)S(1)} %reshape.101.pick_down.picks, bf16[1,256,4096]{2,1,0:T(8,128)(2,1)S(1)} %copy-done.7, bf16[2,256,4096]{2,1,0:T(8,128)(2,1)S(1)} %copy-done.12, ...), custom_call_target="tpu_custom_call" | custom-call | flops 1610612736 | bytes 13631488 | tf_op jit(solution)/shard_map/products/pallas_call | solution.py:335
  189.1 3.5 %collective-permute-done.15 = bf16[256,2048]{1,0:T(8,128)(2,1)S(1)} collective-permute-done((bf16[256,2048]{1,0:T(8,128)(2,1)S(1)}, bf16[256,2048]{1,0:T(8,128)(2,1)S(1)}, u32[]{:S(2)}, u32[]{:S(2)}) %collective-permute-start.15) | collective-permute-done | bytes 1048608 | tf_op jit(solution)/shard_map/ppermute | solution.py:32
  192.7 0.5 add_convert_fusion
  193.2 0.5 copy-done.25
  193.9 1.1 maximum_select_fusion
  195.0 5.0 %collective-permute-done.22 = bf16[3,8,64,256]{3,2,1,0:T(8,128)(2,1)S(1)} collective-permute-done((bf16[3,8,64,256]{3,2,1,0:T(8,128)(2,1)S(1)}, bf16[3,8,64,256]{3,2,1,0:T(8,128)(2,1)S(1)}, u32[]{:S(2)}, u32[]{:S(2)}) %collective-permute-start.22) | collective-permute-done | bytes 786464 | tf_op jit(solution)/shard_map/ppermute | solution.py:32
  200.2 16.5 %collective-permute-done.20 = bf16[3,8,64,256]{3,2,1,0:T(8,128)(2,1)S(1)} collective-permute-done((bf16[3,8,64,256]{3,2,1,0:T(8,128)(2,1)S(1)}, bf16[3,8,64,256]{3,2,1,0:T(8,128)(2,1)S(1)}, u32[]{:S(2)}, u32[]{:S(2)}) %collective-permute-start.20) | collective-permute-done | bytes 786464 | tf_op jit(solution)/shard_map/ppermute | solution.py:32
  216.9 2.0 maximum_bitcast_fusion
  218.9 29.0 %collective-permute-done.26 = bf16[3,16,64,256]{3,2,1,0:T(8,128)(2,1)S(1)} collective-permute-done((bf16[3,16,64,256]{3,2,1,0:T(8,128)(2,1)S(1)}, bf16[3,16,64,256]{3,2,1,0:T(8,128)(2,1)S(1)}, u32[]{:S(2)}, u32[]{:S(2)}) %collective-permute-start.26) | collective-permute-done | bytes 1572896 | tf_op jit(solution)/shard_map/ppermute | solution.py:32
  247.9 2.2 add_bitcast_fusion
  (89 shorter events, 3.3 us)
Async XLA Ops:
  7.2 123.1 %all-gather.2.cloned.1.call-start = ((), (), s32[]{:S(2)}) async-start(), calls=%async_computation | async-start | bytes 6291456 | tf_op jit(solution)/shard_map/all_gather | solution.py:385
  11.5 1.2 copy-start.22
  11.5 5.7 %copy-start.29 = (s32[1,3,16]{2,0,1:T(1,128)S(1)}, s32[1,3,16]{2,0,1:T(1,128)}, u32[]{:S(2)}) copy-start(s32[1,3,16]{2,0,1:T(1,128)} %param.13) | copy-start | bytes 580
  11.5 5.8 %copy-start.30 = (s32[1,3,16]{2,0,1:T(1,128)S(1)}, s32[1,3,16]{2,0,1:T(1,128)}, u32[]{:S(2)}) copy-start(s32[1,3,16]{2,0,1:T(1,128)} %param.14) | copy-start | bytes 580
  11.5 5.9 %copy-start.28 = (s32[1,3]{1,0:T(1,128)S(1)}, s32[1,3]{1,0:T(1,128)}, u32[]{:S(2)}) copy-start(s32[1,3]{1,0:T(1,128)} %param.15) | copy-start | bytes 40
  12.9 4.6 %collective-permute-start = (bf16[128,2048]{1,0:T(8,128)(2,1)S(1)}, bf16[128,2048]{1,0:T(8,128)(2,1)S(1)}, u32[]{:S(2)}, u32[]{:S(2)}) collective-permute-start(bf16[128,2048]{1,0:T(8,128)(2,1)S(1)} %get-tuple-element.57.refs_0_), channel_id=1, source_target_pairs={{16,20},{17,21},{18,22},{19,23},{20,16},{21,17},{22,18},{23,19},{2... | collective-permute-start | bytes 1572872 | tf_op jit(solution)/shard_map/ppermute | solution.py:32
  13.6 4.7 %collective-permute-start.1 = (bf16[128,2048]{1,0:T(8,128)(2,1)S(1)}, bf16[128,2048]{1,0:T(8,128)(2,1)S(1)}, u32[]{:S(2)}, u32[]{:S(2)}) collective-permute-start(bf16[128,2048]{1,0:T(8,128)(2,1)S(1)} %get-tuple-element.57.refs_0_), channel_id=1, source_target_pairs={{16,24},{17,25},{18,26},{19,27},{20,28},{21,29},{22,30},{23,31},{2... | collective-permute-start | bytes 1572872 | tf_op jit(solution)/shard_map/ppermute | solution.py:32
  14.3 20.4 %collective-permute-start.5 = (bf16[128,2048]{1,0:T(8,128)(2,1)S(1)}, bf16[128,2048]{1,0:T(8,128)(2,1)}, u32[]{:S(2)}, u32[]{:S(2)}) collective-permute-start(bf16[128,2048]{1,0:T(8,128)(2,1)S(1)} %get-tuple-element.58.refs_0_), channel_id=1, source_target_pairs={{16,20},{17,21},{18,22},{19,23},{20,16},{21,17},{22,18},{23,19},{2... | collective-permute-start | bytes 1572872 | tf_op jit(solution)/shard_map/ppermute | solution.py:32
  15.8 18.9 %collective-permute-start.6 = (bf16[128,2048]{1,0:T(8,128)(2,1)S(1)}, bf16[128,2048]{1,0:T(8,128)(2,1)}, u32[]{:S(2)}, u32[]{:S(2)}) collective-permute-start(bf16[128,2048]{1,0:T(8,128)(2,1)S(1)} %get-tuple-element.58.refs_0_), channel_id=1, source_target_pairs={{16,24},{17,25},{18,26},{19,27},{20,28},{21,29},{22,30},{23,31},{2... | collective-permute-start | bytes 1572872 | tf_op jit(solution)/shard_map/ppermute | solution.py:32
  17.5 0.8 copy-start.16
  18.3 0.8 copy-start.18
  19.1 1.1 copy-start.17
  19.1 1.3 copy-start.19
  20.4 3.6 %copy-start = (bf16[1,3,16,256,256]{4,3,2,1,0:T(8,128)(2,1)S(1)}, bf16[1,3,16,256,256]{4,3,2,1,0:T(8,128)(2,1)}, u32[]{:S(2)}) copy-start(bf16[1,3,16,256,256]{4,3,2,1,0:T(8,128)(2,1)} %refs_2_.1) | copy-start | bytes 18874372
  24.0 3.3 %copy-start.3 = (bf16[1,3,16,256,256]{4,3,2,1,0:T(8,128)(2,1)S(1)}, bf16[1,3,16,256,256]{4,3,2,1,0:T(8,128)(2,1)}, u32[]{:S(2)}) copy-start(bf16[1,3,16,256,256]{4,3,2,1,0:T(8,128)(2,1)} %refs_4_.7) | copy-start | bytes 18874372
  27.3 1.6 copy-start.5
  30.8 1.0 copy-start.14
  31.8 16.3 %collective-permute-start.3 = (bf16[128,2048]{1,0:T(8,128)(2,1)}, bf16[128,2048]{1,0:T(8,128)(2,1)}, u32[]{:S(2)}, u32[]{:S(2)}) collective-permute-start(bf16[128,2048]{1,0:T(8,128)(2,1)} %get-tuple-element.30), channel_id=1, source_target_pairs={{16,24},{17,25},{18,26},{19,27},{20,28},{21,29},{22,30},{23,31},{2... | collective-permute-start | bytes 1572872 | tf_op jit(solution)/shard_map/ppermute | solution.py:32
  33.2 14.9 %collective-permute-start.2 = (bf16[128,2048]{1,0:T(8,128)(2,1)}, bf16[128,2048]{1,0:T(8,128)(2,1)}, u32[]{:S(2)}, u32[]{:S(2)}) collective-permute-start(bf16[128,2048]{1,0:T(8,128)(2,1)} %get-tuple-element.29), channel_id=1, source_target_pairs={{16,20},{17,21},{18,22},{19,23},{20,16},{21,17},{22,18},{23,19},{2... | collective-permute-start | bytes 1572872 | tf_op jit(solution)/shard_map/ppermute | solution.py:32
  34.7 2.8 %copy-start.1 = (bf16[1,3,16,256,256]{4,3,2,1,0:T(8,128)(2,1)S(1)}, bf16[1,3,16,256,256]{4,3,2,1,0:T(8,128)(2,1)}, u32[]{:S(2)}) copy-start(bf16[1,3,16,256,256]{4,3,2,1,0:T(8,128)(2,1)} %refs_2_.1) | copy-start | bytes 18874372
  37.5 2.8 %copy-start.4 = (bf16[1,3,16,256,256]{4,3,2,1,0:T(8,128)(2,1)S(1)}, bf16[1,3,16,256,256]{4,3,2,1,0:T(8,128)(2,1)}, u32[]{:S(2)}) copy-start(bf16[1,3,16,256,256]{4,3,2,1,0:T(8,128)(2,1)} %refs_4_.7) | copy-start | bytes 18874372
  40.2 1.6 copy-start.6
  41.8 2.4 copy-start.13
  41.8 6.3 %copy-start.15 = (f32[128,2048]{1,0:T(8,128)S(1)}, f32[128,2048]{1,0:T(8,128)}, u32[]{:S(2)}) copy-start(f32[128,2048]{1,0:T(8,128)} %copy-done.14) | copy-start | bytes 3145732
  42.7 8.1 %collective-permute-start.8 = (bf16[128,2048]{1,0:T(8,128)(2,1)S(1)}, bf16[128,2048]{1,0:T(8,128)(2,1)S(1)}, u32[]{:S(2)}, u32[]{:S(2)}) collective-permute-start(bf16[128,2048]{1,0:T(8,128)(2,1)S(1)} %get-tuple-element.34), channel_id=1, source_target_pairs={{16,24},{17,25},{18,26},{19,27},{20,28},{21,29},{22,30},{23,31},{2... | collective-permute-start | bytes 1572872 | tf_op jit(solution)/shard_map/ppermute | solution.py:32
  43.4 7.4 %collective-permute-start.7 = (bf16[128,2048]{1,0:T(8,128)(2,1)S(1)}, bf16[128,2048]{1,0:T(8,128)(2,1)S(1)}, u32[]{:S(2)}, u32[]{:S(2)}) collective-permute-start(bf16[128,2048]{1,0:T(8,128)(2,1)S(1)} %get-tuple-element.33), channel_id=1, source_target_pairs={{16,20},{17,21},{18,22},{19,23},{20,16},{21,17},{22,18},{23,19},{2... | collective-permute-start | bytes 1572872 | tf_op jit(solution)/shard_map/ppermute | solution.py:32
  45.1 56.1 %collective-permute-start.17 = (bf16[1024,256]{1,0:T(8,128)(2,1)S(1)}, bf16[1024,256]{1,0:T(8,128)(2,1)S(1)}, u32[]{:S(2)}, u32[]{:S(2)}) collective-permute-start(bf16[1024,256]{1,0:T(8,128)(2,1)S(1)} %get-tuple-element.41), channel_id=1, source_target_pairs={{0,1},{1,0},{2,3},{3,2},{4,5},{5,4},{6,7},{7,6},{8,9},{9,8},{10,11... | collective-permute-start | bytes 1572872 | tf_op jit(solution)/shard_map/ppermute | solution.py:32
  49.5 51.7 %copy-start.24 = (bf16[128,2048]{1,0:T(8,128)(2,1)}, bf16[128,2048]{1,0:T(8,128)(2,1)S(1)}, u32[]{:S(2)}) copy-start(bf16[128,2048]{1,0:T(8,128)(2,1)S(1)} %add_convert_fusion.2) | copy-start | bytes 1572868
  49.5 46.3 %collective-permute-start.4 = (bf16[128,2048]{1,0:T(8,128)(2,1)S(1)}, bf16[128,2048]{1,0:T(8,128)(2,1)S(1)}, u32[]{:S(2)}, u32[]{:S(2)}) collective-permute-start(bf16[128,2048]{1,0:T(8,128)(2,1)S(1)} %add_convert_fusion.2), channel_id=1, source_target_pairs={{16,0},{17,1},{18,2},{19,3},{20,4},{21,5},{22,6},{23,7},{24,8},{25... | collective-permute-start | bytes 1572872 | tf_op jit(solution)/shard_map/ppermute | solution.py:32
  50.9 61.0 %copy-start.23 = (bf16[2,128,2048]{2,1,0:T(8,128)(2,1)S(1)}, bf16[2,128,2048]{2,1,0:T(8,128)(2,1)}, u32[]{:S(2)}) copy-start(bf16[2,128,2048]{2,1,0:T(8,128)(2,1)} %param.10) | copy-start | bytes 3145732
  51.1 57.3 %copy-start.26 = (bf16[128,2048]{1,0:T(8,128)(2,1)}, bf16[128,2048]{1,0:T(8,128)(2,1)S(1)}, u32[]{:S(2)}) copy-start(bf16[128,2048]{1,0:T(8,128)(2,1)S(1)} %add_convert_fusion.1) | copy-start | bytes 1572868
  51.1 55.4 %collective-permute-start.9 = (bf16[128,2048]{1,0:T(8,128)(2,1)S(1)}, bf16[128,2048]{1,0:T(8,128)(2,1)S(1)}, u32[]{:S(2)}, u32[]{:S(2)}) collective-permute-start(bf16[128,2048]{1,0:T(8,128)(2,1)S(1)} %add_convert_fusion.1), channel_id=1, source_target_pairs={{16,0},{17,1},{18,2},{19,3},{20,4},{21,5},{22,6},{23,7},{24,8},{25... | collective-permute-start | bytes 1572872 | tf_op jit(solution)/shard_map/ppermute | solution.py:32
  95.9 21.7 %copy-start.8 = (bf16[128,2048]{1,0:T(8,128)(2,1)}, bf16[128,2048]{1,0:T(8,128)(2,1)S(1)}, u32[]{:S(2)}) copy-start(bf16[128,2048]{1,0:T(8,128)(2,1)S(1)} %collective-permute-done.4.refs_0_) | copy-start | bytes 1572868
  95.9 18.7 %collective-permute-start.12 = (bf16[128,2048]{1,0:T(8,128)(2,1)S(1)}, bf16[128,2048]{1,0:T(8,128)(2,1)S(1)}, u32[]{:S(2)}, u32[]{:S(2)}) collective-permute-start(bf16[128,2048]{1,0:T(8,128)(2,1)S(1)} %collective-permute-done.4.refs_0_), channel_id=1, source_target_pairs={{0,4},{1,5},{2,6},{3,7},{4,0},{5,1},{6,2},{7,3},{8,12},{9,13},{10,... | collective-permute-start | bytes 1572872 | tf_op jit(solution)/shard_map/ppermute | solution.py:32
  97.8 17.4 %collective-permute-start.13 = (bf16[128,2048]{1,0:T(8,128)(2,1)S(1)}, bf16[128,2048]{1,0:T(8,128)(2,1)S(1)}, u32[]{:S(2)}, u32[]{:S(2)}) collective-permute-start(bf16[128,2048]{1,0:T(8,128)(2,1)S(1)} %collective-permute-done.4.refs_0_), channel_id=1, source_target_pairs={{0,8},{1,9},{2,10},{3,11},{4,12},{5,13},{6,14},{7,15},{8,0},{9,1},... | collective-permute-start | bytes 1572872 | tf_op jit(solution)/shard_map/ppermute | solution.py:32
  101.3 41.8 %collective-permute-start.18 = (bf16[2,1024,256]{2,1,0:T(8,128)(2,1)S(1)}, bf16[2,1024,256]{2,1,0:T(8,128)(2,1)}, u32[]{:S(2)}, u32[]{:S(2)}) collective-permute-start(bf16[2,1024,256]{2,1,0:T(8,128)(2,1)S(1)} %pad_maximum_fusion.1.refs_0_), channel_id=1, source_target_pairs={{0,4},{1,5},{2,6},{3,7},{4,0},{5,1},{6,2},{7,3},{8,12},{9,13},{10,... | collective-permute-start | bytes 3145736 | tf_op jit(solution)/shard_map/ppermute | solution.py:32
  106.5 19.2 %copy-start.10 = (bf16[128,2048]{1,0:T(8,128)(2,1)}, bf16[128,2048]{1,0:T(8,128)(2,1)S(1)}, u32[]{:S(2)}) copy-start(bf16[128,2048]{1,0:T(8,128)(2,1)S(1)} %collective-permute-done.9.refs_0_) | copy-start | bytes 1572868
  106.5 15.5 %collective-permute-start.10 = (bf16[128,2048]{1,0:T(8,128)(2,1)S(1)}, bf16[128,2048]{1,0:T(8,128)(2,1)S(1)}, u32[]{:S(2)}, u32[]{:S(2)}) collective-permute-start(bf16[128,2048]{1,0:T(8,128)(2,1)S(1)} %collective-permute-done.9.refs_0_), channel_id=1, source_target_pairs={{0,4},{1,5},{2,6},{3,7},{4,0},{5,1},{6,2},{7,3},{8,12},{9,13},{10,... | collective-permute-start | bytes 1572872 | tf_op jit(solution)/shard_map/ppermute | solution.py:32
  108.4 17.2 %collective-permute-start.11 = (bf16[128,2048]{1,0:T(8,128)(2,1)S(1)}, bf16[128,2048]{1,0:T(8,128)(2,1)S(1)}, u32[]{:S(2)}, u32[]{:S(2)}) collective-permute-start(bf16[128,2048]{1,0:T(8,128)(2,1)S(1)} %collective-permute-done.9.refs_0_), channel_id=1, source_target_pairs={{0,8},{1,9},{2,10},{3,11},{4,12},{5,13},{6,14},{7,15},{8,0},{9,1},... | collective-permute-start | bytes 1572872 | tf_op jit(solution)/shard_map/ppermute | solution.py:32
  113.8 0.8 copy-start.20
  114.6 37.7 %collective-permute-start.19 = (bf16[2,1024,256]{2,1,0:T(8,128)(2,1)S(1)}, bf16[2,1024,256]{2,1,0:T(8,128)(2,1)}, u32[]{:S(2)}, u32[]{:S(2)}) collective-permute-start(bf16[2,1024,256]{2,1,0:T(8,128)(2,1)S(1)} %pad_maximum_fusion.1.refs_0_), channel_id=1, source_target_pairs={{0,8},{1,9},{2,10},{3,11},{4,12},{5,13},{6,14},{7,15},{8,0},{9,1},... | collective-permute-start | bytes 3145736 | tf_op jit(solution)/shard_map/ppermute | solution.py:32
  115.1 16.0 %collective-permute-start.23 = (bf16[1024,256]{1,0:T(8,128)(2,1)}, bf16[1024,256]{1,0:T(8,128)(2,1)}, u32[]{:S(2)}, u32[]{:S(2)}) collective-permute-start(bf16[1024,256]{1,0:T(8,128)(2,1)} %get-tuple-element.49), channel_id=1, source_target_pairs={{0,3},{1,2},{2,1},{3,0},{4,7},{5,6},{6,5},{7,4},{8,11},{9,10},{10,... | collective-permute-start | bytes 1572872 | tf_op jit(solution)/shard_map/ppermute | solution.py:32
  130.3 1.0 copy-start.21
  130.4 12.6 %copy-start.9 = (bf16[128,2048]{1,0:T(8,128)(2,1)S(1)}, bf16[128,2048]{1,0:T(8,128)(2,1)}, u32[]{:S(2)}) copy-start(bf16[128,2048]{1,0:T(8,128)(2,1)} %copy-done.8) | copy-start | bytes 1572868
  130.4 12.6 %copy-start.11 = (bf16[128,2048]{1,0:T(8,128)(2,1)S(1)}, bf16[128,2048]{1,0:T(8,128)(2,1)}, u32[]{:S(2)}) copy-start(bf16[128,2048]{1,0:T(8,128)(2,1)} %copy-done.10) | copy-start | bytes 1572868
  130.5 26.2 %collective-permute-start.21 = (bf16[256,2048]{1,0:T(8,128)(2,1)S(1)}, bf16[256,2048]{1,0:T(8,128)(2,1)S(1)}, u32[]{:S(2)}, u32[]{:S(2)}) collective-permute-start(bf16[256,2048]{1,0:T(8,128)(2,1)S(1)} %get-tuple-element.54), channel_id=1, source_target_pairs={{0,1},{1,0},{2,3},{3,2},{4,5},{5,4},{6,7},{7,6},{8,9},{9,8},{10,11... | collective-permute-start | bytes 3145736 | tf_op jit(solution)/shard_map/ppermute | solution.py:32
  132.5 45.0 %collective-permute-start.16 = (bf16[256,2048]{1,0:T(8,128)(2,1)S(1)}, bf16[256,2048]{1,0:T(8,128)(2,1)S(1)}, u32[]{:S(2)}, u32[]{:S(2)}) collective-permute-start(bf16[256,2048]{1,0:T(8,128)(2,1)S(1)} %get-tuple-element.53), channel_id=1, source_target_pairs={{0,1},{1,0},{2,3},{3,2},{4,5},{5,4},{6,7},{7,6},{8,9},{9,8},{10,11... | collective-permute-start | bytes 3145736 | tf_op jit(solution)/shard_map/ppermute | solution.py:32
  143.1 40.8 %collective-permute-start.24 = (bf16[2,1024,256]{2,1,0:T(8,128)(2,1)S(1)}, bf16[2,1024,256]{2,1,0:T(8,128)(2,1)S(1)}, u32[]{:S(2)}, u32[]{:S(2)}) collective-permute-start(bf16[2,1024,256]{2,1,0:T(8,128)(2,1)S(1)} %pad_maximum_fusion.2.refs_0_), channel_id=1, source_target_pairs={{0,4},{1,5},{2,6},{3,7},{4,0},{5,1},{6,2},{7,3},{8,12},{9,13},{10,... | collective-permute-start | bytes 3145736 | tf_op jit(solution)/shard_map/ppermute | solution.py:32
  143.2 42.1 %collective-permute-start.25 = (bf16[2,1024,256]{2,1,0:T(8,128)(2,1)S(1)}, bf16[2,1024,256]{2,1,0:T(8,128)(2,1)S(1)}, u32[]{:S(2)}, u32[]{:S(2)}) collective-permute-start(bf16[2,1024,256]{2,1,0:T(8,128)(2,1)S(1)} %pad_maximum_fusion.2.refs_0_), channel_id=1, source_target_pairs={{0,8},{1,9},{2,10},{3,11},{4,12},{5,13},{6,14},{7,15},{8,0},{9,1},... | collective-permute-start | bytes 3145736 | tf_op jit(solution)/shard_map/ppermute | solution.py:32
  144.7 2.8 %copy-start.2 = (bf16[1,3,16,256,256]{4,3,2,1,0:T(8,128)(2,1)S(1)}, bf16[1,3,16,256,256]{4,3,2,1,0:T(8,128)(2,1)}, u32[]{:S(2)}) copy-start(bf16[1,3,16,256,256]{4,3,2,1,0:T(8,128)(2,1)} %refs_2_.1) | copy-start | bytes 18874372
  152.3 40.4 %collective-permute-start.15 = (bf16[256,2048]{1,0:T(8,128)(2,1)S(1)}, bf16[256,2048]{1,0:T(8,128)(2,1)S(1)}, u32[]{:S(2)}, u32[]{:S(2)}) collective-permute-start(bf16[256,2048]{1,0:T(8,128)(2,1)S(1)} %get-tuple-element.39), channel_id=1, source_target_pairs={{0,8},{1,9},{2,10},{3,11},{4,12},{5,13},{6,14},{7,15},{8,0},{9,1},... | collective-permute-start | bytes 3145736 | tf_op jit(solution)/shard_map/ppermute | solution.py:32
  156.6 36.0 %collective-permute-start.14 = (bf16[256,2048]{1,0:T(8,128)(2,1)S(1)}, bf16[256,2048]{1,0:T(8,128)(2,1)S(1)}, u32[]{:S(2)}, u32[]{:S(2)}) collective-permute-start(bf16[256,2048]{1,0:T(8,128)(2,1)S(1)} %get-tuple-element.38), channel_id=1, source_target_pairs={{0,4},{1,5},{2,6},{3,7},{4,0},{5,1},{6,2},{7,3},{8,12},{9,13},{10,... | collective-permute-start | bytes 3145736 | tf_op jit(solution)/shard_map/ppermute | solution.py:32
  177.5 22.4 %collective-permute-start.22 = (bf16[3,8,64,256]{3,2,1,0:T(8,128)(2,1)S(1)}, bf16[3,8,64,256]{3,2,1,0:T(8,128)(2,1)S(1)}, u32[]{:S(2)}, u32[]{:S(2)}) collective-permute-start(bf16[3,8,64,256]{3,2,1,0:T(8,128)(2,1)S(1)} %get-tuple-element.46), channel_id=1, source_target_pairs={{0,3},{1,2},{2,1},{3,0},{4,7},{5,6},{6,5},{7,4},{8,11},{9,10},{10,... | collective-permute-start | bytes 2359304 | tf_op jit(solution)/shard_map/ppermute | solution.py:32
  179.9 5.3 %copy-start.7 = (bf16[1,256,4096]{2,1,0:T(8,128)(2,1)S(1)}, bf16[1,256,4096]{2,1,0:T(8,128)(2,1)}, u32[]{:S(2)}) copy-start(bf16[1,256,4096]{2,1,0:T(8,128)(2,1)} %fusion.5.own_ref) | copy-start | bytes 6291460
  179.9 5.3 %copy-start.12 = (bf16[2,256,4096]{2,1,0:T(8,128)(2,1)S(1)}, bf16[2,256,4096]{2,1,0:T(8,128)(2,1)}, u32[]{:S(2)}) copy-start(bf16[2,256,4096]{2,1,0:T(8,128)(2,1)} %all-gather.2.cloned.1.call-done.other_ref) | copy-start | bytes 12582916
  183.8 32.8 %collective-permute-start.20 = (bf16[3,8,64,256]{3,2,1,0:T(8,128)(2,1)S(1)}, bf16[3,8,64,256]{3,2,1,0:T(8,128)(2,1)S(1)}, u32[]{:S(2)}, u32[]{:S(2)}) collective-permute-start(bf16[3,8,64,256]{3,2,1,0:T(8,128)(2,1)S(1)} %get-tuple-element.44), channel_id=1, source_target_pairs={{0,3},{1,2},{2,1},{3,0},{4,7},{5,6},{6,5},{7,4},{8,11},{9,10},{10,... | collective-permute-start | bytes 2359304 | tf_op jit(solution)/shard_map/ppermute | solution.py:32
  189.0 58.9 %collective-permute-start.26 = (bf16[3,16,64,256]{3,2,1,0:T(8,128)(2,1)S(1)}, bf16[3,16,64,256]{3,2,1,0:T(8,128)(2,1)S(1)}, u32[]{:S(2)}, u32[]{:S(2)}) collective-permute-start(bf16[3,16,64,256]{3,2,1,0:T(8,128)(2,1)S(1)} %get-tuple-element.52), channel_id=1, source_target_pairs={{0,1},{1,0},{2,3},{3,2},{4,5},{5,4},{6,7},{7,6},{8,9},{9,8},{10,11... | collective-permute-start | bytes 4718600 | tf_op jit(solution)/shard_map/ppermute | solution.py:32
  192.7 1.0 copy-start.25
  192.7 1.2 copy-start.27
Sparse Core Ops, SparseCore 0:
  11.7 72.6 all-gather.1

commit v4 on v3

--- a/solution.py
+++ b/solution.py
@@ -410,12 +410,12 @@
             results.append(total.astype(BF16))
         grad = [results[m] if step == 0 else jnp.where(here, results[m], grad[m]) for m in range(micros)]
         g_now = [section_down(results[m], active) for m in range(micros)]
-        if step == 0:
-            x_groups = groups(after(jnp.stack([x_keep, x_came]), du))
     g_keep, g_give = select(jnp.stack([z, z ^ 1, z ^ 3, z ^ 2]), g_layer, blk)
     g_came = along_dp(g_give, 3)
     for m in range(micros):
         (du,) = chain(info, picks, g_all[m], pre_act, down_weight, up_weight, du, m, False)
+        if m == 0:
+            x_groups = groups(after(jnp.stack([x_keep, x_came]), du))
 
     du, act_pair = lax.optimization_barrier((du, act_pair))
     place = jnp.concatenate([0 * z[None], order])

time: 258 us -> 258 us (level)
  transfers between devices with their start and end apart: 28 -> 28, of which waited for: 10 -> 9; matrix products, arithmetic and copies ran while one was open for 3% -> 3% of each run, Pallas kernels for 12% -> 12%
where the time goes in v4:
time: 258 us; the launch traced here: 257 us
  waiting for transfers between devices  123 us (48%)
  starting transfers between devices  48.7 us (19%)
  Pallas kernels  30.4 us (12%)
  local copies, waits for them, and re-layouts  25.9 us (10%)
  between operations  14.5 us (6%)
  other arithmetic  14 us (5%)
    ppermute x27, waiting for transfers between devices, send(): return lax.ppermute(value, AXES, route)  123 us
    ppermute x27, starting transfers between devices, send(): return lax.ppermute(value, AXES, route)  48.6 us
    unnamed x62, local copies, waits for them, and re-layouts  25.2 us
    pallas_call x4, Pallas kernels, chain(): pl.pallas_call(functools.partial(chain_body, cfg), grid_spec=pltpu.Prefet...  11.8 us
    pallas_call x3, Pallas kernels, products(): pl.pallas_call(functools.partial(products_body, factors, per_step, hgroup...  11.2 us
  transfers between devices with their start and end apart: 28, of which 9 were waited for; matrix products, arithmetic and copies ran while one was open for 3% of the time, Pallas kernels for 12%

profile of v4, /device:TPU:0, one launch (start us, length us, event | category | flops | bytes accessed | tf_op | source)
XLA Modules:
  0.0 256.9 jit_solution(5041634127333354298)
XLA Ops:
  7.2 4.3 %fusion.5.own_ref = bf16[1,256,4096]{2,1,0:T(8,128)(2,1)} fusion(bf16[1,2,128,4096]{3,2,1,0:T(8,128)(2,1)} %refs_3_.7), kind=kLoop, calls=%fused_computation.9 | loop fusion | flops 10485760 | bytes 4194304 | tf_op jit(solution)/shard_map/convert_element_type | solution.py:384
  11.6 1.2 copy-done.22
  12.9 0.7 collective-permute-start
  13.6 0.7 collective-permute-start.1
  14.3 1.5 collective-permute-start.5
  15.8 1.5 collective-permute-start.6
  17.5 0.8 copy-done.16
  18.3 0.8 copy-done.18
  19.4 0.8 copy-done.17
  20.4 3.6 %copy-done = bf16[1,3,16,256,256]{4,3,2,1,0:T(8,128)(2,1)S(1)} copy-done((bf16[1,3,16,256,256]{4,3,2,1,0:T(8,128)(2,1)S(1)}, bf16[1,3,16,256,256]{4,3,2,1,0:T(8,128)(2,1)}, u32[]{:S(2)}) %copy-start) | copy-done | bytes 6291480
  24.0 3.3 %copy-done.3 = bf16[1,3,16,256,256]{4,3,2,1,0:T(8,128)(2,1)S(1)} copy-done((bf16[1,3,16,256,256]{4,3,2,1,0:T(8,128)(2,1)S(1)}, bf16[1,3,16,256,256]{4,3,2,1,0:T(8,128)(2,1)}, u32[]{:S(2)}) %copy-start.3) | copy-done | bytes 6291480
  27.3 1.6 copy-done.5
  28.9 1.9 chain.4
  30.8 1.0 copy-done.14
  31.8 1.5 collective-permute-start.3
  33.2 1.4 collective-permute-start.2
  34.7 2.8 %copy-done.1 = bf16[1,3,16,256,256]{4,3,2,1,0:T(8,128)(2,1)S(1)} copy-done((bf16[1,3,16,256,256]{4,3,2,1,0:T(8,128)(2,1)S(1)}, bf16[1,3,16,256,256]{4,3,2,1,0:T(8,128)(2,1)}, u32[]{:S(2)}) %copy-start.1) | copy-done | bytes 6291480
  37.5 2.8 %copy-done.4 = bf16[1,3,16,256,256]{4,3,2,1,0:T(8,128)(2,1)S(1)} copy-done((bf16[1,3,16,256,256]{4,3,2,1,0:T(8,128)(2,1)S(1)}, bf16[1,3,16,256,256]{4,3,2,1,0:T(8,128)(2,1)}, u32[]{:S(2)}) %copy-start.4) | copy-done | bytes 6291480
  40.2 1.6 copy-done.6
  41.8 0.9 chain.5
  42.7 0.7 collective-permute-start.8
  43.4 0.7 collective-permute-start.7
  44.2 0.9 select.6
  45.1 3.0 %collective-permute-start.17 = (bf16[1024,256]{1,0:T(8,128)(2,1)S(1)}, bf16[1024,256]{1,0:T(8,128)(2,1)S(1)}, u32[]{:S(2)}, u32[]{:S(2)}) collective-permute-start(bf16[1024,256]{1,0:T(8,128)(2,1)S(1)} %get-tuple-element.41), channel_id=1, source_target_pairs={{0,1},{1,0},{2,3},{3,2},{4,5},{5,4},{6,7},{7,6},{8,9},{9,8},{10,11... | collective-permute-start | bytes 1572872 | tf_op jit(solution)/shard_map/ppermute | solution.py:32
  48.1 1.4 add_convert_fusion.2
  49.5 1.3 collective-permute-start.4
  51.1 1.4 collective-permute-start.9
  52.6 43.3 %collective-permute-done.4.refs_0_ = bf16[128,2048]{1,0:T(8,128)(2,1)S(1)} collective-permute-done((bf16[128,2048]{1,0:T(8,128)(2,1)S(1)}, bf16[128,2048]{1,0:T(8,128)(2,1)S(1)}, u32[]{:S(2)}, u32[]{:S(2)}) %collective-permute-start.4) | collective-permute-done | bytes 524320 | tf_op jit(solution)/shard_map/ppermute | solution.py:32
  95.9 1.9 collective-permute-start.12
  97.8 3.4 %collective-permute-start.13 = (bf16[128,2048]{1,0:T(8,128)(2,1)S(1)}, bf16[128,2048]{1,0:T(8,128)(2,1)S(1)}, u32[]{:S(2)}, u32[]{:S(2)}) collective-permute-start(bf16[128,2048]{1,0:T(8,128)(2,1)S(1)} %collective-permute-done.4.refs_0_), channel_id=1, source_target_pairs={{0,8},{1,9},{2,10},{3,11},{4,12},{5,13},{6,14},{7,15},{8,0},{9,1},... | collective-permute-start | bytes 1572872 | tf_op jit(solution)/shard_map/ppermute | solution.py:32
  101.3 5.1 %collective-permute-done.9.refs_0_ = bf16[128,2048]{1,0:T(8,128)(2,1)S(1)} collective-permute-done((bf16[128,2048]{1,0:T(8,128)(2,1)S(1)}, bf16[128,2048]{1,0:T(8,128)(2,1)S(1)}, u32[]{:S(2)}, u32[]{:S(2)}) %collective-permute-start.9) | collective-permute-done | bytes 524320 | tf_op jit(solution)/shard_map/ppermute | solution.py:32
  106.5 1.9 collective-permute-start.10
  108.4 3.4 %collective-permute-start.11 = (bf16[128,2048]{1,0:T(8,128)(2,1)S(1)}, bf16[128,2048]{1,0:T(8,128)(2,1)S(1)}, u32[]{:S(2)}, u32[]{:S(2)}) collective-permute-start(bf16[128,2048]{1,0:T(8,128)(2,1)S(1)} %collective-permute-done.9.refs_0_), channel_id=1, source_target_pairs={{0,8},{1,9},{2,10},{3,11},{4,12},{5,13},{6,14},{7,15},{8,0},{9,1},... | collective-permute-start | bytes 1572872 | tf_op jit(solution)/shard_map/ppermute | solution.py:32
  111.9 1.8 select.7
  113.8 0.8 copy-done.20
  114.5 2.5 collective-permute-start.23
  117.0 4.5 %chain.6.refs_5_ = bf16[2,256,2048]{2,1,0:T(8,128)(2,1)S(1)} custom-call(s32[5]{0:T(128)S(1)} %get-tuple-element.62.info, s32[48]{0:T(128)S(1)} %reshape.100.pick_up.picks, s32[48]{0:T(128)S(1)} %reshape.101.pick_down.picks, bf16[128,2048]{1,0:T(8,128)(2,1)S(1)} %collective-permute-done.4.refs_0_, ...), custom_call_target="tpu_custom_call", output_to_operand_aliasing={{}: (8, {})} | custom-call | flops 805306368 | bytes 6291456 | tf_op jit(solution)/shard_map/chain/pallas_call | solution.py:198
  121.6 0.6 collective-permute-start.19
  122.2 3.5 %collective-permute-done.11.refs_2_ = bf16[128,2048]{1,0:T(8,128)(2,1)S(1)} collective-permute-done((bf16[128,2048]{1,0:T(8,128)(2,1)S(1)}, bf16[128,2048]{1,0:T(8,128)(2,1)S(1)}, u32[]{:S(2)}, u32[]{:S(2)}) %collective-permute-start.11) | collective-permute-done | bytes 524320 | tf_op jit(solution)/shard_map/ppermute | solution.py:32
  125.6 4.6 %chain.7.du_ref.own_ref = bf16[2,256,2048]{2,1,0:T(8,128)(2,1)S(1)} custom-call(s32[5]{0:T(128)S(1)} %get-tuple-element.62.info, s32[48]{0:T(128)S(1)} %reshape.100.pick_up.picks, s32[48]{0:T(128)S(1)} %reshape.101.pick_down.picks, bf16[128,2048]{1,0:T(8,128)(2,1)S(1)} %collective-permute-done.9.refs_0_, ...), custom_call_target="tpu_custom_call", output_to_operand_aliasing={{}: (8, {})} | custom-call | flops 805306368 | bytes 6291456 | tf_op jit(solution)/shard_map/chain/pallas_call | solution.py:198
  130.9 0.5 copy-done.21
  131.3 1.1 pad_maximum_fusion.2.refs_0_
  132.5 10.3 %collective-permute-start.16 = (bf16[256,2048]{1,0:T(8,128)(2,1)S(1)}, bf16[256,2048]{1,0:T(8,128)(2,1)S(1)}, u32[]{:S(2)}, u32[]{:S(2)}) collective-permute-start(bf16[256,2048]{1,0:T(8,128)(2,1)S(1)} %get-tuple-element.53), channel_id=1, source_target_pairs={{0,1},{1,0},{2,3},{3,2},{4,5},{5,4},{6,7},{7,6},{8,9},{9,8},{10,11... | collective-permute-start | bytes 3145736 | tf_op jit(solution)/shard_map/ppermute | solution.py:32
  142.9 0.6 collective-permute-start.25
  143.5 2.8 %copy-done.2 = bf16[1,3,16,256,256]{4,3,2,1,0:T(8,128)(2,1)S(1)} copy-done((bf16[1,3,16,256,256]{4,3,2,1,0:T(8,128)(2,1)S(1)}, bf16[1,3,16,256,256]{4,3,2,1,0:T(8,128)(2,1)}, u32[]{:S(2)}) %copy-start.2) | copy-done | bytes 6291480
  146.2 4.7 %last_terms.1 = (f32[256,2048]{1,0:T(8,128)S(1)}, bf16[256,2048]{1,0:T(8,128)(2,1)S(1)}, bf16[256,2048]{1,0:T(8,128)(2,1)S(1)}) custom-call(s32[5]{0:T(128)S(1)} %get-tuple-element.62.info, s32[48]{0:T(128)S(1)} %reshape.100.pick_up.picks, bf16[256,2048]{1,0:T(8,128)(2,1)S(1)} %pad_maximum_fusion.g_ref, bf16[2,256,2048]{2,1,0:T(8,128)(2,1)S(1)} %chain.7.du_ref.own_ref, ...), custom_call_target="tpu_custom_call" | custom-call | flops 1610612736 | bytes 6291456 | tf_op jit(solution)/shard_map/last_terms/pallas_call | solution.py:257
  151.0 3.4 %collective-permute-start.15 = (bf16[256,2048]{1,0:T(8,128)(2,1)S(1)}, bf16[256,2048]{1,0:T(8,128)(2,1)S(1)}, u32[]{:S(2)}, u32[]{:S(2)}) collective-permute-start(bf16[256,2048]{1,0:T(8,128)(2,1)S(1)} %get-tuple-element.39), channel_id=1, source_target_pairs={{0,8},{1,9},{2,10},{3,11},{4,12},{5,13},{6,14},{7,15},{8,0},{9,1},... | collective-permute-start | bytes 3145736 | tf_op jit(solution)/shard_map/ppermute | solution.py:32
  154.4 2.2 collective-permute-done.21
  156.6 1.9 collective-permute-start.14
  158.7 3.6 %products.4 = (f32[3,8,64,256]{3,2,1,0:T(8,128)S(1)}, bf16[3,8,64,256]{3,2,1,0:T(8,128)(2,1)S(1)}) custom-call(s32[4]{0:T(128)S(1)} %get-tuple-element.60.info, s32[48]{0:T(128)S(1)} %reshape.100.pick_up.picks, bf16[2,256,2048]{2,1,0:T(8,128)(2,1)S(1)} %chain.7.du_ref.own_ref, bf16[1,256,2048]{2,1,0:T(8,128)(2,1)S(1)} %bitcast.40, ...), custom_call_target="tpu_custom_call" | custom-call | flops 805306368 | bytes 6815744 | tf_op jit(solution)/shard_map/products/pallas_call | solution.py:335
  162.2 15.3 %collective-permute-done.16 = bf16[256,2048]{1,0:T(8,128)(2,1)S(1)} collective-permute-done((bf16[256,2048]{1,0:T(8,128)(2,1)S(1)}, bf16[256,2048]{1,0:T(8,128)(2,1)S(1)}, u32[]{:S(2)}, u32[]{:S(2)}) %collective-permute-start.16) | collective-permute-done | bytes 1048608 | tf_op jit(solution)/shard_map/ppermute | solution.py:32
  177.5 2.5 collective-permute-start.22
  180.0 3.9 %products.3 = (f32[3,8,64,256]{3,2,1,0:T(8,128)S(1)}, bf16[3,8,64,256]{3,2,1,0:T(8,128)(2,1)S(1)}) custom-call(s32[4]{0:T(128)S(1)} %get-tuple-element.60.info, s32[48]{0:T(128)S(1)} %reshape.100.pick_up.picks, bf16[2,256,2048]{2,1,0:T(8,128)(2,1)S(1)} %chain.7.du_ref.own_ref, bf16[1,256,2048]{2,1,0:T(8,128)(2,1)S(1)} %bitcast.39, ...), custom_call_target="tpu_custom_call" | custom-call | flops 805306368 | bytes 6815744 | tf_op jit(solution)/shard_map/products/pallas_call | solution.py:335
  183.9 1.4 collective-permute-start.20
  185.3 3.8 %products.5 = (f32[3,16,64,256]{3,2,1,0:T(8,128)S(1)}, bf16[3,16,64,256]{3,2,1,0:T(8,128)(2,1)S(1)}) custom-call(s32[4]{0:T(128)S(1)} %get-tuple-element.59.info, s32[48]{0:T(128)S(1)} %reshape.101.pick_down.picks, bf16[1,256,4096]{2,1,0:T(8,128)(2,1)S(1)} %copy-done.7, bf16[2,256,4096]{2,1,0:T(8,128)(2,1)S(1)} %copy-done.12, ...), custom_call_target="tpu_custom_call" | custom-call | flops 1610612736 | bytes 13631488 | tf_op jit(solution)/shard_map/products/pallas_call | solution.py:335
  189.1 3.5 %collective-permute-done.15 = bf16[256,2048]{1,0:T(8,128)(2,1)S(1)} collective-permute-done((bf16[256,2048]{1,0:T(8,128)(2,1)S(1)}, bf16[256,2048]{1,0:T(8,128)(2,1)S(1)}, u32[]{:S(2)}, u32[]{:S(2)}) %collective-permute-start.15) | collective-permute-done | bytes 1048608 | tf_op jit(solution)/shard_map/ppermute | solution.py:32
  192.7 0.5 add_convert_fusion
  193.2 0.5 copy-done.25
  193.9 1.1 maximum_select_fusion
  195.0 5.0 %collective-permute-done.22 = bf16[3,8,64,256]{3,2,1,0:T(8,128)(2,1)S(1)} collective-permute-done((bf16[3,8,64,256]{3,2,1,0:T(8,128)(2,1)S(1)}, bf16[3,8,64,256]{3,2,1,0:T(8,128)(2,1)S(1)}, u32[]{:S(2)}, u32[]{:S(2)}) %collective-permute-start.22) | collective-permute-done | bytes 786464 | tf_op jit(solution)/shard_map/ppermute | solution.py:32
  200.2 16.5 %collective-permute-done.20 = bf16[3,8,64,256]{3,2,1,0:T(8,128)(2,1)S(1)} collective-permute-done((bf16[3,8,64,256]{3,2,1,0:T(8,128)(2,1)S(1)}, bf16[3,8,64,256]{3,2,1,0:T(8,128)(2,1)S(1)}, u32[]{:S(2)}, u32[]{:S(2)}) %collective-permute-start.20) | collective-permute-done | bytes 786464 | tf_op jit(solution)/shard_map/ppermute | solution.py:32
  216.9 2.0 maximum_bitcast_fusion
  218.9 28.9 %collective-permute-done.26 = bf16[3,16,64,256]{3,2,1,0:T(8,128)(2,1)S(1)} collective-permute-done((bf16[3,16,64,256]{3,2,1,0:T(8,128)(2,1)S(1)}, bf16[3,16,64,256]{3,2,1,0:T(8,128)(2,1)S(1)}, u32[]{:S(2)}, u32[]{:S(2)}) %collective-permute-start.26) | collective-permute-done | bytes 1572896 | tf_op jit(solution)/shard_map/ppermute | solution.py:32
  247.9 2.2 add_bitcast_fusion
  (89 shorter events, 3.1 us)
Async XLA Ops:
  7.2 123.1 %all-gather.2.cloned.1.call-start = ((), (), s32[]{:S(2)}) async-start(), calls=%async_computation | async-start | bytes 6291456 | tf_op jit(solution)/shard_map/all_gather | solution.py:385
  11.5 1.2 copy-start.22
  11.5 5.7 %copy-start.29 = (s32[1,3,16]{2,0,1:T(1,128)S(1)}, s32[1,3,16]{2,0,1:T(1,128)}, u32[]{:S(2)}) copy-start(s32[1,3,16]{2,0,1:T(1,128)} %param.13) | copy-start | bytes 580
  11.5 5.8 %copy-start.30 = (s32[1,3,16]{2,0,1:T(1,128)S(1)}, s32[1,3,16]{2,0,1:T(1,128)}, u32[]{:S(2)}) copy-start(s32[1,3,16]{2,0,1:T(1,128)} %param.14) | copy-start | bytes 580
  11.5 5.9 %copy-start.28 = (s32[1,3]{1,0:T(1,128)S(1)}, s32[1,3]{1,0:T(1,128)}, u32[]{:S(2)}) copy-start(s32[1,3]{1,0:T(1,128)} %param.15) | copy-start | bytes 40
  12.9 4.6 %collective-permute-start = (bf16[128,2048]{1,0:T(8,128)(2,1)S(1)}, bf16[128,2048]{1,0:T(8,128)(2,1)S(1)}, u32[]{:S(2)}, u32[]{:S(2)}) collective-permute-start(bf16[128,2048]{1,0:T(8,128)(2,1)S(1)} %get-tuple-element.57.refs_0_), channel_id=1, source_target_pairs={{16,20},{17,21},{18,22},{19,23},{20,16},{21,17},{22,18},{23,19},{2... | collective-permute-start | bytes 1572872 | tf_op jit(solution)/shard_map/ppermute | solution.py:32
  13.6 4.7 %collective-permute-start.1 = (bf16[128,2048]{1,0:T(8,128)(2,1)S(1)}, bf16[128,2048]{1,0:T(8,128)(2,1)S(1)}, u32[]{:S(2)}, u32[]{:S(2)}) collective-permute-start(bf16[128,2048]{1,0:T(8,128)(2,1)S(1)} %get-tuple-element.57.refs_0_), channel_id=1, source_target_pairs={{16,24},{17,25},{18,26},{19,27},{20,28},{21,29},{22,30},{23,31},{2... | collective-permute-start | bytes 1572872 | tf_op jit(solution)/shard_map/ppermute | solution.py:32
  14.3 20.4 %collective-permute-start.5 = (bf16[128,2048]{1,0:T(8,128)(2,1)S(1)}, bf16[128,2048]{1,0:T(8,128)(2,1)}, u32[]{:S(2)}, u32[]{:S(2)}) collective-permute-start(bf16[128,2048]{1,0:T(8,128)(2,1)S(1)} %get-tuple-element.58.refs_0_), channel_id=1, source_target_pairs={{16,20},{17,21},{18,22},{19,23},{20,16},{21,17},{22,18},{23,19},{2... | collective-permute-start | bytes 1572872 | tf_op jit(solution)/shard_map/ppermute | solution.py:32
  15.8 18.9 %collective-permute-start.6 = (bf16[128,2048]{1,0:T(8,128)(2,1)S(1)}, bf16[128,2048]{1,0:T(8,128)(2,1)}, u32[]{:S(2)}, u32[]{:S(2)}) collective-permute-start(bf16[128,2048]{1,0:T(8,128)(2,1)S(1)} %get-tuple-element.58.refs_0_), channel_id=1, source_target_pairs={{16,24},{17,25},{18,26},{19,27},{20,28},{21,29},{22,30},{23,31},{2... | collective-permute-start | bytes 1572872 | tf_op jit(solution)/shard_map/ppermute | solution.py:32
  17.5 0.8 copy-start.16
  18.3 0.8 copy-start.18
  19.1 1.1 copy-start.17
  19.1 1.3 copy-start.19
  20.4 3.6 %copy-start = (bf16[1,3,16,256,256]{4,3,2,1,0:T(8,128)(2,1)S(1)}, bf16[1,3,16,256,256]{4,3,2,1,0:T(8,128)(2,1)}, u32[]{:S(2)}) copy-start(bf16[1,3,16,256,256]{4,3,2,1,0:T(8,128)(2,1)} %refs_2_.1) | copy-start | bytes 18874372
  24.0 3.3 %copy-start.3 = (bf16[1,3,16,256,256]{4,3,2,1,0:T(8,128)(2,1)S(1)}, bf16[1,3,16,256,256]{4,3,2,1,0:T(8,128)(2,1)}, u32[]{:S(2)}) copy-start(bf16[1,3,16,256,256]{4,3,2,1,0:T(8,128)(2,1)} %refs_4_.7) | copy-start | bytes 18874372
  27.3 1.6 copy-start.5
  30.8 1.0 copy-start.14
  31.8 16.3 %collective-permute-start.3 = (bf16[128,2048]{1,0:T(8,128)(2,1)}, bf16[128,2048]{1,0:T(8,128)(2,1)}, u32[]{:S(2)}, u32[]{:S(2)}) collective-permute-start(bf16[128,2048]{1,0:T(8,128)(2,1)} %get-tuple-element.30), channel_id=1, source_target_pairs={{16,24},{17,25},{18,26},{19,27},{20,28},{21,29},{22,30},{23,31},{2... | collective-permute-start | bytes 1572872 | tf_op jit(solution)/shard_map/ppermute | solution.py:32
  33.2 14.9 %collective-permute-start.2 = (bf16[128,2048]{1,0:T(8,128)(2,1)}, bf16[128,2048]{1,0:T(8,128)(2,1)}, u32[]{:S(2)}, u32[]{:S(2)}) collective-permute-start(bf16[128,2048]{1,0:T(8,128)(2,1)} %get-tuple-element.29), channel_id=1, source_target_pairs={{16,20},{17,21},{18,22},{19,23},{20,16},{21,17},{22,18},{23,19},{2... | collective-permute-start | bytes 1572872 | tf_op jit(solution)/shard_map/ppermute | solution.py:32
  34.7 2.8 %copy-start.1 = (bf16[1,3,16,256,256]{4,3,2,1,0:T(8,128)(2,1)S(1)}, bf16[1,3,16,256,256]{4,3,2,1,0:T(8,128)(2,1)}, u32[]{:S(2)}) copy-start(bf16[1,3,16,256,256]{4,3,2,1,0:T(8,128)(2,1)} %refs_2_.1) | copy-start | bytes 18874372
  37.5 2.8 %copy-start.4 = (bf16[1,3,16,256,256]{4,3,2,1,0:T(8,128)(2,1)S(1)}, bf16[1,3,16,256,256]{4,3,2,1,0:T(8,128)(2,1)}, u32[]{:S(2)}) copy-start(bf16[1,3,16,256,256]{4,3,2,1,0:T(8,128)(2,1)} %refs_4_.7) | copy-start | bytes 18874372
  40.2 1.6 copy-start.6
  41.8 2.4 copy-start.13
  41.8 6.3 %copy-start.15 = (f32[128,2048]{1,0:T(8,128)S(1)}, f32[128,2048]{1,0:T(8,128)}, u32[]{:S(2)}) copy-start(f32[128,2048]{1,0:T(8,128)} %copy-done.14) | copy-start | bytes 3145732
  42.7 8.1 %collective-permute-start.8 = (bf16[128,2048]{1,0:T(8,128)(2,1)S(1)}, bf16[128,2048]{1,0:T(8,128)(2,1)S(1)}, u32[]{:S(2)}, u32[]{:S(2)}) collective-permute-start(bf16[128,2048]{1,0:T(8,128)(2,1)S(1)} %get-tuple-element.34), channel_id=1, source_target_pairs={{16,24},{17,25},{18,26},{19,27},{20,28},{21,29},{22,30},{23,31},{2... | collective-permute-start | bytes 1572872 | tf_op jit(solution)/shard_map/ppermute | solution.py:32
  43.4 7.4 %collective-permute-start.7 = (bf16[128,2048]{1,0:T(8,128)(2,1)S(1)}, bf16[128,2048]{1,0:T(8,128)(2,1)S(1)}, u32[]{:S(2)}, u32[]{:S(2)}) collective-permute-start(bf16[128,2048]{1,0:T(8,128)(2,1)S(1)} %get-tuple-element.33), channel_id=1, source_target_pairs={{16,20},{17,21},{18,22},{19,23},{20,16},{21,17},{22,18},{23,19},{2... | collective-permute-start | bytes 1572872 | tf_op jit(solution)/shard_map/ppermute | solution.py:32
  45.1 56.1 %collective-permute-start.17 = (bf16[1024,256]{1,0:T(8,128)(2,1)S(1)}, bf16[1024,256]{1,0:T(8,128)(2,1)S(1)}, u32[]{:S(2)}, u32[]{:S(2)}) collective-permute-start(bf16[1024,256]{1,0:T(8,128)(2,1)S(1)} %get-tuple-element.41), channel_id=1, source_target_pairs={{0,1},{1,0},{2,3},{3,2},{4,5},{5,4},{6,7},{7,6},{8,9},{9,8},{10,11... | collective-permute-start | bytes 1572872 | tf_op jit(solution)/shard_map/ppermute | solution.py:32
  49.5 51.7 %copy-start.24 = (bf16[128,2048]{1,0:T(8,128)(2,1)}, bf16[128,2048]{1,0:T(8,128)(2,1)S(1)}, u32[]{:S(2)}) copy-start(bf16[128,2048]{1,0:T(8,128)(2,1)S(1)} %add_convert_fusion.2) | copy-start | bytes 1572868
  49.5 46.3 %collective-permute-start.4 = (bf16[128,2048]{1,0:T(8,128)(2,1)S(1)}, bf16[128,2048]{1,0:T(8,128)(2,1)S(1)}, u32[]{:S(2)}, u32[]{:S(2)}) collective-permute-start(bf16[128,2048]{1,0:T(8,128)(2,1)S(1)} %add_convert_fusion.2), channel_id=1, source_target_pairs={{16,0},{17,1},{18,2},{19,3},{20,4},{21,5},{22,6},{23,7},{24,8},{25... | collective-permute-start | bytes 1572872 | tf_op jit(solution)/shard_map/ppermute | solution.py:32
  50.9 61.0 %copy-start.23 = (bf16[2,128,2048]{2,1,0:T(8,128)(2,1)S(1)}, bf16[2,128,2048]{2,1,0:T(8,128)(2,1)}, u32[]{:S(2)}) copy-start(bf16[2,128,2048]{2,1,0:T(8,128)(2,1)} %param.10) | copy-start | bytes 3145732
  51.1 57.3 %copy-start.26 = (bf16[128,2048]{1,0:T(8,128)(2,1)}, bf16[128,2048]{1,0:T(8,128)(2,1)S(1)}, u32[]{:S(2)}) copy-start(bf16[128,2048]{1,0:T(8,128)(2,1)S(1)} %add_convert_fusion.1) | copy-start | bytes 1572868
  51.1 55.4 %collective-permute-start.9 = (bf16[128,2048]{1,0:T(8,128)(2,1)S(1)}, bf16[128,2048]{1,0:T(8,128)(2,1)S(1)}, u32[]{:S(2)}, u32[]{:S(2)}) collective-permute-start(bf16[128,2048]{1,0:T(8,128)(2,1)S(1)} %add_convert_fusion.1), channel_id=1, source_target_pairs={{16,0},{17,1},{18,2},{19,3},{20,4},{21,5},{22,6},{23,7},{24,8},{25... | collective-permute-start | bytes 1572872 | tf_op jit(solution)/shard_map/ppermute | solution.py:32
  95.9 21.2 %copy-start.8 = (bf16[128,2048]{1,0:T(8,128)(2,1)}, bf16[128,2048]{1,0:T(8,128)(2,1)S(1)}, u32[]{:S(2)}) copy-start(bf16[128,2048]{1,0:T(8,128)(2,1)S(1)} %collective-permute-done.4.refs_0_) | copy-start | bytes 1572868
  95.9 21.1 %collective-permute-start.12 = (bf16[128,2048]{1,0:T(8,128)(2,1)S(1)}, bf16[128,2048]{1,0:T(8,128)(2,1)S(1)}, u32[]{:S(2)}, u32[]{:S(2)}) collective-permute-start(bf16[128,2048]{1,0:T(8,128)(2,1)S(1)} %collective-permute-done.4.refs_0_), channel_id=1, source_target_pairs={{0,4},{1,5},{2,6},{3,7},{4,0},{5,1},{6,2},{7,3},{8,12},{9,13},{10,... | collective-permute-start | bytes 1572872 | tf_op jit(solution)/shard_map/ppermute | solution.py:32
  97.8 19.2 %collective-permute-start.13 = (bf16[128,2048]{1,0:T(8,128)(2,1)S(1)}, bf16[128,2048]{1,0:T(8,128)(2,1)S(1)}, u32[]{:S(2)}, u32[]{:S(2)}) collective-permute-start(bf16[128,2048]{1,0:T(8,128)(2,1)S(1)} %collective-permute-done.4.refs_0_), channel_id=1, source_target_pairs={{0,8},{1,9},{2,10},{3,11},{4,12},{5,13},{6,14},{7,15},{8,0},{9,1},... | collective-permute-start | bytes 1572872 | tf_op jit(solution)/shard_map/ppermute | solution.py:32
  106.5 19.2 %copy-start.10 = (bf16[128,2048]{1,0:T(8,128)(2,1)}, bf16[128,2048]{1,0:T(8,128)(2,1)S(1)}, u32[]{:S(2)}) copy-start(bf16[128,2048]{1,0:T(8,128)(2,1)S(1)} %collective-permute-done.9.refs_0_) | copy-start | bytes 1572868
  106.5 15.7 %collective-permute-start.10 = (bf16[128,2048]{1,0:T(8,128)(2,1)S(1)}, bf16[128,2048]{1,0:T(8,128)(2,1)S(1)}, u32[]{:S(2)}, u32[]{:S(2)}) collective-permute-start(bf16[128,2048]{1,0:T(8,128)(2,1)S(1)} %collective-permute-done.9.refs_0_), channel_id=1, source_target_pairs={{0,4},{1,5},{2,6},{3,7},{4,0},{5,1},{6,2},{7,3},{8,12},{9,13},{10,... | collective-permute-start | bytes 1572872 | tf_op jit(solution)/shard_map/ppermute | solution.py:32
  108.4 17.2 %collective-permute-start.11 = (bf16[128,2048]{1,0:T(8,128)(2,1)S(1)}, bf16[128,2048]{1,0:T(8,128)(2,1)S(1)}, u32[]{:S(2)}, u32[]{:S(2)}) collective-permute-start(bf16[128,2048]{1,0:T(8,128)(2,1)S(1)} %collective-permute-done.9.refs_0_), channel_id=1, source_target_pairs={{0,8},{1,9},{2,10},{3,11},{4,12},{5,13},{6,14},{7,15},{8,0},{9,1},... | collective-permute-start | bytes 1572872 | tf_op jit(solution)/shard_map/ppermute | solution.py:32
  113.8 0.8 copy-start.20
  114.5 16.3 %collective-permute-start.23 = (bf16[1024,256]{1,0:T(8,128)(2,1)}, bf16[1024,256]{1,0:T(8,128)(2,1)}, u32[]{:S(2)}, u32[]{:S(2)}) collective-permute-start(bf16[1024,256]{1,0:T(8,128)(2,1)} %get-tuple-element.49), channel_id=1, source_target_pairs={{0,3},{1,2},{2,1},{3,0},{4,7},{5,6},{6,5},{7,4},{8,11},{9,10},{10,... | collective-permute-start | bytes 1572872 | tf_op jit(solution)/shard_map/ppermute | solution.py:32
  121.5 21.4 %collective-permute-start.18 = (bf16[2,1024,256]{2,1,0:T(8,128)(2,1)S(1)}, bf16[2,1024,256]{2,1,0:T(8,128)(2,1)}, u32[]{:S(2)}, u32[]{:S(2)}) collective-permute-start(bf16[2,1024,256]{2,1,0:T(8,128)(2,1)S(1)} %pad_maximum_fusion.1.refs_0_), channel_id=1, source_target_pairs={{0,4},{1,5},{2,6},{3,7},{4,0},{5,1},{6,2},{7,3},{8,12},{9,13},{10,... | collective-permute-start | bytes 3145736 | tf_op jit(solution)/shard_map/ppermute | solution.py:32
  121.6 29.4 %collective-permute-start.19 = (bf16[2,1024,256]{2,1,0:T(8,128)(2,1)S(1)}, bf16[2,1024,256]{2,1,0:T(8,128)(2,1)}, u32[]{:S(2)}, u32[]{:S(2)}) collective-permute-start(bf16[2,1024,256]{2,1,0:T(8,128)(2,1)S(1)} %pad_maximum_fusion.1.refs_0_), channel_id=1, source_target_pairs={{0,8},{1,9},{2,10},{3,11},{4,12},{5,13},{6,14},{7,15},{8,0},{9,1},... | collective-permute-start | bytes 3145736 | tf_op jit(solution)/shard_map/ppermute | solution.py:32
  130.3 1.0 copy-start.21
  130.5 12.3 %copy-start.9 = (bf16[128,2048]{1,0:T(8,128)(2,1)S(1)}, bf16[128,2048]{1,0:T(8,128)(2,1)}, u32[]{:S(2)}) copy-start(bf16[128,2048]{1,0:T(8,128)(2,1)} %copy-done.8) | copy-start | bytes 1572868
  130.5 12.3 %copy-start.11 = (bf16[128,2048]{1,0:T(8,128)(2,1)S(1)}, bf16[128,2048]{1,0:T(8,128)(2,1)}, u32[]{:S(2)}) copy-start(bf16[128,2048]{1,0:T(8,128)(2,1)} %copy-done.10) | copy-start | bytes 1572868
  130.5 26.2 %collective-permute-start.21 = (bf16[256,2048]{1,0:T(8,128)(2,1)S(1)}, bf16[256,2048]{1,0:T(8,128)(2,1)S(1)}, u32[]{:S(2)}, u32[]{:S(2)}) collective-permute-start(bf16[256,2048]{1,0:T(8,128)(2,1)S(1)} %get-tuple-element.54), channel_id=1, source_target_pairs={{0,1},{1,0},{2,3},{3,2},{4,5},{5,4},{6,7},{7,6},{8,9},{9,8},{10,11... | collective-permute-start | bytes 3145736 | tf_op jit(solution)/shard_map/ppermute | solution.py:32
  132.5 45.0 %collective-permute-start.16 = (bf16[256,2048]{1,0:T(8,128)(2,1)S(1)}, bf16[256,2048]{1,0:T(8,128)(2,1)S(1)}, u32[]{:S(2)}, u32[]{:S(2)}) collective-permute-start(bf16[256,2048]{1,0:T(8,128)(2,1)S(1)} %get-tuple-element.53), channel_id=1, source_target_pairs={{0,1},{1,0},{2,3},{3,2},{4,5},{5,4},{6,7},{7,6},{8,9},{9,8},{10,11... | collective-permute-start | bytes 3145736 | tf_op jit(solution)/shard_map/ppermute | solution.py:32
  142.8 41.1 %collective-permute-start.24 = (bf16[2,1024,256]{2,1,0:T(8,128)(2,1)S(1)}, bf16[2,1024,256]{2,1,0:T(8,128)(2,1)S(1)}, u32[]{:S(2)}, u32[]{:S(2)}) collective-permute-start(bf16[2,1024,256]{2,1,0:T(8,128)(2,1)S(1)} %pad_maximum_fusion.2.refs_0_), channel_id=1, source_target_pairs={{0,4},{1,5},{2,6},{3,7},{4,0},{5,1},{6,2},{7,3},{8,12},{9,13},{10,... | collective-permute-start | bytes 3145736 | tf_op jit(solution)/shard_map/ppermute | solution.py:32
  142.9 42.4 %collective-permute-start.25 = (bf16[2,1024,256]{2,1,0:T(8,128)(2,1)S(1)}, bf16[2,1024,256]{2,1,0:T(8,128)(2,1)S(1)}, u32[]{:S(2)}, u32[]{:S(2)}) collective-permute-start(bf16[2,1024,256]{2,1,0:T(8,128)(2,1)S(1)} %pad_maximum_fusion.2.refs_0_), channel_id=1, source_target_pairs={{0,8},{1,9},{2,10},{3,11},{4,12},{5,13},{6,14},{7,15},{8,0},{9,1},... | collective-permute-start | bytes 3145736 | tf_op jit(solution)/shard_map/ppermute | solution.py:32
  143.5 2.8 %copy-start.2 = (bf16[1,3,16,256,256]{4,3,2,1,0:T(8,128)(2,1)S(1)}, bf16[1,3,16,256,256]{4,3,2,1,0:T(8,128)(2,1)}, u32[]{:S(2)}) copy-start(bf16[1,3,16,256,256]{4,3,2,1,0:T(8,128)(2,1)} %refs_2_.1) | copy-start | bytes 18874372
  151.0 41.7 %collective-permute-start.15 = (bf16[256,2048]{1,0:T(8,128)(2,1)S(1)}, bf16[256,2048]{1,0:T(8,128)(2,1)S(1)}, u32[]{:S(2)}, u32[]{:S(2)}) collective-permute-start(bf16[256,2048]{1,0:T(8,128)(2,1)S(1)} %get-tuple-element.39), channel_id=1, source_target_pairs={{0,8},{1,9},{2,10},{3,11},{4,12},{5,13},{6,14},{7,15},{8,0},{9,1},... | collective-permute-start | bytes 3145736 | tf_op jit(solution)/shard_map/ppermute | solution.py:32
  156.6 36.0 %collective-permute-start.14 = (bf16[256,2048]{1,0:T(8,128)(2,1)S(1)}, bf16[256,2048]{1,0:T(8,128)(2,1)S(1)}, u32[]{:S(2)}, u32[]{:S(2)}) collective-permute-start(bf16[256,2048]{1,0:T(8,128)(2,1)S(1)} %get-tuple-element.38), channel_id=1, source_target_pairs={{0,4},{1,5},{2,6},{3,7},{4,0},{5,1},{6,2},{7,3},{8,12},{9,13},{10,... | collective-permute-start | bytes 3145736 | tf_op jit(solution)/shard_map/ppermute | solution.py:32
  177.5 22.4 %collective-permute-start.22 = (bf16[3,8,64,256]{3,2,1,0:T(8,128)(2,1)S(1)}, bf16[3,8,64,256]{3,2,1,0:T(8,128)(2,1)S(1)}, u32[]{:S(2)}, u32[]{:S(2)}) collective-permute-start(bf16[3,8,64,256]{3,2,1,0:T(8,128)(2,1)S(1)} %get-tuple-element.46), channel_id=1, source_target_pairs={{0,3},{1,2},{2,1},{3,0},{4,7},{5,6},{6,5},{7,4},{8,11},{9,10},{10,... | collective-permute-start | bytes 2359304 | tf_op jit(solution)/shard_map/ppermute | solution.py:32
  180.0 5.3 %copy-start.7 = (bf16[1,256,4096]{2,1,0:T(8,128)(2,1)S(1)}, bf16[1,256,4096]{2,1,0:T(8,128)(2,1)}, u32[]{:S(2)}) copy-start(bf16[1,256,4096]{2,1,0:T(8,128)(2,1)} %fusion.5.own_ref) | copy-start | bytes 6291460
  180.0 5.3 %copy-start.12 = (bf16[2,256,4096]{2,1,0:T(8,128)(2,1)S(1)}, bf16[2,256,4096]{2,1,0:T(8,128)(2,1)}, u32[]{:S(2)}) copy-start(bf16[2,256,4096]{2,1,0:T(8,128)(2,1)} %all-gather.2.cloned.1.call-done.other_ref) | copy-start | bytes 12582916
  183.9 32.8 %collective-permute-start.20 = (bf16[3,8,64,256]{3,2,1,0:T(8,128)(2,1)S(1)}, bf16[3,8,64,256]{3,2,1,0:T(8,128)(2,1)S(1)}, u32[]{:S(2)}, u32[]{:S(2)}) collective-permute-start(bf16[3,8,64,256]{3,2,1,0:T(8,128)(2,1)S(1)} %get-tuple-element.44), channel_id=1, source_target_pairs={{0,3},{1,2},{2,1},{3,0},{4,7},{5,6},{6,5},{7,4},{8,11},{9,10},{10,... | collective-permute-start | bytes 2359304 | tf_op jit(solution)/shard_map/ppermute | solution.py:32
  189.0 58.9 %collective-permute-start.26 = (bf16[3,16,64,256]{3,2,1,0:T(8,128)(2,1)S(1)}, bf16[3,16,64,256]{3,2,1,0:T(8,128)(2,1)S(1)}, u32[]{:S(2)}, u32[]{:S(2)}) collective-permute-start(bf16[3,16,64,256]{3,2,1,0:T(8,128)(2,1)S(1)} %get-tuple-element.52), channel_id=1, source_target_pairs={{0,1},{1,0},{2,3},{3,2},{4,5},{5,4},{6,7},{7,6},{8,9},{9,8},{10,11... | collective-permute-start | bytes 4718600 | tf_op jit(solution)/shard_map/ppermute | solution.py:32
  192.7 1.0 copy-start.25
  192.7 1.2 copy-start.27
Sparse Core Ops, SparseCore 0:
  11.7 72.6 all-gather.1
